TPU v7x, 512 devices: a whole 4x4x16 slice. The times are simulated.
512 devices in a mesh: guide: 2 (over y_lo), patch: 64 (over x, z), tensor: 4 (over y_hi, core).
Axes of the slice: x: 4, y: 4 (y_hi: 2, y_lo: 2; y = y_hi * 2 + y_lo), z: 16, core: 2. Of those that a mesh axis runs over, the one named last changes fastest.
Arguments:
- query: bfloat16 [2, 5120, 2560], P('guide', 'patch', 'tensor'), may hold values from -160 to 160
- fresh_kv: bfloat16 [2, 2, 5120, 2560], P('guide', None, 'patch', 'tensor'), may hold values from -16 to 16
- stale_kv: bfloat16 [2, 2, 5120, 2560], P('guide', None, 'patch', 'tensor'), may hold values from -32 to 32
- assign: int32 [5120], P('patch'), may hold values from 0 to 5119, each once
- timestep: int32 [1], replicated, may hold values from 0 to 49
- gate_table: float32 [50, 5120], P(None, ('guide', 'tensor')), may hold values from -6 to 6
- residual: bfloat16 [2, 5120, 5120], P(None, 'patch', ('guide', 'tensor')), may hold values from -1.796875 to 1.796875
- out_weight: bfloat16 [2560, 5120], P('tensor', 'guide'), may hold values from -0.125 to 0.125
Outputs:
- guided: bfloat16 [5120, 5120], P('patch', ('guide', 'tensor'))
All inputs are finite; a program needn't handle non-finite values.
Results may differ from a plain program's by a relative error of at most 0.015.
Values may be sent and summed in bfloat16 or wider, within the bound.
No kernel may reach another device: no remote copies, remote signals or barrier semaphores. Data moves between devices by JAX's collectives and lax.ppermute only.
A program may use at most 128 MiB of HBM per device.

v0:
```python
import jax
import jax.numpy as jnp
from jax import lax
from jax.sharding import PartitionSpec as P

HD = 128


guide_scale = 5.0


def from_partner(value, axis, bit):
    return lax.ppermute(value, axis, [(i, i ^ 1 << bit) for i in range(lax.axis_size(axis))])


def shards(query, fresh_kv, stale_kv, assign, timestep, gate_table, residual, out_weight):
    tok_rows = query.shape[1]
    head_width = query.shape[2]
    head_count = head_width // HD
    score_scale = HD ** (-0.5)
    queries = query[0].reshape(tok_rows, head_count, HD)

    def absorb(carried, key_rows, value_rows, key_bias):
        maxima, totals, accumulated = carried
        count_rows = key_rows.shape[0]
        scores = jnp.einsum(
            "qhd,khd->hqk",
            queries,
            key_rows.reshape(count_rows, head_count, HD),
            preferred_element_type=jnp.float32,
        )
        scores = scores * score_scale + key_bias[None, None, :]
        new_maxima = jnp.maximum(maxima, jnp.max(scores, axis=-1))
        shrink = jnp.exp(maxima - new_maxima)
        weights = jnp.exp(scores - new_maxima[..., None])
        totals = totals * shrink + jnp.sum(weights, axis=-1)
        update = jnp.einsum(
            "hqk,khd->hqd",
            weights.astype(jnp.bfloat16),
            value_rows.reshape(count_rows, head_count, HD),
            preferred_element_type=jnp.float32,
        )
        accumulated = accumulated * shrink[..., None] + update
        return (new_maxima, totals, accumulated)

    start_carry = (
        jnp.full((head_count, tok_rows), -1e30, jnp.float32),
        jnp.zeros((head_count, tok_rows), jnp.float32),
        jnp.zeros((head_count, tok_rows, HD), jnp.float32),
    )
    carried = absorb(
        start_carry, fresh_kv[0, 0], fresh_kv[0, 1], jnp.zeros((tok_rows,), jnp.float32)
    )
    gathered = lax.all_gather(stale_kv, "patch", axis=2, tiled=True)
    row_ids = jnp.arange(gathered.shape[2], dtype=jnp.int32)
    is_own = jnp.any(row_ids[:, None] == assign[None, :], axis=1)
    carried = absorb(
        carried,
        gathered[0, 0],
        gathered[0, 1],
        jnp.where(is_own, jnp.float32(-1e30), jnp.float32(0.0)),
    )
    maxima, totals, accumulated = carried
    attended = (
        (accumulated / totals[..., None])
        .transpose(1, 0, 2)
        .reshape(tok_rows, head_width)
        .astype(jnp.bfloat16)
    )
    swapped = from_partner(attended, "guide", 0)
    is_cond = lax.axis_index("guide") == 0
    cond_out = jnp.where(is_cond, attended, swapped)
    uncond_out = jnp.where(is_cond, swapped, attended)
    proj_cond = jnp.dot(cond_out, out_weight, preferred_element_type=jnp.float32)
    proj_uncond = jnp.dot(uncond_out, out_weight, preferred_element_type=jnp.float32)
    step_count = gate_table.shape[0]
    chosen = jnp.arange(step_count, dtype=jnp.int32) == timestep[0]
    gate_row = jnp.sum(jnp.where(chosen[:, None], gate_table, jnp.float32(0.0)), axis=0)
    residual_f = residual.astype(jnp.float32)
    summed = lax.psum_scatter(
        jnp.stack([proj_cond, proj_uncond]).astype(jnp.bfloat16),
        "tensor",
        scatter_dimension=2,
        tiled=True,
    ).astype(jnp.float32)
    block_cond = residual_f[0] + gate_row[None, :] * summed[0]
    block_uncond = residual_f[1] + gate_row[None, :] * summed[1]
    guided = block_uncond + guide_scale * (block_cond - block_uncond)
    return guided.astype(jnp.bfloat16)


def solution(mesh):
    placed = (
        P("guide", "patch", "tensor"),
        P("guide", None, "patch", "tensor"),
        P("guide", None, "patch", "tensor"),
        P("patch"),
        P(),
        P(None, ("guide", "tensor")),
        P(None, "patch", ("guide", "tensor")),
        P("tensor", "guide"),
    )
    return jax.shard_map(
        shards,
        mesh=mesh,
        in_specs=placed,
        out_specs=P("patch", ("guide", "tensor")),
        check_vma=False,
    )
```

profile of v0, /device:TPU:1, one launch (start us, length us, event | category | flops | bytes accessed | tf_op | source)
XLA Modules:
  0.0 352.7 jit_solution(9586994175986765069)
XLA Ops:
  6.5 1.9 copy.36
  8.5 0.0 all-gather.2.cloned.1.call-update
  8.5 0.0 reduce-scatter.4.cloned.1.call-start
  8.5 1.0 reshape_squeeze.15
  9.6 1.6 fusion.44
  11.2 1.7 reshape_squeeze.16
  12.9 0.8 reshape_squeeze.17
  13.7 0.9 fusion.7
  14.6 1.8 fusion.45
  16.4 171.3 %all-gather.2.cloned.1.call-done = bf16[1,2,5120,640]{3,1,0,2:T(2,128)(2,1)} async-done(((bf16[1,2,80,640]{3,1,0,2:T(2,128)(2,1)}), bf16[1,2,5120,640]{3,1,0,2:T(2,128)(2,1)}) %all-gather.2.cloned.1.call-update) | async-done | bytes 13107216 | tf_op jit(solution)/shard_map/all_gather | solution.py:54
  187.7 26.1 %fusion.43 = (bf16[1,1,5120,640]{3,1,0,2:T(2,128)(2,1)}, bf16[1,1,5120,640]{3,1,0,2:T(2,128)(2,1)}) fusion(bf16[1,2,5120,640]{3,1,0,2:T(2,128)(2,1)} %all-gather.2.cloned.1.call-done), kind=kLoop, calls=%fused_computation.60 | loop fusion | bytes 26214400 | tf_op jit(solution)/shard_map/slice | solution.py:59
  213.8 26.0 %copy.48 = bf16[1,1,5120,640]{2,3,1,0:T(8,128)(2,1)} copy(bf16[1,1,5120,640]{3,1,0,2:T(2,128)(2,1)} %get-tuple-element.7) | data formatting | bytes 13107200
  239.8 26.0 %copy.49 = bf16[1,1,5120,640]{2,3,1,0:T(8,128)(2,1)} copy(bf16[1,1,5120,640]{3,1,0,2:T(2,128)(2,1)} %get-tuple-element.8) | data formatting | bytes 13107200
  265.9 4.4 %fusion.46 = (f32[5,80]{1,0:T(8,128)S(1)}, f32[5,80,5120]{2,1,0:T(8,128)S(1)}) fusion(f32[5120]{0:T(1024)S(1)} %broadcast_select_fusion, bf16[5120,5,128]{0,2,1:T(8,128)(2,1)} %bitcast.96, bf16[80,5,128]{2,1,0:T(8,128)(2,1)S(1)} %reshape_squeeze.15), kind=kOutput, calls=%fused_computation.63 | convolution fusion | flops 530431616 | bytes 14870080 | tf_op jit(solution)/shard_map/qhd,khd->hqk/dot_general | solution.py:26
  270.3 1.3 fusion
  271.6 5.5 %fusion.12 = f32[80,5,128]{2,0,1:T(8,128)S(1)} fusion(bf16[5120,5,128]{0,2,1:T(8,128)(2,1)} %bitcast.97, f32[5,80,5120]{2,1,0:T(8,128)S(1)} %get-tuple-element.17, f32[5,80]{1,0:T(8,128)S(1)} %get-tuple-element.13), kind=kOutput, calls=%fused_computation.18 | convolution fusion | flops 528384000 | bytes 14952000 | tf_op jit(solution)/shard_map/hqk,khd->hqd/dot_general | solution.py:37
  277.2 0.3 fusion.16
  277.5 0.7 copy.72
  278.1 3.1 collective-permute-start
  281.3 2.5 collective-permute-done
  283.7 0.7 fusion.5
  284.5 0.7 fusion.6
  285.2 1.0 pad_maximum_fusion
  286.2 3.8 %copy.46 = bf16[2,80,2560]{1,0,2:T(2,128)(2,1)} copy(bf16[2,80,2560]{2,1,0:T(8,128)(2,1)} %pad_maximum_fusion) | data formatting | bytes 1638400
  289.9 3.9 %reshape.41 = bf16[2560,160]{1,0:T(8,128)(2,1)} reshape(bf16[2560,2,80]{2,1,0:T(2,128)(2,1)} %bitcast.98) | data formatting | bytes 1638400
  293.9 0.0 reduce-scatter.4.cloned.1.call-update
  293.9 1.7 convert_element_type.22
  296.3 0.1 select_reduce_fusion
  296.4 44.6 %reduce-scatter.4.cloned.1.call-done = bf16[640,160]{1,0:T(8,128)(2,1)} async-done(((bf16[2560,160]{1,0:T(8,128)(2,1)}), bf16[640,160]{1,0:T(8,128)(2,1)}) %reduce-scatter.4.cloned.1.call-update) | async-done | bytes 204816
  341.0 1.9 reshape.42
  342.9 1.2 copy.47
  344.1 1.7 fusion.22
  (15 shorter events, 0.1 us)
Async XLA Ops:
  6.5 277.2 %copy-start = (bf16[640,2560]{1,0:T(8,128)(2,1)S(1)}, bf16[640,2560]{1,0:T(8,128)(2,1)}, u32[]{:S(2)}) copy-start(bf16[640,2560]{1,0:T(8,128)(2,1)} %param.15) | copy-start | bytes 9830404
  6.5 181.2 %all-gather.2.cloned.1.call-start = ((), (), s32[]{:S(2)}) async-start(), calls=%async_computation.1 | async-start | bytes 13312000 | tf_op jit(solution)/shard_map/all_gather | solution.py:54
  8.5 332.5 %reduce-scatter.4.cloned.1.call-start = ((), (), s32[]{:S(2)}) async-start(), calls=%async_computation.2 | async-start | bytes 1638400
  271.6 5.5 %copy-start.1 = (f32[5,80,80]{1,2,0:T(8,128)S(1)}, f32[5,80,80]{1,2,0:T(8,128)}, u32[]{:S(2)}) copy-start(f32[5,80,80]{1,2,0:T(8,128)} %get-tuple-element.15) | copy-start | bytes 384004
  271.6 5.6 %copy-start.2 = (bf16[80,5,128]{2,1,0:T(8,128)(2,1)S(1)}, bf16[80,5,128]{2,1,0:T(8,128)(2,1)}, u32[]{:S(2)}) copy-start(bf16[80,5,128]{2,1,0:T(8,128)(2,1)} %reshape_squeeze.17) | copy-start | bytes 307204
  278.1 5.6 %collective-permute-start = (bf16[80,640]{1,0:T(8,128)(2,1)}, bf16[80,640]{1,0:T(8,128)(2,1)S(1)}, u32[]{:S(2)}, u32[]{:S(2)}) collective-permute-start(bf16[80,640]{1,0:T(8,128)(2,1)} %bitcast.94), channel_id=1, source_target_pairs={{0,256},{256,0},{1,257},{257,1},{2,258},{258,2},{3,259},{259,3},{4... | collective-permute-start | bytes 307208 | tf_op jit(solution)/shard_map/ppermute | solution.py:13
  285.2 11.1 %copy-start.3 = (f32[50,640]{1,0:T(8,128)S(1)}, f32[50,640]{1,0:T(8,128)}, u32[]{:S(2)}) copy-start(f32[50,640]{1,0:T(8,128)} %param.13) | copy-start | bytes 384004
Sparse Core Ops, SparseCore 0:
  10.3 177.3 all-gather.1
  294.0 46.9 reduce-scatter.3
where the time goes:
time: 354 us; the launch traced here: 353 us
  waiting for transfers between devices  218 us (62%)
  local copies, waits for them, and re-layouts  96.6 us (27%)
  between operations  14.2 us (4%)
  matrix products  13.4 us (4%)
  other arithmetic  6.82 us (2%)
    all_gather x1, waiting for transfers between devices, shards(): gathered = lax.all_gather(stale_kv, 'patch', axis=2, tiled=True)  171 us
    unnamed x15, local copies, waits for them, and re-layouts  64.7 us
    unnamed x3, waiting for transfers between devices  44.7 us
    slice x1, local copies, waits for them, and re-layouts, shards(): gathered[0, 0]  26.1 us
  transfers between devices with their start and end apart: 3, of which 3 were waited for; matrix products, arithmetic and copies ran while one was open for 3% of the time, Pallas kernels for 0%

commit v1 on v0

v1 whole, which is shorter than its diff:
```python
import functools

import jax
import jax.numpy as jnp
from jax import lax
from jax.experimental import pallas as pl
from jax.experimental.pallas import tpu as pltpu
from jax.sharding import Mesh
from jax.sharding import PartitionSpec as P

HD = 128
LANES = 128
GUIDE = 5.0
MASKED = -1e30
SCALE = HD**-0.5
VMEM = pl.BlockSpec(memory_space=pltpu.VMEM)
SMEM = pl.BlockSpec(memory_space=pltpu.SMEM)
PARAMS = pltpu.CompilerParams(vmem_limit_bytes=40 * 1024 * 1024)


def shift(value, axis, step):
    size = lax.axis_size(axis)
    return lax.ppermute(value, axis, [(i, (i + step) % size) for i in range(size)])


def head_lanes(head):
    return slice(head * HD, (head + 1) * HD)


def softmax_part(queries, keys, values, bias):
    scores = lax.dot_general(
        queries, keys, (((1,), (1,)), ((), ())), preferred_element_type=jnp.float32
    )
    scores = scores * SCALE
    if bias is not None:
        slabs = bias.shape[0]
        scores = (scores.reshape(slabs, -1, scores.shape[1]) + bias).reshape(scores.shape)
    maxima = jnp.max(scores, axis=1, keepdims=True)
    weights = jnp.exp(scores - maxima)
    totals = jnp.sum(weights, axis=1, keepdims=True)
    update = jnp.dot(weights.astype(jnp.bfloat16), values, preferred_element_type=jnp.float32)
    return update / totals, maxima, totals


def in_three(value):
    high = value.astype(jnp.bfloat16).astype(jnp.float32)
    mid = (value - high).astype(jnp.bfloat16).astype(jnp.float32)
    return [high, mid, value - high - mid]


def fresh_kernel(query_ref, fresh_ref, out_ref, stats_ref):
    rows, width = query_ref.shape
    lane = lax.broadcasted_iota(jnp.int32, (rows, LANES), 1)
    stats = jnp.zeros((rows, LANES), jnp.float32)
    for head in range(width // HD):
        at = head_lanes(head)
        part, maxima, totals = softmax_part(
            query_ref[:, at], fresh_ref[0, :, at], fresh_ref[1, :, at], None
        )
        out_ref[:, at] = part
        stats = jnp.where(lane == 2 * head, maxima, stats)
        stats = jnp.where(lane == 2 * head + 1, totals, stats)
    stats_ref[...] = stats


def stale_kernel(keys_ref, query_ref, *refs):
    blocks, last_key, last_value, out_ref = refs[:-3], refs[-3], refs[-2], refs[-1]
    slabs, rows, wide = query_ref.shape
    width = wide - LANES
    owned = query_ref[:, :, width : width + LANES].astype(jnp.float32)
    key_ids = keys_ref[0:1, :]
    bias = []
    for slab in range(slabs):
        own_ids = owned[slab, :, 0:1] * float(LANES) + owned[slab, :, 1:2]
        bias.append(
            jnp.min(
                jnp.where(own_ids == key_ids, jnp.float32(MASKED), jnp.float32(0.0)),
                axis=0,
                keepdims=True,
            )[None]
        )
    bias = jnp.concatenate(bias, axis=0)
    lane = lax.broadcasted_iota(jnp.int32, (slabs * rows, LANES), 1)
    stats = jnp.zeros((slabs * rows, LANES), jnp.float32)
    for head in range(width // HD):
        at = head_lanes(head)
        keys = jnp.concatenate([b[0, :, at] for b in blocks] + [last_key[:, at]], axis=0)
        values = jnp.concatenate([b[1, :, at] for b in blocks] + [last_value[:, at]], axis=0)
        queries = query_ref[:, :, at].reshape(slabs * rows, HD)
        part, maxima, totals = softmax_part(queries, keys, values, bias)
        out_ref[:, :, at] = part.astype(jnp.bfloat16).reshape(slabs, rows, HD)
        for place, piece in enumerate(in_three(maxima) + in_three(totals)):
            stats = jnp.where(lane == 6 * head + place, piece, stats)
    out_ref[:, :, width:] = stats.astype(jnp.bfloat16).reshape(slabs, rows, LANES)


def combine_kernel(parts_ref, fresh_ref, fresh_stats_ref, out_ref):
    count, rows, wide = parts_ref.shape
    width = wide - LANES
    stats = parts_ref[:, :, width:].astype(jnp.float32)

    def from_three(part, first):
        high, mid, low = (stats[part, :, first + k : first + k + 1] for k in range(3))
        return high + mid + low

    for head in range(width // HD):
        at = head_lanes(head)
        maxima = [from_three(i, 6 * head) for i in range(count)]
        totals = [from_three(i, 6 * head + 3) for i in range(count)]
        maxima.append(fresh_stats_ref[:, 2 * head : 2 * head + 1])
        totals.append(fresh_stats_ref[:, 2 * head + 1 : 2 * head + 2])
        highest = functools.reduce(jnp.maximum, maxima)
        shares = [
            jnp.exp(maximum - highest) * total
            for maximum, total in zip(maxima, totals, strict=True)
        ]
        total = functools.reduce(jnp.add, shares)
        joined = fresh_ref[:, at] * shares[-1]
        for i in range(count):
            joined = joined + parts_ref[i, :, at].astype(jnp.float32) * shares[i]
        out_ref[:, at] = (joined / total).astype(jnp.bfloat16)


def project_kernel(factor_ref, own_ref, other_ref, weight_ref, out_ref):
    mixed = own_ref[...].astype(jnp.float32) * factor_ref[0] + other_ref[...].astype(
        jnp.float32
    ) * factor_ref[1]
    out_ref[0] = jnp.dot(
        mixed.astype(jnp.bfloat16), weight_ref[...], preferred_element_type=jnp.float32
    ).astype(jnp.bfloat16)


def shards(query, fresh_kv, stale_kv, assign, timestep, gate_table, residual, out_weight):
    rows, width = query.shape[1:]
    ring = lax.axis_size("zh")
    slabs = lax.axis_size("x") * lax.axis_size("zl")
    parts = lax.axis_size("t")

    places = jnp.stack([assign // LANES, assign % LANES], axis=1).astype(jnp.bfloat16)
    message = jnp.concatenate(
        [query[0], places, jnp.zeros((rows, LANES - 2), jnp.bfloat16)], axis=1
    )
    queries = lax.all_to_all(
        jnp.broadcast_to(message[None], (slabs, *message.shape)), ("x", "zl"), 0, 0
    )

    own_kv = stale_kv[0]
    blocks, offsets = [own_kv], [0]
    ahead = behind = own_kv
    for step in range(1, ring // 2):
        ahead = shift(ahead, "zh", 1)
        behind = shift(behind, "zh", -1)
        blocks += [ahead, behind]
        offsets += [-step, step]
    last_key = shift(ahead[0], "zh", 1)
    last_value = shift(behind[1], "zh", -1)
    offsets.append(ring // 2)
    z_far = (lax.axis_index("zh") + jnp.array(offsets, jnp.int32)) % ring
    slab_ids = (lax.axis_index("x") * ring + z_far) * lax.axis_size("zl") + lax.axis_index("zl")
    key_ids = (slab_ids[:, None] * rows + jnp.arange(rows, dtype=jnp.int32)).reshape(1, -1)
    key_ids = jnp.broadcast_to(key_ids.astype(jnp.float32), (8, key_ids.shape[1]))

    fresh_out, fresh_stats = pl.pallas_call(
        fresh_kernel,
        out_shape=(
            jax.ShapeDtypeStruct((rows, width), jnp.float32),
            jax.ShapeDtypeStruct((rows, LANES), jnp.float32),
        ),
        in_specs=[VMEM] * 2,
        out_specs=(VMEM, VMEM),
        compiler_params=PARAMS,
        name="fresh",
    )(query[0], fresh_kv[0])

    stale_out = pl.pallas_call(
        stale_kernel,
        out_shape=jax.ShapeDtypeStruct((slabs, rows, width + LANES), jnp.bfloat16),
        in_specs=[VMEM] * (len(blocks) + 4),
        out_specs=VMEM,
        compiler_params=PARAMS,
        name="stale",
    )(key_ids, queries, *blocks, last_key, last_value)
    stale_out = lax.all_to_all(stale_out, ("x", "zl"), 0, 0)

    attended = pl.pallas_call(
        combine_kernel,
        out_shape=jax.ShapeDtypeStruct((rows, width), jnp.bfloat16),
        in_specs=[VMEM] * 3,
        out_specs=VMEM,
        compiler_params=PARAMS,
        name="combine",
    )(stale_out, fresh_out, fresh_stats)

    other = shift(attended, "g", 1)
    factors = jnp.where(
        lax.axis_index("g") == 0,
        jnp.array([GUIDE, 1.0 - GUIDE], jnp.float32),
        jnp.array([1.0 - GUIDE, GUIDE], jnp.float32),
    )
    columns = out_weight.shape[1] // parts
    projected = pl.pallas_call(
        project_kernel,
        out_shape=jax.ShapeDtypeStruct((parts, rows, columns), jnp.bfloat16),
        grid=(parts,),
        in_specs=[
            SMEM,
            pl.BlockSpec((rows, width), lambda i: (0, 0)),
            pl.BlockSpec((rows, width), lambda i: (0, 0)),
            pl.BlockSpec((width, columns), lambda i: (0, i)),
        ],
        out_specs=pl.BlockSpec((1, rows, columns), lambda i: (i, 0, 0)),
        compiler_params=PARAMS,
        name="project",
    )(factors, attended, other, out_weight)
    projected = lax.all_to_all(projected, "t", 0, 0)

    chosen = jnp.arange(gate_table.shape[0], dtype=jnp.int32) == timestep[0]
    gate_row = jnp.sum(jnp.where(chosen[:, None], gate_table, jnp.float32(0.0)), axis=0)
    summed = jnp.sum(projected.astype(jnp.float32), axis=0)
    residual_f = residual.astype(jnp.float32)
    base = residual_f[1] + GUIDE * (residual_f[0] - residual_f[1])
    return (base + gate_row[None, :] * summed).astype(jnp.bfloat16)


def solution(mesh):
    guide, patch, tensor = mesh.devices.shape
    x_size, z_low = 4, 2
    z_high = patch // (x_size * z_low)
    fine = Mesh(
        mesh.devices.reshape(guide, x_size, z_high, z_low, tensor), ("g", "x", "zh", "zl", "t")
    )
    slab = ("x", "zh", "zl")
    placed = (
        P("g", slab, "t"),
        P("g", None, slab, "t"),
        P("g", None, slab, "t"),
        P(slab),
        P(),
        P(None, ("g", "t")),
        P(None, slab, ("g", "t")),
        P("t", "g"),
    )
    return jax.shard_map(
        shards,
        mesh=fine,
        in_specs=placed,
        out_specs=P(slab, ("g", "t")),
        check_vma=False,
    )
```

time: 354 us -> 128 us (0.36)
  waiting for transfers between devices: 218 us -> 48.4 us
  local copies, waits for them, and re-layouts: 96.6 us -> 3.4 us
  starting transfers between devices: 3.14 us -> 61.2 us
  matrix products: 13.4 us -> 0 us
  between operations: 14.2 us -> 0.9 us
  Pallas kernels: 0 us -> 10.4 us
  other arithmetic: 6.82 us -> 2.65 us
    all_gather x1 -> x0, waiting for transfers between devices: 171 us -> none  [shards(): gathered = lax.all_gather(stale_kv, 'patch', axis=2, tiled=True)]
    unnamed x15 -> x18, local copies, waits for them, and re-layouts: 64.7 us -> 1.96 us
    unnamed x3 -> x0, waiting for transfers between devices: 44.7 us -> none
    ppermute x1 -> x9, starting transfers between devices: 3.1 us -> 41.7 us  [shift(): lax.ppermute(value, axis, [(i, (i + step) % size) for i in range(size)])]
    slice x2 -> x0, local copies, waits for them, and re-layouts: 27.7 us -> none  [the longest x1 26.1 us: shards(): gathered[0, 0]]
    ppermute x1 -> x9, waiting for transfers between devices: 2.49 us -> 29.5 us  [shift(): lax.ppermute(value, axis, [(i, (i + step) % size) for i in range(size)])]
    all_to_all x0 -> x3, starting transfers between devices: none -> 19.5 us  [the longest x1 9.5 us: shards(): projected = lax.all_to_all(projected, 't', 0, 0)]
    all_to_all x0 -> x3, waiting for transfers between devices: none -> 18.9 us  [the longest x1 11.5 us: shards(): stale_out = lax.all_to_all(stale_out, ('x', 'zl'), 0, 0)]
  transfers between devices with their start and end apart: 3 -> 12, of which waited for: 3 -> 7; matrix products, arithmetic and copies ran while one was open for 3% -> 0% of each run, Pallas kernels for 0% -> 1%
where the time goes in v1:
time: 128 us; the launch traced here: 127 us
  starting transfers between devices  61.2 us (48%)
  waiting for transfers between devices  48.4 us (38%)
  Pallas kernels  10.4 us (8%)
  local copies, waits for them, and re-layouts  3.4 us (3%)
  other arithmetic  2.65 us (2%)
    ppermute x9, starting transfers between devices, shift(): lax.ppermute(value, axis, [(i, (i + step) % size) for i in range(size)])  41.7 us
    ppermute x9, waiting for transfers between devices, shift(): lax.ppermute(value, axis, [(i, (i + step) % size) for i in range(size)])  29.5 us
    all_to_all x1, waiting for transfers between devices, shards(): stale_out = lax.all_to_all(stale_out, ('x', 'zl'), 0, 0)  11.5 us
    all_to_all x1, starting transfers between devices, shards(): projected = lax.all_to_all(projected, 't', 0, 0)  9.5 us
    all_to_all x1, waiting for transfers between devices, shards(): projected = lax.all_to_all(projected, 't', 0, 0)  7.45 us
    all_to_all x1, starting transfers between devices, shards(): lax.all_to_all(jnp.broadcast_to(message[None], (slabs, *message.shape)),...  6.2 us
    pallas_call x1, Pallas kernels, shards(): pl.pallas_call(stale_kernel, out_shape=jax.ShapeDtypeStruct((slabs, rows,...  5.33 us
    all_to_all x1, starting transfers between devices, shards(): stale_out = lax.all_to_all(stale_out, ('x', 'zl'), 0, 0)  3.79 us
  transfers between devices with their start and end apart: 12, of which 7 were waited for; matrix products, arithmetic and copies ran while one was open for 0% of the time, Pallas kernels for 1%

profile of v1, /device:TPU:1, one launch (start us, length us, event | category | flops | bytes accessed | tf_op | source)
XLA Modules:
  0.0 127.0 jit_solution(2971250759402099831)
XLA Ops:
  0.0 0.7 convert_bitcast_fusion
  0.7 0.1 copy.12
  0.8 0.1 copy.13
  1.0 0.1 pad.3.clone
  1.0 1.0 maximum_maximum_fusion
  2.0 1.0 broadcast_in_dim.34
  3.0 6.2 %all-to-all-start = ((bf16[8,80,768]{2,1,0:T(8,128)(2,1)}), bf16[8,80,768]{2,1,0:T(8,128)(2,1)S(1)}, u32[]{:S(2)}, u32[]{:S(2)}) async-start(bf16[8,80,768]{2,1,0:T(8,128)(2,1)} %broadcast_in_dim.34), calls=%async_computation | async-start | bytes 1966080 | tf_op jit(solution)/shard_map/all_to_all | solution.py:143
  9.3 5.0 %collective-permute-start = (bf16[2,80,640]{2,1,0:T(8,128)(2,1)S(1)}, bf16[2,80,640]{2,1,0:T(8,128)(2,1)S(1)}, u32[]{:S(2)}, u32[]{:S(2)}) collective-permute-start(bf16[2,80,640]{2,1,0:T(8,128)(2,1)S(1)} %bitcast.31), channel_id=1, source_target_pairs={{0,8},{8,16},{16,24},{24,32},{32,40},{40,48},{48,56},{56,0},{1,9},... | collective-permute-start | bytes 614408 | tf_op jit(solution)/shard_map/ppermute | solution.py:23
  14.3 7.7 %collective-permute-start.1 = (bf16[2,80,640]{2,1,0:T(8,128)(2,1)S(1)}, bf16[2,80,640]{2,1,0:T(8,128)(2,1)S(1)}, u32[]{:S(2)}, u32[]{:S(2)}) collective-permute-start(bf16[2,80,640]{2,1,0:T(8,128)(2,1)S(1)} %bitcast.32), channel_id=1, source_target_pairs={{0,56},{8,0},{16,8},{24,16},{32,24},{40,32},{48,40},{56,48},{1,57}... | collective-permute-start | bytes 614408 | tf_op jit(solution)/shard_map/ppermute | solution.py:23
  22.0 20.0 %collective-permute-done.refs_1_ = bf16[2,80,640]{2,1,0:T(8,128)(2,1)S(1)} collective-permute-done((bf16[2,80,640]{2,1,0:T(8,128)(2,1)S(1)}, bf16[2,80,640]{2,1,0:T(8,128)(2,1)S(1)}, u32[]{:S(2)}, u32[]{:S(2)}) %collective-permute-start) | collective-permute-done | bytes 204832 | tf_op jit(solution)/shard_map/ppermute | solution.py:23
  42.0 1.9 %collective-permute-start.2 = (bf16[2,80,640]{2,1,0:T(8,128)(2,1)S(1)}, bf16[2,80,640]{2,1,0:T(8,128)(2,1)S(1)}, u32[]{:S(2)}, u32[]{:S(2)}) collective-permute-start(bf16[2,80,640]{2,1,0:T(8,128)(2,1)S(1)} %collective-permute-done.refs_1_), channel_id=1, source_target_pairs={{0,8},{8,16},{16,24},{24,32},{32,40},{40,48},{48,56},{56,0},{1,9},... | collective-permute-start | bytes 614408 | tf_op jit(solution)/shard_map/ppermute | solution.py:23
  43.9 5.5 %collective-permute-start.3 = (bf16[2,80,640]{2,1,0:T(8,128)(2,1)S(1)}, bf16[2,80,640]{2,1,0:T(8,128)(2,1)S(1)}, u32[]{:S(2)}, u32[]{:S(2)}) collective-permute-start(bf16[2,80,640]{2,1,0:T(8,128)(2,1)S(1)} %collective-permute-done.1.refs_2_), channel_id=1, source_target_pairs={{0,56},{8,0},{16,8},{24,16},{32,24},{40,32},{48,40},{56,48},{1,57}... | collective-permute-start | bytes 614408 | tf_op jit(solution)/shard_map/ppermute | solution.py:23
  49.4 3.6 %collective-permute-done.2.refs_3_ = bf16[2,80,640]{2,1,0:T(8,128)(2,1)S(1)} collective-permute-done((bf16[2,80,640]{2,1,0:T(8,128)(2,1)S(1)}, bf16[2,80,640]{2,1,0:T(8,128)(2,1)S(1)}, u32[]{:S(2)}, u32[]{:S(2)}) %collective-permute-start.2) | collective-permute-done | bytes 204832 | tf_op jit(solution)/shard_map/ppermute | solution.py:23
  53.0 5.0 %collective-permute-start.4 = (bf16[2,80,640]{2,1,0:T(8,128)(2,1)S(1)}, bf16[2,80,640]{2,1,0:T(8,128)(2,1)S(1)}, u32[]{:S(2)}, u32[]{:S(2)}) collective-permute-start(bf16[2,80,640]{2,1,0:T(8,128)(2,1)S(1)} %collective-permute-done.2.refs_3_), channel_id=1, source_target_pairs={{0,8},{8,16},{16,24},{24,32},{32,40},{40,48},{48,56},{56,0},{1,9},... | collective-permute-start | bytes 614408 | tf_op jit(solution)/shard_map/ppermute | solution.py:23
  58.1 4.8 %collective-permute-start.5 = (bf16[2,80,640]{2,1,0:T(8,128)(2,1)S(1)}, bf16[2,80,640]{2,1,0:T(8,128)(2,1)S(1)}, u32[]{:S(2)}, u32[]{:S(2)}) collective-permute-start(bf16[2,80,640]{2,1,0:T(8,128)(2,1)S(1)} %collective-permute-done.3.refs_4_), channel_id=1, source_target_pairs={{0,56},{8,0},{16,8},{24,16},{32,24},{40,32},{48,40},{56,48},{1,57}... | collective-permute-start | bytes 614408 | tf_op jit(solution)/shard_map/ppermute | solution.py:23
  62.9 5.2 %collective-permute-start.6 = (bf16[80,640]{1,0:T(8,128)(2,1)S(1)}, bf16[80,640]{1,0:T(8,128)(2,1)S(1)}, u32[]{:S(2)}, u32[]{:S(2)}) collective-permute-start(bf16[80,640]{1,0:T(8,128)(2,1)S(1)} %slice_bitcast_fusion.3), channel_id=1, source_target_pairs={{0,8},{8,16},{16,24},{24,32},{32,40},{40,48},{48,56},{56,0},{1,9},... | collective-permute-start | bytes 307208 | tf_op jit(solution)/shard_map/ppermute | solution.py:23
  68.0 1.0 collective-permute-done.5.refs_6_
  69.1 3.5 %collective-permute-start.7 = (bf16[80,640]{1,0:T(8,128)(2,1)S(1)}, bf16[80,640]{1,0:T(8,128)(2,1)S(1)}, u32[]{:S(2)}, u32[]{:S(2)}) collective-permute-start(bf16[80,640]{1,0:T(8,128)(2,1)S(1)} %slice_bitcast_fusion.2), channel_id=1, source_target_pairs={{0,56},{8,0},{16,8},{24,16},{32,24},{40,32},{48,40},{56,48},{1,57}... | collective-permute-start | bytes 307208 | tf_op jit(solution)/shard_map/ppermute | solution.py:23
  72.8 2.6 %collective-permute-done.7.refs_8_ = bf16[80,640]{1,0:T(8,128)(2,1)S(1)} collective-permute-done((bf16[80,640]{1,0:T(8,128)(2,1)S(1)}, bf16[80,640]{1,0:T(8,128)(2,1)S(1)}, u32[]{:S(2)}, u32[]{:S(2)}) %collective-permute-start.7) | collective-permute-done | bytes 102432 | tf_op jit(solution)/shard_map/ppermute | solution.py:23
  75.4 5.3 %stale.1 = bf16[8,80,768]{2,1,0:T(8,128)(2,1)} custom-call(f32[8,640]{1,0:T(8,128)S(1)} %broadcast_in_dim.32.keys_ref, bf16[8,80,768]{2,1,0:T(8,128)(2,1)S(1)} %all-to-all-done.query_ref, bf16[2,80,640]{2,1,0:T(8,128)(2,1)S(1)} %bitcast.33, bf16[2,80,640]{2,1,0:T(8,128)(2,1)S(1)} %collective-permute-done.refs_1_, ...), custom_call_target="tpu_custom_call" | custom-call | tf_op jit(solution)/shard_map/stale/pallas_call | solution.py:175
  80.7 3.8 %all-to-all-start.1 = ((bf16[8,80,768]{2,1,0:T(8,128)(2,1)}), bf16[8,80,768]{2,1,0:T(8,128)(2,1)S(1)}, u32[]{:S(2)}, u32[]{:S(2)}) async-start(bf16[8,80,768]{2,1,0:T(8,128)(2,1)} %stale.1), calls=%async_computation.1 | async-start | bytes 1966080 | tf_op jit(solution)/shard_map/all_to_all | solution.py:183
  84.6 0.6 fresh.1
  85.2 11.5 %all-to-all-done.1.parts_ref = bf16[8,80,768]{2,1,0:T(8,128)(2,1)S(1)} async-done(((bf16[8,80,768]{2,1,0:T(8,128)(2,1)}), bf16[8,80,768]{2,1,0:T(8,128)(2,1)S(1)}, u32[]{:S(2)}, u32[]{:S(2)}) %all-to-all-start.1) | async-done | bytes 983072 | tf_op jit(solution)/shard_map/all_to_all | solution.py:183
  96.7 1.6 %combine.1.own_ref = bf16[80,640]{1,0:T(8,128)(2,1)S(1)} custom-call(bf16[8,80,768]{2,1,0:T(8,128)(2,1)S(1)} %all-to-all-done.1.parts_ref, f32[80,640]{1,0:T(8,128)S(1)} %get-tuple-element.7.fresh_ref, f32[80,128]{1,0:T(8,128)S(1)} %get-tuple-element.8.fresh_stats_ref), custom_call_target="tpu_custom_call" | custom-call | tf_op jit(solution)/shard_map/combine/pallas_call | solution.py:185
  98.3 3.2 %collective-permute-start.8 = (bf16[80,640]{1,0:T(8,128)(2,1)S(1)}, bf16[80,640]{1,0:T(8,128)(2,1)S(1)}, u32[]{:S(2)}, u32[]{:S(2)}) collective-permute-start(bf16[80,640]{1,0:T(8,128)(2,1)S(1)} %combine.1.own_ref), channel_id=1, source_target_pairs={{0,256},{256,0},{1,257},{257,1},{2,258},{258,2},{3,259},{259,3},{4... | collective-permute-start | bytes 307208 | tf_op jit(solution)/shard_map/ppermute | solution.py:23
  101.5 2.1 %collective-permute-done.8.other_ref = bf16[80,640]{1,0:T(8,128)(2,1)S(1)} collective-permute-done((bf16[80,640]{1,0:T(8,128)(2,1)S(1)}, bf16[80,640]{1,0:T(8,128)(2,1)S(1)}, u32[]{:S(2)}, u32[]{:S(2)}) %collective-permute-start.8) | collective-permute-done | bytes 102432 | tf_op jit(solution)/shard_map/ppermute | solution.py:23
  103.7 1.9 %copy-done = bf16[640,2560]{1,0:T(8,128)(2,1)S(1)} copy-done((bf16[640,2560]{1,0:T(8,128)(2,1)S(1)}, bf16[640,2560]{1,0:T(8,128)(2,1)}, u32[]{:S(2)}) %copy-start) | copy-done | bytes 3276824
  105.6 2.9 %project.1 = bf16[4,80,640]{2,1,0:T(8,128)(2,1)} custom-call(f32[2]{0:T(128)S(1)} %broadcast_select_fusion.factor_ref, bf16[80,640]{1,0:T(8,128)(2,1)S(1)} %combine.1.own_ref, bf16[80,640]{1,0:T(8,128)(2,1)S(1)} %collective-permute-done.8.other_ref, bf16[640,2560]{1,0:T(8,128)(2,1)S(1)} %copy-done), custom_call_target="tpu_custom_call" | custom-call | tf_op jit(solution)/shard_map/project/pallas_call | solution.py:201
  108.5 9.5 %all-to-all-start.2 = ((bf16[4,80,640]{2,1,0:T(8,128)(2,1)}), bf16[4,80,640]{2,1,0:T(8,128)(2,1)S(1)}, u32[]{:S(2)}, u32[]{:S(2)}) async-start(bf16[4,80,640]{2,1,0:T(8,128)(2,1)} %project.1), calls=%async_computation.2 | async-start | bytes 819200 | tf_op jit(solution)/shard_map/all_to_all | solution.py:215
  118.7 0.1 select_reduce_fusion
  118.8 7.5 %all-to-all-done.2 = bf16[4,80,640]{2,1,0:T(8,128)(2,1)S(1)} async-done(((bf16[4,80,640]{2,1,0:T(8,128)(2,1)}), bf16[4,80,640]{2,1,0:T(8,128)(2,1)S(1)}, u32[]{:S(2)}, u32[]{:S(2)}) %all-to-all-start.2) | async-done | bytes 409632 | tf_op jit(solution)/shard_map/all_to_all | solution.py:215
  126.3 0.7 fusion.4
  (33 shorter events, 0.4 us)
Async XLA Ops:
  0.0 58.0 %copy-start.6 = (s32[8]{0:T(128)S(1)}, s32[8]{0:T(128)}, u32[]{:S(2)}) copy-start(s32[8]{0:T(128)} %constant.77.clone) | copy-start | bytes 100
  0.0 9.3 %copy-start.2 = (bf16[1,2,80,640]{3,2,1,0:T(8,128)(2,1)S(1)}, bf16[1,2,80,640]{3,2,1,0:T(8,128)(2,1)}, u32[]{:S(2)}) copy-start(bf16[1,2,80,640]{3,2,1,0:T(8,128)(2,1)} %param.13) | copy-start | bytes 614404
  3.0 72.4 %all-to-all-start = ((bf16[8,80,768]{2,1,0:T(8,128)(2,1)}), bf16[8,80,768]{2,1,0:T(8,128)(2,1)S(1)}, u32[]{:S(2)}, u32[]{:S(2)}) async-start(bf16[8,80,768]{2,1,0:T(8,128)(2,1)} %broadcast_in_dim.34), calls=%async_computation | async-start | bytes 1966080 | tf_op jit(solution)/shard_map/all_to_all | solution.py:143
  9.2 75.3 %copy-start.1 = (bf16[1,80,640]{2,1,0:T(8,128)(2,1)S(1)}, bf16[1,80,640]{2,1,0:T(8,128)(2,1)}, u32[]{:S(2)}) copy-start(bf16[1,80,640]{2,1,0:T(8,128)(2,1)} %param.11) | copy-start | bytes 307204
  9.2 75.3 %copy-start.3 = (bf16[1,2,80,640]{3,2,1,0:T(8,128)(2,1)S(1)}, bf16[1,2,80,640]{3,2,1,0:T(8,128)(2,1)}, u32[]{:S(2)}) copy-start(bf16[1,2,80,640]{3,2,1,0:T(8,128)(2,1)} %param.12) | copy-start | bytes 614404
  9.3 32.7 %collective-permute-start = (bf16[2,80,640]{2,1,0:T(8,128)(2,1)S(1)}, bf16[2,80,640]{2,1,0:T(8,128)(2,1)S(1)}, u32[]{:S(2)}, u32[]{:S(2)}) collective-permute-start(bf16[2,80,640]{2,1,0:T(8,128)(2,1)S(1)} %bitcast.31), channel_id=1, source_target_pairs={{0,8},{8,16},{16,24},{24,32},{32,40},{40,48},{48,56},{56,0},{1,9},... | collective-permute-start | bytes 614408 | tf_op jit(solution)/shard_map/ppermute | solution.py:23
  14.3 29.6 %collective-permute-start.1 = (bf16[2,80,640]{2,1,0:T(8,128)(2,1)S(1)}, bf16[2,80,640]{2,1,0:T(8,128)(2,1)S(1)}, u32[]{:S(2)}, u32[]{:S(2)}) collective-permute-start(bf16[2,80,640]{2,1,0:T(8,128)(2,1)S(1)} %bitcast.32), channel_id=1, source_target_pairs={{0,56},{8,0},{16,8},{24,16},{32,24},{40,32},{48,40},{56,48},{1,57}... | collective-permute-start | bytes 614408 | tf_op jit(solution)/shard_map/ppermute | solution.py:23
  42.0 11.0 %collective-permute-start.2 = (bf16[2,80,640]{2,1,0:T(8,128)(2,1)S(1)}, bf16[2,80,640]{2,1,0:T(8,128)(2,1)S(1)}, u32[]{:S(2)}, u32[]{:S(2)}) collective-permute-start(bf16[2,80,640]{2,1,0:T(8,128)(2,1)S(1)} %collective-permute-done.refs_1_), channel_id=1, source_target_pairs={{0,8},{8,16},{16,24},{24,32},{32,40},{40,48},{48,56},{56,0},{1,9},... | collective-permute-start | bytes 614408 | tf_op jit(solution)/shard_map/ppermute | solution.py:23
  43.9 14.1 %collective-permute-start.3 = (bf16[2,80,640]{2,1,0:T(8,128)(2,1)S(1)}, bf16[2,80,640]{2,1,0:T(8,128)(2,1)S(1)}, u32[]{:S(2)}, u32[]{:S(2)}) collective-permute-start(bf16[2,80,640]{2,1,0:T(8,128)(2,1)S(1)} %collective-permute-done.1.refs_2_), channel_id=1, source_target_pairs={{0,56},{8,0},{16,8},{24,16},{32,24},{40,32},{48,40},{56,48},{1,57}... | collective-permute-start | bytes 614408 | tf_op jit(solution)/shard_map/ppermute | solution.py:23
  53.0 9.8 %collective-permute-start.4 = (bf16[2,80,640]{2,1,0:T(8,128)(2,1)S(1)}, bf16[2,80,640]{2,1,0:T(8,128)(2,1)S(1)}, u32[]{:S(2)}, u32[]{:S(2)}) collective-permute-start(bf16[2,80,640]{2,1,0:T(8,128)(2,1)S(1)} %collective-permute-done.2.refs_3_), channel_id=1, source_target_pairs={{0,8},{8,16},{16,24},{24,32},{32,40},{40,48},{48,56},{56,0},{1,9},... | collective-permute-start | bytes 614408 | tf_op jit(solution)/shard_map/ppermute | solution.py:23
  58.1 11.0 %collective-permute-start.5 = (bf16[2,80,640]{2,1,0:T(8,128)(2,1)S(1)}, bf16[2,80,640]{2,1,0:T(8,128)(2,1)S(1)}, u32[]{:S(2)}, u32[]{:S(2)}) collective-permute-start(bf16[2,80,640]{2,1,0:T(8,128)(2,1)S(1)} %collective-permute-done.3.refs_4_), channel_id=1, source_target_pairs={{0,56},{8,0},{16,8},{24,16},{32,24},{40,32},{48,40},{56,48},{1,57}... | collective-permute-start | bytes 614408 | tf_op jit(solution)/shard_map/ppermute | solution.py:23
  62.9 9.9 %collective-permute-start.6 = (bf16[80,640]{1,0:T(8,128)(2,1)S(1)}, bf16[80,640]{1,0:T(8,128)(2,1)S(1)}, u32[]{:S(2)}, u32[]{:S(2)}) collective-permute-start(bf16[80,640]{1,0:T(8,128)(2,1)S(1)} %slice_bitcast_fusion.3), channel_id=1, source_target_pairs={{0,8},{8,16},{16,24},{24,32},{32,40},{40,48},{48,56},{56,0},{1,9},... | collective-permute-start | bytes 307208 | tf_op jit(solution)/shard_map/ppermute | solution.py:23
  69.1 6.3 %collective-permute-start.7 = (bf16[80,640]{1,0:T(8,128)(2,1)S(1)}, bf16[80,640]{1,0:T(8,128)(2,1)S(1)}, u32[]{:S(2)}, u32[]{:S(2)}) collective-permute-start(bf16[80,640]{1,0:T(8,128)(2,1)S(1)} %slice_bitcast_fusion.2), channel_id=1, source_target_pairs={{0,56},{8,0},{16,8},{24,16},{32,24},{40,32},{48,40},{56,48},{1,57}... | collective-permute-start | bytes 307208 | tf_op jit(solution)/shard_map/ppermute | solution.py:23
  75.4 26.1 %copy-start.7 = (f32[2]{0:T(128)S(1)}, f32[2]{0:T(128)}, u32[]{:S(2)}) copy-start(f32[2]{0:T(128)} %constant.78.clone) | copy-start | bytes 28
  75.4 26.1 %copy-start.8 = (f32[2]{0:T(128)S(1)}, f32[2]{0:T(128)}, u32[]{:S(2)}) copy-start(f32[2]{0:T(128)} %constant.79.clone) | copy-start | bytes 28
  80.7 15.9 %all-to-all-start.1 = ((bf16[8,80,768]{2,1,0:T(8,128)(2,1)}), bf16[8,80,768]{2,1,0:T(8,128)(2,1)S(1)}, u32[]{:S(2)}, u32[]{:S(2)}) async-start(bf16[8,80,768]{2,1,0:T(8,128)(2,1)} %stale.1), calls=%async_computation.1 | async-start | bytes 1966080 | tf_op jit(solution)/shard_map/all_to_all | solution.py:183
  84.5 33.4 %copy-start.4 = (bf16[2,80,640]{2,1,0:T(8,128)(2,1)S(1)}, bf16[2,80,640]{2,1,0:T(8,128)(2,1)}, u32[]{:S(2)}) copy-start(bf16[2,80,640]{2,1,0:T(8,128)(2,1)} %param.17) | copy-start | bytes 614404
  96.7 22.0 %copy-start.5 = (f32[50,640]{1,0:T(8,128)S(1)}, f32[50,640]{1,0:T(8,128)}, u32[]{:S(2)}) copy-start(f32[50,640]{1,0:T(8,128)} %param.16) | copy-start | bytes 384004
  98.3 5.4 %collective-permute-start.8 = (bf16[80,640]{1,0:T(8,128)(2,1)S(1)}, bf16[80,640]{1,0:T(8,128)(2,1)S(1)}, u32[]{:S(2)}, u32[]{:S(2)}) collective-permute-start(bf16[80,640]{1,0:T(8,128)(2,1)S(1)} %combine.1.own_ref), channel_id=1, source_target_pairs={{0,256},{256,0},{1,257},{257,1},{2,258},{258,2},{3,259},{259,3},{4... | collective-permute-start | bytes 307208 | tf_op jit(solution)/shard_map/ppermute | solution.py:23
  103.7 1.9 %copy-start = (bf16[640,2560]{1,0:T(8,128)(2,1)S(1)}, bf16[640,2560]{1,0:T(8,128)(2,1)}, u32[]{:S(2)}) copy-start(bf16[640,2560]{1,0:T(8,128)(2,1)} %weight_ref.1) | copy-start | bytes 9830404
  108.5 17.8 %all-to-all-start.2 = ((bf16[4,80,640]{2,1,0:T(8,128)(2,1)}), bf16[4,80,640]{2,1,0:T(8,128)(2,1)S(1)}, u32[]{:S(2)}, u32[]{:S(2)}) async-start(bf16[4,80,640]{2,1,0:T(8,128)(2,1)} %project.1), calls=%async_computation.2 | async-start | bytes 819200 | tf_op jit(solution)/shard_map/all_to_all | solution.py:215

commit v2 on v1

v2 whole, which is shorter than its diff:
```python
import functools
import math

import jax
import jax.numpy as jnp
from jax import lax
from jax.experimental import pallas as pl
from jax.experimental.pallas import tpu as pltpu
from jax.sharding import Mesh
from jax.sharding import PartitionSpec as P

HD = 128
LANES = 128
SPAN = 16
GUIDE = 5.0
MASKED = -1e30
EXPONENT = HD**-0.5 * math.log2(math.e)
VMEM = pl.BlockSpec(memory_space=pltpu.VMEM)
SMEM = pl.BlockSpec(memory_space=pltpu.SMEM)
MIB = 1024 * 1024


def shift(value, axis, step):
    size = lax.axis_size(axis)
    return lax.ppermute(value, axis, [(i, (i + step) % size) for i in range(size)])


def head_lanes(head):
    return slice(head * HD, (head + 1) * HD)


def scores_of(queries, keys, bias):
    scores = lax.dot_general(
        queries, keys, (((1,), (1,)), ((), ())), preferred_element_type=jnp.float32
    )
    if bias is not None:
        slabs = bias.shape[0]
        scores = (scores.reshape(slabs, -1, scores.shape[1]) + bias).reshape(scores.shape)
    return scores


def weighted(scores, maxima, values):
    weights = jnp.exp2((scores - maxima) * EXPONENT)
    totals = jnp.sum(weights, axis=1, keepdims=True)
    update = jnp.dot(weights.astype(jnp.bfloat16), values, preferred_element_type=jnp.float32)
    return update, totals


def place_stats(stats, lane, head, maxima, totals):
    stats = jnp.where(lane % SPAN == head, maxima, stats)
    return jnp.where(lane % SPAN == head + SPAN // 2, totals, stats)


def fresh_kernel(query_ref, fresh_ref, out_ref, stats_ref):
    rows, width = query_ref.shape
    lane = lax.broadcasted_iota(jnp.int32, (rows, LANES), 1)
    stats = jnp.zeros((rows, LANES), jnp.float32)
    for head in range(width // HD):
        at = head_lanes(head)
        scores = scores_of(query_ref[:, at], fresh_ref[0, :, at], None)
        maxima = jnp.max(scores, axis=1, keepdims=True)
        update, totals = weighted(scores, maxima, fresh_ref[1, :, at])
        out_ref[:, at] = update / totals
        stats = place_stats(stats, lane, head, maxima, totals)
    stats_ref[...] = stats


def own_bias(query_ref, key_ids):
    slabs, _, wide = query_ref.shape
    owned = query_ref[:, :, wide - LANES :].astype(jnp.float32)
    bias = []
    for slab in range(slabs):
        own_ids = owned[slab, :, 0:1] * float(LANES) + owned[slab, :, 1:2]
        kept = jnp.where(own_ids == key_ids, jnp.float32(MASKED), jnp.float32(0.0))
        bias.append(jnp.min(kept, axis=0, keepdims=True)[None])
    return jnp.concatenate(bias, axis=0)


def stale_kernel(keys_ref, query_ref, *refs):
    blocks, last_key, last_value, out_ref = refs[:-3], refs[-3], refs[-2], refs[-1]
    slabs, rows, wide = query_ref.shape
    bias = own_bias(query_ref, keys_ref[0:1, :])
    lane = lax.broadcasted_iota(jnp.int32, (slabs * rows, LANES), 1)
    stats = jnp.zeros((slabs * rows, LANES), jnp.float32)
    for head in range(wide // HD - 1):
        at = head_lanes(head)
        keys = jnp.concatenate([b[0, :, at] for b in blocks] + [last_key[:, at]], axis=0)
        values = jnp.concatenate([b[1, :, at] for b in blocks] + [last_value[:, at]], axis=0)
        scores = scores_of(query_ref[:, :, at].reshape(slabs * rows, HD), keys, bias)
        maxima = jnp.max(scores, axis=1, keepdims=True)
        update, totals = weighted(scores, maxima, values)
        part = (update / totals).astype(jnp.bfloat16)
        out_ref[:, :, at] = part.reshape(slabs, rows, HD)
        stats = place_stats(stats, lane, head, maxima, totals)
    high = stats.astype(jnp.bfloat16).astype(jnp.float32)
    mid = (stats - high).astype(jnp.bfloat16).astype(jnp.float32)
    low = stats - high - mid
    sent = jnp.where(lane < SPAN, high, jnp.where(lane < 2 * SPAN, mid, low))
    out_ref[:, :, wide - LANES :] = sent.astype(jnp.bfloat16).reshape(slabs, rows, LANES)


def combine_kernel(parts_ref, fresh_ref, fresh_stats_ref, out_ref):
    count, rows, wide = parts_ref.shape
    stats = []
    for part in range(count):
        sent = parts_ref[part, :, wide - LANES :].astype(jnp.float32)
        whole = sent + pltpu.roll(sent, LANES - SPAN, 1) + pltpu.roll(sent, LANES - 2 * SPAN, 1)
        stats.append(whole)
    stats.append(fresh_stats_ref[...])
    highest = functools.reduce(jnp.maximum, stats)
    shares = [
        jnp.exp2((s - highest) * EXPONENT) * pltpu.roll(s, LANES - SPAN // 2, 1) for s in stats
    ]
    total = functools.reduce(jnp.add, shares)
    shares = [share / total for share in shares]
    for head in range(wide // HD - 1):
        at = head_lanes(head)
        joined = fresh_ref[:, at] * shares[-1][:, head : head + 1]
        for part in range(count):
            share = shares[part][:, head : head + 1]
            joined = joined + parts_ref[part, :, at].astype(jnp.float32) * share
        out_ref[:, at] = joined.astype(jnp.bfloat16)


def project_kernel(factor_ref, own_ref, other_ref, weight_ref, out_ref):
    own = own_ref[...].astype(jnp.float32) * factor_ref[0]
    other = other_ref[...].astype(jnp.float32) * factor_ref[1]
    mixed = (own + other).astype(jnp.bfloat16)
    columns = out_ref.shape[2]
    for part in range(out_ref.shape[0]):
        weights = weight_ref[:, part * columns : (part + 1) * columns]
        product = jnp.dot(mixed, weights, preferred_element_type=jnp.float32)
        out_ref[part] = product.astype(jnp.bfloat16)


def local_call(kernel, out_shape, specs, mib):
    return pl.pallas_call(
        kernel,
        out_shape=out_shape,
        in_specs=specs,
        out_specs=jax.tree.map(lambda _: VMEM, out_shape),
        compiler_params=pltpu.CompilerParams(vmem_limit_bytes=mib * MIB),
    )


def shards(query, fresh_kv, stale_kv, assign, timestep, gate_table, residual, out_weight):
    rows, width = query.shape[1:]
    ring = lax.axis_size("zh")
    slabs = lax.axis_size("x") * lax.axis_size("zl")
    parts = lax.axis_size("t")

    places = jnp.stack([assign // LANES, assign % LANES], axis=1).astype(jnp.bfloat16)
    message = jnp.concatenate(
        [query[0], places, jnp.zeros((rows, LANES - 2), jnp.bfloat16)], axis=1
    )

    blocks, offsets = [stale_kv[0]], [0]
    ahead, behind = stale_kv[0], lax.optimization_barrier((stale_kv[0], message))[0]
    for step in range(1, ring // 2):
        ahead = shift(ahead, "zh", 1)
        behind = shift(behind, "zh", -1)
        blocks += [ahead, behind]
        offsets += [-step, step]
    last_key = shift(ahead[0], "zh", 1)
    last_value = shift(behind[1], "zh", -1)
    offsets.append(ring // 2)
    z_far = (lax.axis_index("zh") + jnp.array(offsets, jnp.int32)) % ring
    slab_ids = (lax.axis_index("x") * ring + z_far) * lax.axis_size("zl") + lax.axis_index("zl")
    key_ids = (slab_ids[:, None] * rows + jnp.arange(rows, dtype=jnp.int32)).astype(jnp.float32)
    key_ids = jnp.broadcast_to(key_ids.reshape(1, -1), (8, ring * rows))

    swapped = shift(message, "zl", 1)
    is_low = lax.axis_index("zl") == 0
    pair = jnp.stack(
        [jnp.where(is_low, message, swapped), jnp.where(is_low, swapped, message)]
    )
    queries = lax.all_to_all(
        jnp.broadcast_to(pair[None], (lax.axis_size("x"), *pair.shape)), "x", 0, 0
    ).reshape(slabs, *message.shape)

    sums = jax.ShapeDtypeStruct((rows, width), jnp.float32)
    stats = jax.ShapeDtypeStruct((rows, LANES), jnp.float32)
    fresh_out, fresh_stats = local_call(fresh_kernel, (sums, stats), [VMEM] * 2, 8)(
        query[0], fresh_kv[0]
    )
    parts_out = jax.ShapeDtypeStruct((slabs, rows, width + LANES), jnp.bfloat16)
    parts_out = local_call(stale_kernel, parts_out, [VMEM] * (len(blocks) + 4), 24)(
        key_ids, queries, *blocks, last_key, last_value
    )
    parts_out = lax.all_to_all(parts_out, ("x", "zl"), 0, 0)

    attended = jax.ShapeDtypeStruct((rows, width), jnp.bfloat16)
    attended = local_call(combine_kernel, attended, [VMEM] * 3, 12)(
        parts_out, fresh_out, fresh_stats
    )

    other = shift(attended, "g", 1)
    factors = jnp.where(
        lax.axis_index("g") == 0,
        jnp.array([GUIDE, 1.0 - GUIDE], jnp.float32),
        jnp.array([1.0 - GUIDE, GUIDE], jnp.float32),
    )
    columns = out_weight.shape[1] // parts
    projected = jax.ShapeDtypeStruct((parts, rows, columns), jnp.bfloat16)
    projected = local_call(project_kernel, projected, [SMEM] + [VMEM] * 3, 12)(
        factors, attended, other, out_weight
    )
    projected = lax.all_to_all(projected, "t", 0, 0)

    chosen = jnp.arange(gate_table.shape[0], dtype=jnp.int32) == timestep[0]
    gate_row = jnp.sum(jnp.where(chosen[:, None], gate_table, jnp.float32(0.0)), axis=0)
    summed = jnp.sum(projected.astype(jnp.float32), axis=0)
    residual_f = residual.astype(jnp.float32)
    base = residual_f[1] + GUIDE * (residual_f[0] - residual_f[1])
    return (base + gate_row[None, :] * summed).astype(jnp.bfloat16)


def solution(mesh):
    guide, patch, tensor = mesh.devices.shape
    x_size, z_low = 4, 2
    z_high = patch // (x_size * z_low)
    fine = Mesh(
        mesh.devices.reshape(guide, x_size, z_high, z_low, tensor), ("g", "x", "zh", "zl", "t")
    )
    slab = ("x", "zh", "zl")
    placed = (
        P("g", slab, "t"),
        P("g", None, slab, "t"),
        P("g", None, slab, "t"),
        P(slab),
        P(),
        P(None, ("g", "t")),
        P(None, slab, ("g", "t")),
        P("t", "g"),
    )
    return jax.shard_map(
        shards,
        mesh=fine,
        in_specs=placed,
        out_specs=P(slab, ("g", "t")),
        check_vma=False,
    )
```

time: 128 us -> 116 us (0.906)
  waiting for transfers between devices: 48.4 us -> 32.4 us
  starting transfers between devices: 61.2 us -> 66.7 us
  Pallas kernels: 10.4 us -> 8.23 us
    ppermute x9 -> x10, waiting for transfers between devices: 29.5 us -> 15.5 us  [shift(): lax.ppermute(value, axis, [(i, (i + step) % size) for i in range(size)])]
    ppermute x9 -> x10, starting transfers between devices: 41.7 us -> 45.1 us  [shift(): lax.ppermute(value, axis, [(i, (i + step) % size) for i in range(size)])]
    pallas_call x4, Pallas kernels: 10.4 us -> 8.23 us  [the longest x1 4.8 us: shards(): local_call(stale_kernel, parts_out, [VMEM] * (len(blocks) + 4), 24)]
    all_to_all x2, waiting for transfers between devices: 11.5 us -> 9.41 us  [the longest x1 9.4 us: shards(): parts_out = lax.all_to_all(parts_out, ('x', 'zl'), 0, 0)]
    all_to_all x1, starting transfers between devices: 9.5 us -> 11.5 us  [shards(): projected = lax.all_to_all(projected, 't', 0, 0)]
  transfers between devices with their start and end apart: 12 -> 13, of which waited for: 7 -> 7; matrix products, arithmetic and copies ran while one was open for 0% -> 2% of each run, Pallas kernels for 1% -> 1%
where the time goes in v2:
time: 116 us; the launch traced here: 115 us
  starting transfers between devices  66.7 us (58%)
  waiting for transfers between devices  32.4 us (28%)
  Pallas kernels  8.23 us (7%)
  other arithmetic  3.67 us (3%)
  local copies, waits for them, and re-layouts  3.41 us (3%)
    ppermute x10, starting transfers between devices, shift(): lax.ppermute(value, axis, [(i, (i + step) % size) for i in range(size)])  45.1 us
    ppermute x10, waiting for transfers between devices, shift(): lax.ppermute(value, axis, [(i, (i + step) % size) for i in range(size)])  15.5 us
    all_to_all x1, starting transfers between devices, shards(): projected = lax.all_to_all(projected, 't', 0, 0)  11.5 us
    all_to_all x1, waiting for transfers between devices, shards(): parts_out = lax.all_to_all(parts_out, ('x', 'zl'), 0, 0)  9.4 us
    all_to_all x1, waiting for transfers between devices, shards(): projected = lax.all_to_all(projected, 't', 0, 0)  7.45 us
    all_to_all x1, starting transfers between devices, shards(): parts_out = lax.all_to_all(parts_out, ('x', 'zl'), 0, 0)  6.07 us
    pallas_call x1, Pallas kernels, shards(): local_call(stale_kernel, parts_out, [VMEM] * (len(blocks) + 4), 24)  4.8 us
    all_to_all x1, starting transfers between devices, shards(): lax.all_to_all(jnp.broadcast_to(pair[None], (lax.axis_size('x'), *pair.sh...  4.01 us
  transfers between devices with their start and end apart: 13, of which 7 were waited for; matrix products, arithmetic and copies ran while one was open for 2% of the time, Pallas kernels for 1%

profile of v2, /device:TPU:1, one launch (start us, length us, event | category | flops | bytes accessed | tf_op | source)
XLA Modules:
  0.0 115.3 jit_solution(15718354166913149280)
XLA Ops:
  0.0 0.7 convert_bitcast_fusion
  0.7 0.1 copy.12
  0.8 0.1 copy.13
  1.0 1.0 maximum_maximum_fusion
  2.0 12.4 %collective-permute-start.2 = (bf16[2,80,640]{2,1,0:T(8,128)(2,1)}, bf16[2,80,640]{2,1,0:T(8,128)(2,1)S(1)}, u32[]{:S(2)}, u32[]{:S(2)}) collective-permute-start(bf16[2,80,640]{2,1,0:T(8,128)(2,1)} %bitcast.38), channel_id=1, source_target_pairs={{0,56},{8,0},{16,8},{24,16},{32,24},{40,32},{48,40},{56,48},{1,57}... | collective-permute-start | bytes 614408 | tf_op jit(solution)/shard_map/ppermute | solution.py:25
  14.4 2.6 %collective-permute-start = (bf16[80,768]{1,0:T(8,128)(2,1)S(1)}, bf16[80,768]{1,0:T(8,128)(2,1)S(1)}, u32[]{:S(2)}, u32[]{:S(2)}) collective-permute-start(bf16[80,768]{1,0:T(8,128)(2,1)S(1)} %maximum_maximum_fusion), channel_id=1, source_target_pairs={{0,4},{4,0},{1,5},{5,1},{2,6},{6,2},{3,7},{7,3},{8,12},{12,8},{9,1... | collective-permute-start | bytes 368648 | tf_op jit(solution)/shard_map/ppermute | solution.py:25
  17.1 1.9 %collective-permute-start.1 = (bf16[2,80,640]{2,1,0:T(8,128)(2,1)}, bf16[2,80,640]{2,1,0:T(8,128)(2,1)S(1)}, u32[]{:S(2)}, u32[]{:S(2)}) collective-permute-start(bf16[2,80,640]{2,1,0:T(8,128)(2,1)} %bitcast.39), channel_id=1, source_target_pairs={{0,8},{8,16},{16,24},{24,32},{32,40},{40,48},{48,56},{56,0},{1,9},... | collective-permute-start | bytes 614408 | tf_op jit(solution)/shard_map/ppermute | solution.py:25
  19.0 3.8 %collective-permute-done.2.refs_2_ = bf16[2,80,640]{2,1,0:T(8,128)(2,1)S(1)} collective-permute-done((bf16[2,80,640]{2,1,0:T(8,128)(2,1)}, bf16[2,80,640]{2,1,0:T(8,128)(2,1)S(1)}, u32[]{:S(2)}, u32[]{:S(2)}) %collective-permute-start.2) | collective-permute-done | bytes 204832 | tf_op jit(solution)/shard_map/ppermute | solution.py:25
  22.8 6.2 %collective-permute-start.4 = (bf16[2,80,640]{2,1,0:T(8,128)(2,1)S(1)}, bf16[2,80,640]{2,1,0:T(8,128)(2,1)S(1)}, u32[]{:S(2)}, u32[]{:S(2)}) collective-permute-start(bf16[2,80,640]{2,1,0:T(8,128)(2,1)S(1)} %collective-permute-done.2.refs_2_), channel_id=1, source_target_pairs={{0,56},{8,0},{16,8},{24,16},{32,24},{40,32},{48,40},{56,48},{1,57}... | collective-permute-start | bytes 614408 | tf_op jit(solution)/shard_map/ppermute | solution.py:25
  29.0 1.0 select_bitcast_fusion.1
  30.0 1.0 broadcast_in_dim.34
  31.1 4.0 %all-to-all-start = ((bf16[4,2,80,768]{3,2,1,0:T(8,128)(2,1)}), bf16[4,2,80,768]{3,2,1,0:T(8,128)(2,1)S(1)}, u32[]{:S(2)}, u32[]{:S(2)}) async-start(bf16[4,2,80,768]{3,2,1,0:T(8,128)(2,1)} %broadcast_in_dim.34), calls=%async_computation | async-start | bytes 1966080 | tf_op jit(solution)/shard_map/all_to_all | solution.py:177
  35.1 2.1 %collective-permute-start.3 = (bf16[2,80,640]{2,1,0:T(8,128)(2,1)S(1)}, bf16[2,80,640]{2,1,0:T(8,128)(2,1)S(1)}, u32[]{:S(2)}, u32[]{:S(2)}) collective-permute-start(bf16[2,80,640]{2,1,0:T(8,128)(2,1)S(1)} %collective-permute-done.1.refs_1_), channel_id=1, source_target_pairs={{0,8},{8,16},{16,24},{24,32},{32,40},{40,48},{48,56},{56,0},{1,9},... | collective-permute-start | bytes 614408 | tf_op jit(solution)/shard_map/ppermute | solution.py:25
  37.2 5.7 %collective-permute-start.6 = (bf16[2,80,640]{2,1,0:T(8,128)(2,1)S(1)}, bf16[2,80,640]{2,1,0:T(8,128)(2,1)S(1)}, u32[]{:S(2)}, u32[]{:S(2)}) collective-permute-start(bf16[2,80,640]{2,1,0:T(8,128)(2,1)S(1)} %collective-permute-done.4.refs_4_), channel_id=1, source_target_pairs={{0,56},{8,0},{16,8},{24,16},{32,24},{40,32},{48,40},{56,48},{1,57}... | collective-permute-start | bytes 614408 | tf_op jit(solution)/shard_map/ppermute | solution.py:25
  42.9 1.6 %collective-permute-done.3.refs_3_ = bf16[2,80,640]{2,1,0:T(8,128)(2,1)S(1)} collective-permute-done((bf16[2,80,640]{2,1,0:T(8,128)(2,1)S(1)}, bf16[2,80,640]{2,1,0:T(8,128)(2,1)S(1)}, u32[]{:S(2)}, u32[]{:S(2)}) %collective-permute-start.3) | collective-permute-done | bytes 204832 | tf_op jit(solution)/shard_map/ppermute | solution.py:25
  44.5 5.1 %collective-permute-start.5 = (bf16[2,80,640]{2,1,0:T(8,128)(2,1)S(1)}, bf16[2,80,640]{2,1,0:T(8,128)(2,1)S(1)}, u32[]{:S(2)}, u32[]{:S(2)}) collective-permute-start(bf16[2,80,640]{2,1,0:T(8,128)(2,1)S(1)} %collective-permute-done.3.refs_3_), channel_id=1, source_target_pairs={{0,8},{8,16},{16,24},{24,32},{32,40},{40,48},{48,56},{56,0},{1,9},... | collective-permute-start | bytes 614408 | tf_op jit(solution)/shard_map/ppermute | solution.py:25
  49.7 2.4 %collective-permute-start.8 = (bf16[80,640]{1,0:T(8,128)(2,1)S(1)}, bf16[80,640]{1,0:T(8,128)(2,1)S(1)}, u32[]{:S(2)}, u32[]{:S(2)}) collective-permute-start(bf16[80,640]{1,0:T(8,128)(2,1)S(1)} %slice_bitcast_fusion.2), channel_id=1, source_target_pairs={{0,56},{8,0},{16,8},{24,16},{32,24},{40,32},{48,40},{56,48},{1,57}... | collective-permute-start | bytes 307208 | tf_op jit(solution)/shard_map/ppermute | solution.py:25
  52.1 2.9 %collective-permute-done.5.refs_5_ = bf16[2,80,640]{2,1,0:T(8,128)(2,1)S(1)} collective-permute-done((bf16[2,80,640]{2,1,0:T(8,128)(2,1)S(1)}, bf16[2,80,640]{2,1,0:T(8,128)(2,1)S(1)}, u32[]{:S(2)}, u32[]{:S(2)}) %collective-permute-start.5) | collective-permute-done | bytes 204832 | tf_op jit(solution)/shard_map/ppermute | solution.py:25
  55.0 2.9 %collective-permute-start.7 = (bf16[80,640]{1,0:T(8,128)(2,1)S(1)}, bf16[80,640]{1,0:T(8,128)(2,1)S(1)}, u32[]{:S(2)}, u32[]{:S(2)}) collective-permute-start(bf16[80,640]{1,0:T(8,128)(2,1)S(1)} %slice_bitcast_fusion.3), channel_id=1, source_target_pairs={{0,8},{8,16},{16,24},{24,32},{32,40},{40,48},{48,56},{56,0},{1,9},... | collective-permute-start | bytes 307208 | tf_op jit(solution)/shard_map/ppermute | solution.py:25
  58.1 5.3 %collective-permute-done.7.refs_7_ = bf16[80,640]{1,0:T(8,128)(2,1)S(1)} collective-permute-done((bf16[80,640]{1,0:T(8,128)(2,1)S(1)}, bf16[80,640]{1,0:T(8,128)(2,1)S(1)}, u32[]{:S(2)}, u32[]{:S(2)}) %collective-permute-start.7) | collective-permute-done | bytes 102432 | tf_op jit(solution)/shard_map/ppermute | solution.py:25
  63.4 4.8 %shard_map.109 = bf16[8,80,768]{2,1,0:T(8,128)(2,1)} custom-call(f32[8,640]{1,0:T(8,128)S(1)} %broadcast_in_dim.32.keys_ref, bf16[8,80,768]{2,1,0:T(8,128)(2,1)S(1)} %bitcast.34, bf16[2,80,640]{2,1,0:T(8,128)(2,1)S(1)} %bitcast.40, bf16[2,80,640]{2,1,0:T(8,128)(2,1)S(1)} %collective-permute-done.1.refs_1_, ...), custom_call_target="tpu_custom_call" | custom-call | tf_op jit(solution)/shard_map/pallas_call | solution.py:187
  68.2 6.1 %all-to-all-start.1 = ((bf16[8,80,768]{2,1,0:T(8,128)(2,1)}), bf16[8,80,768]{2,1,0:T(8,128)(2,1)S(1)}, u32[]{:S(2)}, u32[]{:S(2)}) async-start(bf16[8,80,768]{2,1,0:T(8,128)(2,1)} %shard_map.109), calls=%async_computation.1 | async-start | bytes 1966080 | tf_op jit(solution)/shard_map/all_to_all | solution.py:190
  74.3 0.6 shard_map.110
  75.0 9.4 %all-to-all-done.1.parts_ref = bf16[8,80,768]{2,1,0:T(8,128)(2,1)S(1)} async-done(((bf16[8,80,768]{2,1,0:T(8,128)(2,1)}), bf16[8,80,768]{2,1,0:T(8,128)(2,1)S(1)}, u32[]{:S(2)}, u32[]{:S(2)}) %all-to-all-start.1) | async-done | bytes 983072 | tf_op jit(solution)/shard_map/all_to_all | solution.py:190
  84.4 0.8 shard_map.111.own_ref
  85.2 3.6 %collective-permute-start.9 = (bf16[80,640]{1,0:T(8,128)(2,1)S(1)}, bf16[80,640]{1,0:T(8,128)(2,1)S(1)}, u32[]{:S(2)}, u32[]{:S(2)}) collective-permute-start(bf16[80,640]{1,0:T(8,128)(2,1)S(1)} %shard_map.111.own_ref), channel_id=1, source_target_pairs={{0,256},{256,0},{1,257},{257,1},{2,258},{258,2},{3,259},{259,3},{4... | collective-permute-start | bytes 307208 | tf_op jit(solution)/shard_map/ppermute | solution.py:25
  88.8 2.0 %collective-permute-done.9.other_ref = bf16[80,640]{1,0:T(8,128)(2,1)S(1)} collective-permute-done((bf16[80,640]{1,0:T(8,128)(2,1)S(1)}, bf16[80,640]{1,0:T(8,128)(2,1)S(1)}, u32[]{:S(2)}, u32[]{:S(2)}) %collective-permute-start.9) | collective-permute-done | bytes 102432 | tf_op jit(solution)/shard_map/ppermute | solution.py:25
  90.8 1.9 %copy-done = bf16[640,2560]{1,0:T(8,128)(2,1)S(1)} copy-done((bf16[640,2560]{1,0:T(8,128)(2,1)S(1)}, bf16[640,2560]{1,0:T(8,128)(2,1)}, u32[]{:S(2)}) %copy-start) | copy-done | bytes 3276824
  92.8 2.0 %shard_map.112 = bf16[4,80,640]{2,1,0:T(8,128)(2,1)} custom-call(f32[2]{0:T(128)S(1)} %broadcast_select_fusion.factor_ref, bf16[80,640]{1,0:T(8,128)(2,1)S(1)} %shard_map.111.own_ref, bf16[80,640]{1,0:T(8,128)(2,1)S(1)} %collective-permute-done.9.other_ref, bf16[640,2560]{1,0:T(8,128)(2,1)S(1)} %copy-done), custom_call_target="tpu_custom_call" | custom-call | tf_op jit(solution)/shard_map/pallas_call | solution.py:205
  94.7 11.5 %all-to-all-start.2 = ((bf16[4,80,640]{2,1,0:T(8,128)(2,1)}), bf16[4,80,640]{2,1,0:T(8,128)(2,1)S(1)}, u32[]{:S(2)}, u32[]{:S(2)}) async-start(bf16[4,80,640]{2,1,0:T(8,128)(2,1)} %shard_map.112), calls=%async_computation.2 | async-start | bytes 819200 | tf_op jit(solution)/shard_map/all_to_all | solution.py:208
  107.1 7.5 %all-to-all-done.2 = bf16[4,80,640]{2,1,0:T(8,128)(2,1)S(1)} async-done(((bf16[4,80,640]{2,1,0:T(8,128)(2,1)}), bf16[4,80,640]{2,1,0:T(8,128)(2,1)S(1)}, u32[]{:S(2)}, u32[]{:S(2)}) %all-to-all-start.2) | async-done | bytes 409632 | tf_op jit(solution)/shard_map/all_to_all | solution.py:208
  114.6 0.7 fusion.4
  (37 shorter events, 0.5 us)
Async XLA Ops:
  0.0 42.9 %copy-start.6 = (s32[8]{0:T(128)S(1)}, s32[8]{0:T(128)}, u32[]{:S(2)}) copy-start(s32[8]{0:T(128)} %constant.77.clone) | copy-start | bytes 100
  0.0 63.4 %copy-start.2 = (bf16[1,2,80,640]{3,2,1,0:T(8,128)(2,1)S(1)}, bf16[1,2,80,640]{3,2,1,0:T(8,128)(2,1)}, u32[]{:S(2)}) copy-start(bf16[1,2,80,640]{3,2,1,0:T(8,128)(2,1)} %param.13) | copy-start | bytes 614404
  2.0 20.7 %collective-permute-start.2 = (bf16[2,80,640]{2,1,0:T(8,128)(2,1)}, bf16[2,80,640]{2,1,0:T(8,128)(2,1)S(1)}, u32[]{:S(2)}, u32[]{:S(2)}) collective-permute-start(bf16[2,80,640]{2,1,0:T(8,128)(2,1)} %bitcast.38), channel_id=1, source_target_pairs={{0,56},{8,0},{16,8},{24,16},{32,24},{40,32},{48,40},{56,48},{1,57}... | collective-permute-start | bytes 614408 | tf_op jit(solution)/shard_map/ppermute | solution.py:25
  14.4 14.6 %collective-permute-start = (bf16[80,768]{1,0:T(8,128)(2,1)S(1)}, bf16[80,768]{1,0:T(8,128)(2,1)S(1)}, u32[]{:S(2)}, u32[]{:S(2)}) collective-permute-start(bf16[80,768]{1,0:T(8,128)(2,1)S(1)} %maximum_maximum_fusion), channel_id=1, source_target_pairs={{0,4},{4,0},{1,5},{5,1},{2,6},{6,2},{3,7},{7,3},{8,12},{12,8},{9,1... | collective-permute-start | bytes 368648 | tf_op jit(solution)/shard_map/ppermute | solution.py:25
  17.1 18.0 %collective-permute-start.1 = (bf16[2,80,640]{2,1,0:T(8,128)(2,1)}, bf16[2,80,640]{2,1,0:T(8,128)(2,1)S(1)}, u32[]{:S(2)}, u32[]{:S(2)}) collective-permute-start(bf16[2,80,640]{2,1,0:T(8,128)(2,1)} %bitcast.39), channel_id=1, source_target_pairs={{0,8},{8,16},{16,24},{24,32},{32,40},{40,48},{48,56},{56,0},{1,9},... | collective-permute-start | bytes 614408 | tf_op jit(solution)/shard_map/ppermute | solution.py:25
  22.8 14.4 %collective-permute-start.4 = (bf16[2,80,640]{2,1,0:T(8,128)(2,1)S(1)}, bf16[2,80,640]{2,1,0:T(8,128)(2,1)S(1)}, u32[]{:S(2)}, u32[]{:S(2)}) collective-permute-start(bf16[2,80,640]{2,1,0:T(8,128)(2,1)S(1)} %collective-permute-done.2.refs_2_), channel_id=1, source_target_pairs={{0,56},{8,0},{16,8},{24,16},{32,24},{40,32},{48,40},{56,48},{1,57}... | collective-permute-start | bytes 614408 | tf_op jit(solution)/shard_map/ppermute | solution.py:25
  31.1 32.3 %all-to-all-start = ((bf16[4,2,80,768]{3,2,1,0:T(8,128)(2,1)}), bf16[4,2,80,768]{3,2,1,0:T(8,128)(2,1)S(1)}, u32[]{:S(2)}, u32[]{:S(2)}) async-start(bf16[4,2,80,768]{3,2,1,0:T(8,128)(2,1)} %broadcast_in_dim.34), calls=%async_computation | async-start | bytes 1966080 | tf_op jit(solution)/shard_map/all_to_all | solution.py:177
  35.1 39.2 %copy-start.1 = (bf16[1,80,640]{2,1,0:T(8,128)(2,1)S(1)}, bf16[1,80,640]{2,1,0:T(8,128)(2,1)}, u32[]{:S(2)}) copy-start(bf16[1,80,640]{2,1,0:T(8,128)(2,1)} %param.11) | copy-start | bytes 307204
  35.1 39.2 %copy-start.3 = (bf16[1,2,80,640]{3,2,1,0:T(8,128)(2,1)S(1)}, bf16[1,2,80,640]{3,2,1,0:T(8,128)(2,1)}, u32[]{:S(2)}) copy-start(bf16[1,2,80,640]{3,2,1,0:T(8,128)(2,1)} %param.12) | copy-start | bytes 614404
  35.1 9.4 %collective-permute-start.3 = (bf16[2,80,640]{2,1,0:T(8,128)(2,1)S(1)}, bf16[2,80,640]{2,1,0:T(8,128)(2,1)S(1)}, u32[]{:S(2)}, u32[]{:S(2)}) collective-permute-start(bf16[2,80,640]{2,1,0:T(8,128)(2,1)S(1)} %collective-permute-done.1.refs_1_), channel_id=1, source_target_pairs={{0,8},{8,16},{16,24},{24,32},{32,40},{40,48},{48,56},{56,0},{1,9},... | collective-permute-start | bytes 614408 | tf_op jit(solution)/shard_map/ppermute | solution.py:25
  37.2 12.5 %collective-permute-start.6 = (bf16[2,80,640]{2,1,0:T(8,128)(2,1)S(1)}, bf16[2,80,640]{2,1,0:T(8,128)(2,1)S(1)}, u32[]{:S(2)}, u32[]{:S(2)}) collective-permute-start(bf16[2,80,640]{2,1,0:T(8,128)(2,1)S(1)} %collective-permute-done.4.refs_4_), channel_id=1, source_target_pairs={{0,56},{8,0},{16,8},{24,16},{32,24},{40,32},{48,40},{56,48},{1,57}... | collective-permute-start | bytes 614408 | tf_op jit(solution)/shard_map/ppermute | solution.py:25
  44.5 10.5 %collective-permute-start.5 = (bf16[2,80,640]{2,1,0:T(8,128)(2,1)S(1)}, bf16[2,80,640]{2,1,0:T(8,128)(2,1)S(1)}, u32[]{:S(2)}, u32[]{:S(2)}) collective-permute-start(bf16[2,80,640]{2,1,0:T(8,128)(2,1)S(1)} %collective-permute-done.3.refs_3_), channel_id=1, source_target_pairs={{0,8},{8,16},{16,24},{24,32},{32,40},{40,48},{48,56},{56,0},{1,9},... | collective-permute-start | bytes 614408 | tf_op jit(solution)/shard_map/ppermute | solution.py:25
  49.7 8.4 %collective-permute-start.8 = (bf16[80,640]{1,0:T(8,128)(2,1)S(1)}, bf16[80,640]{1,0:T(8,128)(2,1)S(1)}, u32[]{:S(2)}, u32[]{:S(2)}) collective-permute-start(bf16[80,640]{1,0:T(8,128)(2,1)S(1)} %slice_bitcast_fusion.2), channel_id=1, source_target_pairs={{0,56},{8,0},{16,8},{24,16},{32,24},{40,32},{48,40},{56,48},{1,57}... | collective-permute-start | bytes 307208 | tf_op jit(solution)/shard_map/ppermute | solution.py:25
  55.0 8.4 %collective-permute-start.7 = (bf16[80,640]{1,0:T(8,128)(2,1)S(1)}, bf16[80,640]{1,0:T(8,128)(2,1)S(1)}, u32[]{:S(2)}, u32[]{:S(2)}) collective-permute-start(bf16[80,640]{1,0:T(8,128)(2,1)S(1)} %slice_bitcast_fusion.3), channel_id=1, source_target_pairs={{0,8},{8,16},{16,24},{24,32},{32,40},{40,48},{48,56},{56,0},{1,9},... | collective-permute-start | bytes 307208 | tf_op jit(solution)/shard_map/ppermute | solution.py:25
  63.4 25.4 %copy-start.7 = (f32[2]{0:T(128)S(1)}, f32[2]{0:T(128)}, u32[]{:S(2)}) copy-start(f32[2]{0:T(128)} %constant.78.clone) | copy-start | bytes 28
  63.4 25.4 %copy-start.8 = (f32[2]{0:T(128)S(1)}, f32[2]{0:T(128)}, u32[]{:S(2)}) copy-start(f32[2]{0:T(128)} %constant.79.clone) | copy-start | bytes 28
  68.2 16.2 %all-to-all-start.1 = ((bf16[8,80,768]{2,1,0:T(8,128)(2,1)}), bf16[8,80,768]{2,1,0:T(8,128)(2,1)S(1)}, u32[]{:S(2)}, u32[]{:S(2)}) async-start(bf16[8,80,768]{2,1,0:T(8,128)(2,1)} %shard_map.109), calls=%async_computation.1 | async-start | bytes 1966080 | tf_op jit(solution)/shard_map/all_to_all | solution.py:190
  74.3 32.0 %copy-start.4 = (bf16[2,80,640]{2,1,0:T(8,128)(2,1)S(1)}, bf16[2,80,640]{2,1,0:T(8,128)(2,1)}, u32[]{:S(2)}) copy-start(bf16[2,80,640]{2,1,0:T(8,128)(2,1)} %param.17) | copy-start | bytes 614404
  84.4 22.6 %copy-start.5 = (f32[50,640]{1,0:T(8,128)S(1)}, f32[50,640]{1,0:T(8,128)}, u32[]{:S(2)}) copy-start(f32[50,640]{1,0:T(8,128)} %param.16) | copy-start | bytes 384004
  85.2 5.6 %collective-permute-start.9 = (bf16[80,640]{1,0:T(8,128)(2,1)S(1)}, bf16[80,640]{1,0:T(8,128)(2,1)S(1)}, u32[]{:S(2)}, u32[]{:S(2)}) collective-permute-start(bf16[80,640]{1,0:T(8,128)(2,1)S(1)} %shard_map.111.own_ref), channel_id=1, source_target_pairs={{0,256},{256,0},{1,257},{257,1},{2,258},{258,2},{3,259},{259,3},{4... | collective-permute-start | bytes 307208 | tf_op jit(solution)/shard_map/ppermute | solution.py:25
  90.8 1.9 %copy-start = (bf16[640,2560]{1,0:T(8,128)(2,1)S(1)}, bf16[640,2560]{1,0:T(8,128)(2,1)}, u32[]{:S(2)}) copy-start(bf16[640,2560]{1,0:T(8,128)(2,1)} %weight_ref.1) | copy-start | bytes 9830404
  94.7 19.8 %all-to-all-start.2 = ((bf16[4,80,640]{2,1,0:T(8,128)(2,1)}), bf16[4,80,640]{2,1,0:T(8,128)(2,1)S(1)}, u32[]{:S(2)}, u32[]{:S(2)}) async-start(bf16[4,80,640]{2,1,0:T(8,128)(2,1)} %shard_map.112), calls=%async_computation.2 | async-start | bytes 819200 | tf_op jit(solution)/shard_map/all_to_all | solution.py:208

commit v3 on v2

--- a/solution.py
+++ b/solution.py
@@ -25,6 +25,18 @@
     return lax.ppermute(value, axis, [(i, (i + step) % size) for i in range(size)])
 
 
+def trade(value, step):
+    size, parts = lax.axis_size("zh"), lax.axis_size("t")
+    pairs = []
+    for place in range(size):
+        for part in range(parts):
+            even = place ^ 1
+            odd = (((place - 1) ^ 1) + 1) % size
+            partner = even if (step + part) % 2 == 0 else odd
+            pairs.append((place * parts + part, partner * parts + part))
+    return lax.ppermute(value, ("zh", "t"), pairs)
+
+
 def head_lanes(head):
     return slice(head * HD, (head + 1) * HD)
 
@@ -40,10 +52,10 @@
 
 
 def weighted(scores, maxima, values):
-    weights = jnp.exp2((scores - maxima) * EXPONENT)
-    totals = jnp.sum(weights, axis=1, keepdims=True)
-    update = jnp.dot(weights.astype(jnp.bfloat16), values, preferred_element_type=jnp.float32)
-    return update, totals
+    weights = jnp.exp2((scores - maxima) * EXPONENT).astype(jnp.bfloat16)
+    beside = jnp.concatenate([values, jnp.ones_like(values)], axis=1)
+    both = jnp.dot(weights, beside, preferred_element_type=jnp.float32)
+    return both[:, :HD], both[:, HD:]
 
 
 def place_stats(stats, lane, head, maxima, totals):
@@ -65,6 +77,11 @@
     stats_ref[...] = stats
 
 
+def join_kernel(own_ref, other_ref, out_ref):
+    out_ref[0] = own_ref[...]
+    out_ref[1] = other_ref[...]
+
+
 def own_bias(query_ref, key_ids):
     slabs, _, wide = query_ref.shape
     owned = query_ref[:, :, wide - LANES :].astype(jnp.float32)
@@ -77,15 +94,17 @@
 
 
 def stale_kernel(keys_ref, query_ref, *refs):
-    blocks, last_key, last_value, out_ref = refs[:-3], refs[-3], refs[-2], refs[-1]
+    blocks, out_ref = [], refs[-1]
+    for ref in refs[:-1]:
+        blocks += [ref] if len(ref.shape) == 3 else [ref.at[0], ref.at[1]]
     slabs, rows, wide = query_ref.shape
     bias = own_bias(query_ref, keys_ref[0:1, :])
     lane = lax.broadcasted_iota(jnp.int32, (slabs * rows, LANES), 1)
     stats = jnp.zeros((slabs * rows, LANES), jnp.float32)
     for head in range(wide // HD - 1):
         at = head_lanes(head)
-        keys = jnp.concatenate([b[0, :, at] for b in blocks] + [last_key[:, at]], axis=0)
-        values = jnp.concatenate([b[1, :, at] for b in blocks] + [last_value[:, at]], axis=0)
+        keys = jnp.concatenate([b[0, :, at] for b in blocks], axis=0)
+        values = jnp.concatenate([b[1, :, at] for b in blocks], axis=0)
         scores = scores_of(query_ref[:, :, at].reshape(slabs * rows, HD), keys, bias)
         maxima = jnp.max(scores, axis=1, keepdims=True)
         update, totals = weighted(scores, maxima, values)
@@ -133,13 +152,14 @@
         out_ref[part] = product.astype(jnp.bfloat16)
 
 
-def local_call(kernel, out_shape, specs, mib):
+def local_call(kernel, out_shape, specs, mib, flops=0, exps=0):
     return pl.pallas_call(
         kernel,
         out_shape=out_shape,
         in_specs=specs,
         out_specs=jax.tree.map(lambda _: VMEM, out_shape),
         compiler_params=pltpu.CompilerParams(vmem_limit_bytes=mib * MIB),
+        cost_estimate=pl.CostEstimate(flops=flops, bytes_accessed=MIB, transcendentals=exps),
     )
 
 
@@ -154,17 +174,19 @@
         [query[0], places, jnp.zeros((rows, LANES - 2), jnp.bfloat16)], axis=1
     )
 
-    blocks, offsets = [stale_kv[0]], [0]
-    ahead, behind = stale_kv[0], lax.optimization_barrier((stale_kv[0], message))[0]
-    for step in range(1, ring // 2):
-        ahead = shift(ahead, "zh", 1)
-        behind = shift(behind, "zh", -1)
-        blocks += [ahead, behind]
-        offsets += [-step, step]
-    last_key = shift(ahead[0], "zh", 1)
-    last_value = shift(behind[1], "zh", -1)
-    offsets.append(ring // 2)
-    z_far = (lax.axis_index("zh") + jnp.array(offsets, jnp.int32)) % ring
+    own = stale_kv[0]
+    first, second = trade(own, 0), trade(own, 1)
+    behind = trade(first, 1)
+    two = jax.ShapeDtypeStruct((2, *own.shape), own.dtype)
+    two = local_call(join_kernel, two, [VMEM] * 2, 4)(second, behind)
+    singles, pairs, offsets = [own, first, second, behind], [], [0, 1, -1, -2]
+    for step in range(2, ring // 2):
+        two = trade(two, step)
+        pairs.append(two)
+        reach = [2 * (step // 2), 2 * (step // 2) + 1]
+        offsets += reach if step % 2 == 0 else [-1 - k for k in reach]
+    side = 1 - 2 * ((lax.axis_index("zh") + lax.axis_index("t")) % 2)
+    z_far = (lax.axis_index("zh") + side * jnp.array(offsets, jnp.int32)) % ring
     slab_ids = (lax.axis_index("x") * ring + z_far) * lax.axis_size("zl") + lax.axis_index("zl")
     key_ids = (slab_ids[:, None] * rows + jnp.arange(rows, dtype=jnp.int32)).astype(jnp.float32)
     key_ids = jnp.broadcast_to(key_ids.reshape(1, -1), (8, ring * rows))
@@ -180,17 +202,18 @@
 
     sums = jax.ShapeDtypeStruct((rows, width), jnp.float32)
     stats = jax.ShapeDtypeStruct((rows, LANES), jnp.float32)
-    fresh_out, fresh_stats = local_call(fresh_kernel, (sums, stats), [VMEM] * 2, 8)(
+    fresh_out, fresh_stats = local_call(fresh_kernel, (sums, stats), [VMEM] * 2, 4)(
         query[0], fresh_kv[0]
     )
     parts_out = jax.ShapeDtypeStruct((slabs, rows, width + LANES), jnp.bfloat16)
-    parts_out = local_call(stale_kernel, parts_out, [VMEM] * (len(blocks) + 4), 24)(
-        key_ids, queries, *blocks, last_key, last_value
+    specs = [VMEM] * (len(singles) + len(pairs) + 2)
+    parts_out = local_call(stale_kernel, parts_out, specs, 14, 2**32, 2**22)(
+        key_ids, queries, *singles, *pairs
     )
     parts_out = lax.all_to_all(parts_out, ("x", "zl"), 0, 0)
 
     attended = jax.ShapeDtypeStruct((rows, width), jnp.bfloat16)
-    attended = local_call(combine_kernel, attended, [VMEM] * 3, 12)(
+    attended = local_call(combine_kernel, attended, [VMEM] * 3, 4)(
         parts_out, fresh_out, fresh_stats
     )
 
@@ -202,7 +225,7 @@
     )
     columns = out_weight.shape[1] // parts
     projected = jax.ShapeDtypeStruct((parts, rows, columns), jnp.bfloat16)
-    projected = local_call(project_kernel, projected, [SMEM] + [VMEM] * 3, 12)(
+    projected = local_call(project_kernel, projected, [SMEM] + [VMEM] * 3, 6)(
         factors, attended, other, out_weight
     )
     projected = lax.all_to_all(projected, "t", 0, 0)

time: 116 us -> 109 us (0.940)
  starting transfers between devices: 66.7 us -> 56.2 us
  waiting for transfers between devices: 32.4 us -> 35.3 us
    ppermute x10 -> x2, starting transfers between devices: 45.1 us -> 6.51 us  [shift(): lax.ppermute(value, axis, [(i, (i + step) % size) for i in range(size)])]
    ppermute x0 -> x5, starting transfers between devices: none -> 27.4 us  [trade(): return lax.ppermute(value, ('zh', 't'), pairs)]
    ppermute x10 -> x2, waiting for transfers between devices: 15.5 us -> 2.44 us  [shift(): lax.ppermute(value, axis, [(i, (i + step) % size) for i in range(size)])]
    ppermute x0 -> x5, waiting for transfers between devices: none -> 12.6 us  [trade(): return lax.ppermute(value, ('zh', 't'), pairs)]
    all_to_all x1, waiting for transfers between devices: 0.01 us -> 3.5 us  [shards(): lax.all_to_all(jnp.broadcast_to(pair[None], (lax.axis_size('x'), *pair.sh...]
    all_to_all x1, starting transfers between devices: 11.5 us -> 14.2 us  [shards(): projected = lax.all_to_all(projected, 't', 0, 0)]
    all_to_all x1, starting transfers between devices: 6.07 us -> 4.03 us  [shards(): parts_out = lax.all_to_all(parts_out, ('x', 'zl'), 0, 0)]
    pallas_call x4 -> x5, Pallas kernels: 8.23 us -> 8.27 us  [the longest x1 4.78 us: shards(): local_call(stale_kernel, parts_out, specs, 14, 2 ** 32, 2 ** 22)]
  transfers between devices with their start and end apart: 13 -> 10, of which waited for: 7 -> 8; matrix products, arithmetic and copies ran while one was open for 2% -> 4% of each run, Pallas kernels for 1% -> 1%
where the time goes in v3:
time: 109 us; the launch traced here: 108 us
  starting transfers between devices  56.2 us (52%)
  waiting for transfers between devices  35.3 us (32%)
  Pallas kernels  8.27 us (8%)
  other arithmetic  3.63 us (3%)
  local copies, waits for them, and re-layouts  3.38 us (3%)
    ppermute x5, starting transfers between devices, trade(): return lax.ppermute(value, ('zh', 't'), pairs)  27.4 us
    all_to_all x1, starting transfers between devices, shards(): projected = lax.all_to_all(projected, 't', 0, 0)  14.2 us
    ppermute x5, waiting for transfers between devices, trade(): return lax.ppermute(value, ('zh', 't'), pairs)  12.6 us
    all_to_all x1, waiting for transfers between devices, shards(): parts_out = lax.all_to_all(parts_out, ('x', 'zl'), 0, 0)  9.35 us
    all_to_all x1, waiting for transfers between devices, shards(): projected = lax.all_to_all(projected, 't', 0, 0)  7.45 us
    ppermute x2, starting transfers between devices, shift(): lax.ppermute(value, axis, [(i, (i + step) % size) for i in range(size)])  6.51 us
    pallas_call x1, Pallas kernels, shards(): local_call(stale_kernel, parts_out, specs, 14, 2 ** 32, 2 ** 22)  4.78 us
    all_to_all x1, starting transfers between devices, shards(): parts_out = lax.all_to_all(parts_out, ('x', 'zl'), 0, 0)  4.03 us
  transfers between devices with their start and end apart: 10, of which 8 were waited for; matrix products, arithmetic and copies ran while one was open for 4% of the time, Pallas kernels for 1%

profile of v3, /device:TPU:1, one launch (start us, length us, event | category | flops | bytes accessed | tf_op | source)
XLA Modules:
  0.0 107.6 jit_solution(7281608542844031453)
XLA Ops:
  0.0 12.5 %collective-permute-start.1 = (bf16[2,80,640]{2,1,0:T(8,128)(2,1)}, bf16[2,80,640]{2,1,0:T(8,128)(2,1)S(1)}, u32[]{:S(2)}, u32[]{:S(2)}) collective-permute-start(bf16[2,80,640]{2,1,0:T(8,128)(2,1)} %bitcast.35), channel_id=1, source_target_pairs={{0,8},{1,57},{2,10},{3,59},{8,0},{9,17},{10,2},{11,19},{16,24},{17... | collective-permute-start | bytes 614408 | tf_op jit(solution)/shard_map/ppermute | solution.py:37
  12.5 1.9 %collective-permute-start.2 = (bf16[2,80,640]{2,1,0:T(8,128)(2,1)}, bf16[2,80,640]{2,1,0:T(8,128)(2,1)S(1)}, u32[]{:S(2)}, u32[]{:S(2)}) collective-permute-start(bf16[2,80,640]{2,1,0:T(8,128)(2,1)} %bitcast.36), channel_id=1, source_target_pairs={{0,56},{1,9},{2,58},{3,11},{8,16},{9,1},{10,18},{11,3},{16,8},{17,... | collective-permute-start | bytes 614408 | tf_op jit(solution)/shard_map/ppermute | solution.py:37
  14.5 0.7 convert_bitcast_fusion
  15.1 0.1 copy.12
  15.2 0.1 copy.13
  15.4 0.1 pad.5.clone
  15.4 2.3 %collective-permute-done.1.refs_1_ = bf16[2,80,640]{2,1,0:T(8,128)(2,1)S(1)} collective-permute-done((bf16[2,80,640]{2,1,0:T(8,128)(2,1)}, bf16[2,80,640]{2,1,0:T(8,128)(2,1)S(1)}, u32[]{:S(2)}, u32[]{:S(2)}) %collective-permute-start.1) | collective-permute-done | bytes 204832 | tf_op jit(solution)/shard_map/ppermute | solution.py:37
  17.8 1.9 %collective-permute-start.3 = (bf16[2,80,640]{2,1,0:T(8,128)(2,1)S(1)}, bf16[2,80,640]{2,1,0:T(8,128)(2,1)S(1)}, u32[]{:S(2)}, u32[]{:S(2)}) collective-permute-start(bf16[2,80,640]{2,1,0:T(8,128)(2,1)S(1)} %collective-permute-done.1.refs_1_), channel_id=1, source_target_pairs={{0,56},{1,9},{2,58},{3,11},{8,16},{9,1},{10,18},{11,3},{16,8},{17,... | collective-permute-start | bytes 614408 | tf_op jit(solution)/shard_map/ppermute | solution.py:37
  19.7 1.0 maximum_maximum_fusion
  20.7 3.3 %collective-permute-start = (bf16[80,768]{1,0:T(8,128)(2,1)S(1)}, bf16[80,768]{1,0:T(8,128)(2,1)S(1)}, u32[]{:S(2)}, u32[]{:S(2)}) collective-permute-start(bf16[80,768]{1,0:T(8,128)(2,1)S(1)} %maximum_maximum_fusion), channel_id=1, source_target_pairs={{0,4},{4,0},{1,5},{5,1},{2,6},{6,2},{3,7},{7,3},{8,12},{12,8},{9,1... | collective-permute-start | bytes 368648 | tf_op jit(solution)/shard_map/ppermute | solution.py:25
  24.0 1.3 %collective-permute-done.3.other_ref.refs_3_ = bf16[2,80,640]{2,1,0:T(8,128)(2,1)S(1)} collective-permute-done((bf16[2,80,640]{2,1,0:T(8,128)(2,1)S(1)}, bf16[2,80,640]{2,1,0:T(8,128)(2,1)S(1)}, u32[]{:S(2)}, u32[]{:S(2)}) %collective-permute-start.3) | collective-permute-done | bytes 204832 | tf_op jit(solution)/shard_map/ppermute | solution.py:37
  25.4 5.8 %collective-permute-start.4 = (bf16[2,2,80,640]{3,2,1,0:T(8,128)(2,1)S(1)}, bf16[2,2,80,640]{3,2,1,0:T(8,128)(2,1)S(1)}, u32[]{:S(2)}, u32[]{:S(2)}) collective-permute-start(bf16[2,2,80,640]{3,2,1,0:T(8,128)(2,1)S(1)} %shard_map.109), channel_id=1, source_target_pairs={{0,8},{1,57},{2,10},{3,59},{8,0},{9,17},{10,2},{11,19},{16,24},{17... | collective-permute-start | bytes 1228808 | tf_op jit(solution)/shard_map/ppermute | solution.py:37
  31.2 1.0 select_bitcast_fusion.1
  32.2 1.0 broadcast_in_dim.34
  33.2 4.0 %all-to-all-start = ((bf16[4,2,80,768]{3,2,1,0:T(8,128)(2,1)}), bf16[4,2,80,768]{3,2,1,0:T(8,128)(2,1)S(1)}, u32[]{:S(2)}, u32[]{:S(2)}) async-start(bf16[4,2,80,768]{3,2,1,0:T(8,128)(2,1)} %broadcast_in_dim.34), calls=%async_computation | async-start | bytes 1966080 | tf_op jit(solution)/shard_map/all_to_all | solution.py:199
  37.2 2.2 %collective-permute-done.4.refs_4_ = bf16[2,2,80,640]{3,2,1,0:T(8,128)(2,1)S(1)} collective-permute-done((bf16[2,2,80,640]{3,2,1,0:T(8,128)(2,1)S(1)}, bf16[2,2,80,640]{3,2,1,0:T(8,128)(2,1)S(1)}, u32[]{:S(2)}, u32[]{:S(2)}) %collective-permute-start.4) | collective-permute-done | bytes 409632 | tf_op jit(solution)/shard_map/ppermute | solution.py:37
  39.5 5.2 %collective-permute-start.5 = (bf16[2,2,80,640]{3,2,1,0:T(8,128)(2,1)S(1)}, bf16[2,2,80,640]{3,2,1,0:T(8,128)(2,1)S(1)}, u32[]{:S(2)}, u32[]{:S(2)}) collective-permute-start(bf16[2,2,80,640]{3,2,1,0:T(8,128)(2,1)S(1)} %collective-permute-done.4.refs_4_), channel_id=1, source_target_pairs={{0,56},{1,9},{2,58},{3,11},{8,16},{9,1},{10,18},{11,3},{16,8},{17,... | collective-permute-start | bytes 1228808 | tf_op jit(solution)/shard_map/ppermute | solution.py:37
  44.9 3.5 %all-to-all-done = bf16[4,2,80,768]{3,2,1,0:T(8,128)(2,1)S(1)} async-done(((bf16[4,2,80,768]{3,2,1,0:T(8,128)(2,1)}), bf16[4,2,80,768]{3,2,1,0:T(8,128)(2,1)S(1)}, u32[]{:S(2)}, u32[]{:S(2)}) %all-to-all-start) | async-done | bytes 983072 | tf_op jit(solution)/shard_map/all_to_all | solution.py:199
  48.4 6.7 %collective-permute-done.5.refs_5_ = bf16[2,2,80,640]{3,2,1,0:T(8,128)(2,1)S(1)} collective-permute-done((bf16[2,2,80,640]{3,2,1,0:T(8,128)(2,1)S(1)}, bf16[2,2,80,640]{3,2,1,0:T(8,128)(2,1)S(1)}, u32[]{:S(2)}, u32[]{:S(2)}) %collective-permute-start.5) | collective-permute-done | bytes 409632 | tf_op jit(solution)/shard_map/ppermute | solution.py:37
  55.1 4.8 %shard_map.110 = bf16[8,80,768]{2,1,0:T(8,128)(2,1)} custom-call(f32[8,640]{1,0:T(8,128)S(1)} %broadcast_in_dim.32.keys_ref, bf16[8,80,768]{2,1,0:T(8,128)(2,1)S(1)} %bitcast.30, bf16[2,80,640]{2,1,0:T(8,128)(2,1)S(1)} %bitcast.37, bf16[2,80,640]{2,1,0:T(8,128)(2,1)S(1)} %collective-permute-done.1.refs_1_, ...), custom_call_target="tpu_custom_call" | custom-call | flops 4294967296 | bytes 1048576 | tf_op jit(solution)/shard_map/pallas_call | solution.py:210
  59.9 4.0 %all-to-all-start.1 = ((bf16[8,80,768]{2,1,0:T(8,128)(2,1)}), bf16[8,80,768]{2,1,0:T(8,128)(2,1)S(1)}, u32[]{:S(2)}, u32[]{:S(2)}) async-start(bf16[8,80,768]{2,1,0:T(8,128)(2,1)} %shard_map.110), calls=%async_computation.1 | async-start | bytes 1966080 | tf_op jit(solution)/shard_map/all_to_all | solution.py:213
  63.9 0.6 shard_map.111
  64.6 9.4 %all-to-all-done.1.parts_ref = bf16[8,80,768]{2,1,0:T(8,128)(2,1)S(1)} async-done(((bf16[8,80,768]{2,1,0:T(8,128)(2,1)}), bf16[8,80,768]{2,1,0:T(8,128)(2,1)S(1)}, u32[]{:S(2)}, u32[]{:S(2)}) %all-to-all-start.1) | async-done | bytes 983072 | tf_op jit(solution)/shard_map/all_to_all | solution.py:213
  74.0 0.8 shard_map.112.own_ref
  74.8 3.2 %collective-permute-start.6 = (bf16[80,640]{1,0:T(8,128)(2,1)S(1)}, bf16[80,640]{1,0:T(8,128)(2,1)S(1)}, u32[]{:S(2)}, u32[]{:S(2)}) collective-permute-start(bf16[80,640]{1,0:T(8,128)(2,1)S(1)} %shard_map.112.own_ref), channel_id=1, source_target_pairs={{0,256},{256,0},{1,257},{257,1},{2,258},{258,2},{3,259},{259,3},{4... | collective-permute-start | bytes 307208 | tf_op jit(solution)/shard_map/ppermute | solution.py:25
  78.0 2.4 %collective-permute-done.6.other_ref = bf16[80,640]{1,0:T(8,128)(2,1)S(1)} collective-permute-done((bf16[80,640]{1,0:T(8,128)(2,1)S(1)}, bf16[80,640]{1,0:T(8,128)(2,1)S(1)}, u32[]{:S(2)}, u32[]{:S(2)}) %collective-permute-start.6) | collective-permute-done | bytes 102432 | tf_op jit(solution)/shard_map/ppermute | solution.py:25
  80.5 1.9 %copy-done = bf16[640,2560]{1,0:T(8,128)(2,1)S(1)} copy-done((bf16[640,2560]{1,0:T(8,128)(2,1)S(1)}, bf16[640,2560]{1,0:T(8,128)(2,1)}, u32[]{:S(2)}) %copy-start) | copy-done | bytes 3276824
  82.4 2.0 %shard_map.113 = bf16[4,80,640]{2,1,0:T(8,128)(2,1)} custom-call(f32[2]{0:T(128)S(1)} %broadcast_select_fusion.factor_ref, bf16[80,640]{1,0:T(8,128)(2,1)S(1)} %shard_map.112.own_ref, bf16[80,640]{1,0:T(8,128)(2,1)S(1)} %collective-permute-done.6.other_ref, bf16[640,2560]{1,0:T(8,128)(2,1)S(1)} %copy-done), custom_call_target="tpu_custom_call" | custom-call | bytes 1048576 | tf_op jit(solution)/shard_map/pallas_call | solution.py:228
  84.4 14.2 %all-to-all-start.2 = ((bf16[4,80,640]{2,1,0:T(8,128)(2,1)}), bf16[4,80,640]{2,1,0:T(8,128)(2,1)S(1)}, u32[]{:S(2)}, u32[]{:S(2)}) async-start(bf16[4,80,640]{2,1,0:T(8,128)(2,1)} %shard_map.113), calls=%async_computation.2 | async-start | bytes 819200 | tf_op jit(solution)/shard_map/all_to_all | solution.py:231
  99.3 0.1 select_reduce_fusion
  99.4 7.5 %all-to-all-done.2 = bf16[4,80,640]{2,1,0:T(8,128)(2,1)S(1)} async-done(((bf16[4,80,640]{2,1,0:T(8,128)(2,1)}), bf16[4,80,640]{2,1,0:T(8,128)(2,1)S(1)}, u32[]{:S(2)}, u32[]{:S(2)}) %all-to-all-start.2) | async-done | bytes 409632 | tf_op jit(solution)/shard_map/all_to_all | solution.py:231
  106.9 0.7 fusion.4
  (30 shorter events, 0.4 us)
Async XLA Ops:
  0.0 44.7 %copy-start.8 = (s32[8]{0:T(128)S(1)}, s32[8]{0:T(128)}, u32[]{:S(2)}) copy-start(s32[8]{0:T(128)} %constant.90.clone) | copy-start | bytes 100
  0.0 55.1 %copy-start.3 = (bf16[1,2,80,640]{3,2,1,0:T(8,128)(2,1)S(1)}, bf16[1,2,80,640]{3,2,1,0:T(8,128)(2,1)}, u32[]{:S(2)}) copy-start(bf16[1,2,80,640]{3,2,1,0:T(8,128)(2,1)} %param.13) | copy-start | bytes 614404
  0.0 17.7 %collective-permute-start.1 = (bf16[2,80,640]{2,1,0:T(8,128)(2,1)}, bf16[2,80,640]{2,1,0:T(8,128)(2,1)S(1)}, u32[]{:S(2)}, u32[]{:S(2)}) collective-permute-start(bf16[2,80,640]{2,1,0:T(8,128)(2,1)} %bitcast.35), channel_id=1, source_target_pairs={{0,8},{1,57},{2,10},{3,59},{8,0},{9,17},{10,2},{11,19},{16,24},{17... | collective-permute-start | bytes 614408 | tf_op jit(solution)/shard_map/ppermute | solution.py:37
  12.5 11.5 %collective-permute-start.2 = (bf16[2,80,640]{2,1,0:T(8,128)(2,1)}, bf16[2,80,640]{2,1,0:T(8,128)(2,1)S(1)}, u32[]{:S(2)}, u32[]{:S(2)}) collective-permute-start(bf16[2,80,640]{2,1,0:T(8,128)(2,1)} %bitcast.36), channel_id=1, source_target_pairs={{0,56},{1,9},{2,58},{3,11},{8,16},{9,1},{10,18},{11,3},{16,8},{17,... | collective-permute-start | bytes 614408 | tf_op jit(solution)/shard_map/ppermute | solution.py:37
  17.8 7.6 %collective-permute-start.3 = (bf16[2,80,640]{2,1,0:T(8,128)(2,1)S(1)}, bf16[2,80,640]{2,1,0:T(8,128)(2,1)S(1)}, u32[]{:S(2)}, u32[]{:S(2)}) collective-permute-start(bf16[2,80,640]{2,1,0:T(8,128)(2,1)S(1)} %collective-permute-done.1.refs_1_), channel_id=1, source_target_pairs={{0,56},{1,9},{2,58},{3,11},{8,16},{9,1},{10,18},{11,3},{16,8},{17,... | collective-permute-start | bytes 614408 | tf_op jit(solution)/shard_map/ppermute | solution.py:37
  20.7 10.5 %collective-permute-start = (bf16[80,768]{1,0:T(8,128)(2,1)S(1)}, bf16[80,768]{1,0:T(8,128)(2,1)S(1)}, u32[]{:S(2)}, u32[]{:S(2)}) collective-permute-start(bf16[80,768]{1,0:T(8,128)(2,1)S(1)} %maximum_maximum_fusion), channel_id=1, source_target_pairs={{0,4},{4,0},{1,5},{5,1},{2,6},{6,2},{3,7},{7,3},{8,12},{12,8},{9,1... | collective-permute-start | bytes 368648 | tf_op jit(solution)/shard_map/ppermute | solution.py:25
  25.4 14.1 %collective-permute-start.4 = (bf16[2,2,80,640]{3,2,1,0:T(8,128)(2,1)S(1)}, bf16[2,2,80,640]{3,2,1,0:T(8,128)(2,1)S(1)}, u32[]{:S(2)}, u32[]{:S(2)}) collective-permute-start(bf16[2,2,80,640]{3,2,1,0:T(8,128)(2,1)S(1)} %shard_map.109), channel_id=1, source_target_pairs={{0,8},{1,57},{2,10},{3,59},{8,0},{9,17},{10,2},{11,19},{16,24},{17... | collective-permute-start | bytes 1228808 | tf_op jit(solution)/shard_map/ppermute | solution.py:37
  33.2 15.2 %all-to-all-start = ((bf16[4,2,80,768]{3,2,1,0:T(8,128)(2,1)}), bf16[4,2,80,768]{3,2,1,0:T(8,128)(2,1)S(1)}, u32[]{:S(2)}, u32[]{:S(2)}) async-start(bf16[4,2,80,768]{3,2,1,0:T(8,128)(2,1)} %broadcast_in_dim.34), calls=%async_computation | async-start | bytes 1966080 | tf_op jit(solution)/shard_map/all_to_all | solution.py:199
  39.5 15.6 %collective-permute-start.5 = (bf16[2,2,80,640]{3,2,1,0:T(8,128)(2,1)S(1)}, bf16[2,2,80,640]{3,2,1,0:T(8,128)(2,1)S(1)}, u32[]{:S(2)}, u32[]{:S(2)}) collective-permute-start(bf16[2,2,80,640]{3,2,1,0:T(8,128)(2,1)S(1)} %collective-permute-done.4.refs_4_), channel_id=1, source_target_pairs={{0,56},{1,9},{2,58},{3,11},{8,16},{9,1},{10,18},{11,3},{16,8},{17,... | collective-permute-start | bytes 1228808 | tf_op jit(solution)/shard_map/ppermute | solution.py:37
  55.1 8.8 %copy-start.1 = (bf16[1,80,640]{2,1,0:T(8,128)(2,1)S(1)}, bf16[1,80,640]{2,1,0:T(8,128)(2,1)}, u32[]{:S(2)}) copy-start(bf16[1,80,640]{2,1,0:T(8,128)(2,1)} %param.11) | copy-start | bytes 307204
  55.1 8.8 %copy-start.2 = (bf16[1,2,80,640]{3,2,1,0:T(8,128)(2,1)S(1)}, bf16[1,2,80,640]{3,2,1,0:T(8,128)(2,1)}, u32[]{:S(2)}) copy-start(bf16[1,2,80,640]{3,2,1,0:T(8,128)(2,1)} %param.12) | copy-start | bytes 614404
  59.9 18.1 %copy-start.6 = (f32[2]{0:T(128)S(1)}, f32[2]{0:T(128)}, u32[]{:S(2)}) copy-start(f32[2]{0:T(128)} %constant.91.clone) | copy-start | bytes 28
  59.9 18.1 %copy-start.7 = (f32[2]{0:T(128)S(1)}, f32[2]{0:T(128)}, u32[]{:S(2)}) copy-start(f32[2]{0:T(128)} %constant.92.clone) | copy-start | bytes 28
  59.9 14.1 %all-to-all-start.1 = ((bf16[8,80,768]{2,1,0:T(8,128)(2,1)}), bf16[8,80,768]{2,1,0:T(8,128)(2,1)S(1)}, u32[]{:S(2)}, u32[]{:S(2)}) async-start(bf16[8,80,768]{2,1,0:T(8,128)(2,1)} %shard_map.110), calls=%async_computation.1 | async-start | bytes 1966080 | tf_op jit(solution)/shard_map/all_to_all | solution.py:213
  63.9 34.7 %copy-start.4 = (bf16[2,80,640]{2,1,0:T(8,128)(2,1)S(1)}, bf16[2,80,640]{2,1,0:T(8,128)(2,1)}, u32[]{:S(2)}) copy-start(bf16[2,80,640]{2,1,0:T(8,128)(2,1)} %param.17) | copy-start | bytes 614404
  74.0 25.4 %copy-start.5 = (f32[50,640]{1,0:T(8,128)S(1)}, f32[50,640]{1,0:T(8,128)}, u32[]{:S(2)}) copy-start(f32[50,640]{1,0:T(8,128)} %param.16) | copy-start | bytes 384004
  74.8 5.7 %collective-permute-start.6 = (bf16[80,640]{1,0:T(8,128)(2,1)S(1)}, bf16[80,640]{1,0:T(8,128)(2,1)S(1)}, u32[]{:S(2)}, u32[]{:S(2)}) collective-permute-start(bf16[80,640]{1,0:T(8,128)(2,1)S(1)} %shard_map.112.own_ref), channel_id=1, source_target_pairs={{0,256},{256,0},{1,257},{257,1},{2,258},{258,2},{3,259},{259,3},{4... | collective-permute-start | bytes 307208 | tf_op jit(solution)/shard_map/ppermute | solution.py:25
  80.5 1.9 %copy-start = (bf16[640,2560]{1,0:T(8,128)(2,1)S(1)}, bf16[640,2560]{1,0:T(8,128)(2,1)}, u32[]{:S(2)}) copy-start(bf16[640,2560]{1,0:T(8,128)(2,1)} %weight_ref.1) | copy-start | bytes 9830404
  84.4 22.5 %all-to-all-start.2 = ((bf16[4,80,640]{2,1,0:T(8,128)(2,1)}), bf16[4,80,640]{2,1,0:T(8,128)(2,1)S(1)}, u32[]{:S(2)}, u32[]{:S(2)}) async-start(bf16[4,80,640]{2,1,0:T(8,128)(2,1)} %shard_map.113), calls=%async_computation.2 | async-start | bytes 819200 | tf_op jit(solution)/shard_map/all_to_all | solution.py:231

commit v4 on v3

--- a/solution.py
+++ b/solution.py
@@ -41,21 +41,29 @@
     return slice(head * HD, (head + 1) * HD)
 
 
-def scores_of(queries, keys, bias):
-    scores = lax.dot_general(
-        queries, keys, (((1,), (1,)), ((), ())), preferred_element_type=jnp.float32
-    )
-    if bias is not None:
-        slabs = bias.shape[0]
-        scores = (scores.reshape(slabs, -1, scores.shape[1]) + bias).reshape(scores.shape)
-    return scores
-
-
-def weighted(scores, maxima, values):
-    weights = jnp.exp2((scores - maxima) * EXPONENT).astype(jnp.bfloat16)
+def softmax_sums(queries, keys, values, bias):
+    total = keys.shape[0]
+    cut = total * 3 // 5 // LANES * LANES
+    pieces = [(0, cut), (cut, total)] if cut else [(0, total)]
+    scores = []
+    for low, high in pieces:
+        score = lax.dot_general(
+            queries, keys[low:high], (((1,), (1,)), ((), ())), preferred_element_type=jnp.float32
+        )
+        if bias is not None:
+            slabs = bias.shape[0]
+            score = score.reshape(slabs, -1, high - low) + bias[:, :, low:high]
+            score = score.reshape(-1, high - low)
+        scores.append(score)
+    maxima = [jnp.max(score, axis=1, keepdims=True) for score in scores]
+    maxima = functools.reduce(jnp.maximum, maxima)
     beside = jnp.concatenate([values, jnp.ones_like(values)], axis=1)
-    both = jnp.dot(weights, beside, preferred_element_type=jnp.float32)
-    return both[:, :HD], both[:, HD:]
+    sums = None
+    for (low, high), score in zip(pieces, scores, strict=True):
+        weights = jnp.exp2((score - maxima) * EXPONENT).astype(jnp.bfloat16)
+        part = jnp.dot(weights, beside[low:high], preferred_element_type=jnp.float32)
+        sums = part if sums is None else sums + part
+    return sums[:, :HD], sums[:, HD:], maxima
 
 
 def place_stats(stats, lane, head, maxima, totals):
@@ -69,9 +77,9 @@
     stats = jnp.zeros((rows, LANES), jnp.float32)
     for head in range(width // HD):
         at = head_lanes(head)
-        scores = scores_of(query_ref[:, at], fresh_ref[0, :, at], None)
-        maxima = jnp.max(scores, axis=1, keepdims=True)
-        update, totals = weighted(scores, maxima, fresh_ref[1, :, at])
+        update, totals, maxima = softmax_sums(
+            query_ref[:, at], fresh_ref[0, :, at], fresh_ref[1, :, at], None
+        )
         out_ref[:, at] = update / totals
         stats = place_stats(stats, lane, head, maxima, totals)
     stats_ref[...] = stats
@@ -105,9 +113,8 @@
         at = head_lanes(head)
         keys = jnp.concatenate([b[0, :, at] for b in blocks], axis=0)
         values = jnp.concatenate([b[1, :, at] for b in blocks], axis=0)
-        scores = scores_of(query_ref[:, :, at].reshape(slabs * rows, HD), keys, bias)
-        maxima = jnp.max(scores, axis=1, keepdims=True)
-        update, totals = weighted(scores, maxima, values)
+        queries = query_ref[:, :, at].reshape(slabs * rows, HD)
+        update, totals, maxima = softmax_sums(queries, keys, values, bias)
         part = (update / totals).astype(jnp.bfloat16)
         out_ref[:, :, at] = part.reshape(slabs, rows, HD)
         stats = place_stats(stats, lane, head, maxima, totals)
@@ -202,18 +209,18 @@
 
     sums = jax.ShapeDtypeStruct((rows, width), jnp.float32)
     stats = jax.ShapeDtypeStruct((rows, LANES), jnp.float32)
-    fresh_out, fresh_stats = local_call(fresh_kernel, (sums, stats), [VMEM] * 2, 4)(
+    fresh_out, fresh_stats = local_call(fresh_kernel, (sums, stats), [VMEM] * 2, 4, 2**33, 2**20)(
         query[0], fresh_kv[0]
     )
     parts_out = jax.ShapeDtypeStruct((slabs, rows, width + LANES), jnp.bfloat16)
     specs = [VMEM] * (len(singles) + len(pairs) + 2)
-    parts_out = local_call(stale_kernel, parts_out, specs, 14, 2**32, 2**22)(
+    parts_out = local_call(stale_kernel, parts_out, specs, 14, 2**33, 2**22)(
         key_ids, queries, *singles, *pairs
     )
     parts_out = lax.all_to_all(parts_out, ("x", "zl"), 0, 0)
 
     attended = jax.ShapeDtypeStruct((rows, width), jnp.bfloat16)
-    attended = local_call(combine_kernel, attended, [VMEM] * 3, 4)(
+    attended = local_call(combine_kernel, attended, [VMEM] * 3, 4, 2**33, 2**20)(
         parts_out, fresh_out, fresh_stats
     )
 

time: 109 us -> 106 us (0.972)
  local copies, waits for them, and re-layouts: 3.38 us -> 1.46 us
    unnamed x18, local copies, waits for them, and re-layouts: 1.96 us -> 0.04 us
where the time goes in v4:
time: 106 us; the launch traced here: 105 us
  starting transfers between devices  56.3 us (53%)
  waiting for transfers between devices  35.2 us (33%)
  Pallas kernels  7.6 us (7%)
  other arithmetic  3.63 us (3%)
  local copies, waits for them, and re-layouts  1.46 us (1%)
    ppermute x5, starting transfers between devices, trade(): return lax.ppermute(value, ('zh', 't'), pairs)  27.4 us
    all_to_all x1, starting transfers between devices, shards(): projected = lax.all_to_all(projected, 't', 0, 0)  14.4 us
    ppermute x5, waiting for transfers between devices, trade(): return lax.ppermute(value, ('zh', 't'), pairs)  12.6 us
    all_to_all x1, waiting for transfers between devices, shards(): parts_out = lax.all_to_all(parts_out, ('x', 'zl'), 0, 0)  9.37 us
    all_to_all x1, waiting for transfers between devices, shards(): projected = lax.all_to_all(projected, 't', 0, 0)  7.45 us
    ppermute x2, starting transfers between devices, shift(): lax.ppermute(value, axis, [(i, (i + step) % size) for i in range(size)])  6.63 us
    pallas_call x1, Pallas kernels, shards(): local_call(stale_kernel, parts_out, specs, 14, 2 ** 33, 2 ** 22)  4.09 us
    all_to_all x1, starting transfers between devices, shards(): lax.all_to_all(jnp.broadcast_to(pair[None], (lax.axis_size('x'), *pair.sh...  4.01 us
  transfers between devices with their start and end apart: 10, of which 8 were waited for; matrix products, arithmetic and copies ran while one was open for 4% of the time, Pallas kernels for 1%

profile of v4, /device:TPU:1, one launch (start us, length us, event | category | flops | bytes accessed | tf_op | source)
XLA Modules:
  0.0 105.0 jit_solution(14567624329349724184)
XLA Ops:
  0.0 12.5 %collective-permute-start.1 = (bf16[2,80,640]{2,1,0:T(8,128)(2,1)}, bf16[2,80,640]{2,1,0:T(8,128)(2,1)S(1)}, u32[]{:S(2)}, u32[]{:S(2)}) collective-permute-start(bf16[2,80,640]{2,1,0:T(8,128)(2,1)} %bitcast.34), channel_id=1, source_target_pairs={{0,8},{1,57},{2,10},{3,59},{8,0},{9,17},{10,2},{11,19},{16,24},{17... | collective-permute-start | bytes 614408 | tf_op jit(solution)/shard_map/ppermute | solution.py:37
  12.5 1.9 %collective-permute-start.2 = (bf16[2,80,640]{2,1,0:T(8,128)(2,1)}, bf16[2,80,640]{2,1,0:T(8,128)(2,1)S(1)}, u32[]{:S(2)}, u32[]{:S(2)}) collective-permute-start(bf16[2,80,640]{2,1,0:T(8,128)(2,1)} %bitcast.35), channel_id=1, source_target_pairs={{0,56},{1,9},{2,58},{3,11},{8,16},{9,1},{10,18},{11,3},{16,8},{17,... | collective-permute-start | bytes 614408 | tf_op jit(solution)/shard_map/ppermute | solution.py:37
  14.5 0.7 convert_bitcast_fusion
  15.1 0.1 copy.12
  15.2 0.1 copy.13
  15.4 0.1 pad.5.clone
  15.4 2.3 %collective-permute-done.1.refs_1_ = bf16[2,80,640]{2,1,0:T(8,128)(2,1)S(1)} collective-permute-done((bf16[2,80,640]{2,1,0:T(8,128)(2,1)}, bf16[2,80,640]{2,1,0:T(8,128)(2,1)S(1)}, u32[]{:S(2)}, u32[]{:S(2)}) %collective-permute-start.1) | collective-permute-done | bytes 204832 | tf_op jit(solution)/shard_map/ppermute | solution.py:37
  17.8 1.9 %collective-permute-start.3 = (bf16[2,80,640]{2,1,0:T(8,128)(2,1)S(1)}, bf16[2,80,640]{2,1,0:T(8,128)(2,1)S(1)}, u32[]{:S(2)}, u32[]{:S(2)}) collective-permute-start(bf16[2,80,640]{2,1,0:T(8,128)(2,1)S(1)} %collective-permute-done.1.refs_1_), channel_id=1, source_target_pairs={{0,56},{1,9},{2,58},{3,11},{8,16},{9,1},{10,18},{11,3},{16,8},{17,... | collective-permute-start | bytes 614408 | tf_op jit(solution)/shard_map/ppermute | solution.py:37
  19.7 1.0 maximum_maximum_fusion
  20.7 3.3 %collective-permute-start = (bf16[80,768]{1,0:T(8,128)(2,1)S(1)}, bf16[80,768]{1,0:T(8,128)(2,1)S(1)}, u32[]{:S(2)}, u32[]{:S(2)}) collective-permute-start(bf16[80,768]{1,0:T(8,128)(2,1)S(1)} %maximum_maximum_fusion), channel_id=1, source_target_pairs={{0,4},{4,0},{1,5},{5,1},{2,6},{6,2},{3,7},{7,3},{8,12},{12,8},{9,1... | collective-permute-start | bytes 368648 | tf_op jit(solution)/shard_map/ppermute | solution.py:25
  24.0 1.3 %collective-permute-done.3.other_ref.refs_3_ = bf16[2,80,640]{2,1,0:T(8,128)(2,1)S(1)} collective-permute-done((bf16[2,80,640]{2,1,0:T(8,128)(2,1)S(1)}, bf16[2,80,640]{2,1,0:T(8,128)(2,1)S(1)}, u32[]{:S(2)}, u32[]{:S(2)}) %collective-permute-start.3) | collective-permute-done | bytes 204832 | tf_op jit(solution)/shard_map/ppermute | solution.py:37
  25.4 5.8 %collective-permute-start.4 = (bf16[2,2,80,640]{3,2,1,0:T(8,128)(2,1)S(1)}, bf16[2,2,80,640]{3,2,1,0:T(8,128)(2,1)S(1)}, u32[]{:S(2)}, u32[]{:S(2)}) collective-permute-start(bf16[2,2,80,640]{3,2,1,0:T(8,128)(2,1)S(1)} %shard_map.109), channel_id=1, source_target_pairs={{0,8},{1,57},{2,10},{3,59},{8,0},{9,17},{10,2},{11,19},{16,24},{17... | collective-permute-start | bytes 1228808 | tf_op jit(solution)/shard_map/ppermute | solution.py:37
  31.2 1.0 select_bitcast_fusion.1
  32.2 1.0 broadcast_in_dim.34
  33.2 4.0 %all-to-all-start = ((bf16[4,2,80,768]{3,2,1,0:T(8,128)(2,1)}), bf16[4,2,80,768]{3,2,1,0:T(8,128)(2,1)S(1)}, u32[]{:S(2)}, u32[]{:S(2)}) async-start(bf16[4,2,80,768]{3,2,1,0:T(8,128)(2,1)} %broadcast_in_dim.34), calls=%async_computation | async-start | bytes 1966080 | tf_op jit(solution)/shard_map/all_to_all | solution.py:206
  37.2 2.2 %collective-permute-done.4.refs_4_ = bf16[2,2,80,640]{3,2,1,0:T(8,128)(2,1)S(1)} collective-permute-done((bf16[2,2,80,640]{3,2,1,0:T(8,128)(2,1)S(1)}, bf16[2,2,80,640]{3,2,1,0:T(8,128)(2,1)S(1)}, u32[]{:S(2)}, u32[]{:S(2)}) %collective-permute-start.4) | collective-permute-done | bytes 409632 | tf_op jit(solution)/shard_map/ppermute | solution.py:37
  39.5 5.2 %collective-permute-start.5 = (bf16[2,2,80,640]{3,2,1,0:T(8,128)(2,1)S(1)}, bf16[2,2,80,640]{3,2,1,0:T(8,128)(2,1)S(1)}, u32[]{:S(2)}, u32[]{:S(2)}) collective-permute-start(bf16[2,2,80,640]{3,2,1,0:T(8,128)(2,1)S(1)} %collective-permute-done.4.refs_4_), channel_id=1, source_target_pairs={{0,56},{1,9},{2,58},{3,11},{8,16},{9,1},{10,18},{11,3},{16,8},{17,... | collective-permute-start | bytes 1228808 | tf_op jit(solution)/shard_map/ppermute | solution.py:37
  44.8 0.1 convert_element_type.22
  44.9 3.5 %all-to-all-done = bf16[4,2,80,768]{3,2,1,0:T(8,128)(2,1)S(1)} async-done(((bf16[4,2,80,768]{3,2,1,0:T(8,128)(2,1)}), bf16[4,2,80,768]{3,2,1,0:T(8,128)(2,1)S(1)}, u32[]{:S(2)}, u32[]{:S(2)}) %all-to-all-start) | async-done | bytes 983072 | tf_op jit(solution)/shard_map/all_to_all | solution.py:206
  48.4 6.7 %collective-permute-done.5.refs_5_ = bf16[2,2,80,640]{3,2,1,0:T(8,128)(2,1)S(1)} collective-permute-done((bf16[2,2,80,640]{3,2,1,0:T(8,128)(2,1)S(1)}, bf16[2,2,80,640]{3,2,1,0:T(8,128)(2,1)S(1)}, u32[]{:S(2)}, u32[]{:S(2)}) %collective-permute-start.5) | collective-permute-done | bytes 409632 | tf_op jit(solution)/shard_map/ppermute | solution.py:37
  55.1 4.1 %shard_map.110 = bf16[8,80,768]{2,1,0:T(8,128)(2,1)} custom-call(f32[8,640]{1,0:T(8,128)S(1)} %broadcast_in_dim.32.keys_ref, bf16[8,80,768]{2,1,0:T(8,128)(2,1)S(1)} %bitcast.30, bf16[2,80,640]{2,1,0:T(8,128)(2,1)S(1)} %bitcast.36, bf16[2,80,640]{2,1,0:T(8,128)(2,1)S(1)} %collective-permute-done.1.refs_1_, ...), custom_call_target="tpu_custom_call" | custom-call | flops 8589934592 | bytes 1048576 | tf_op jit(solution)/shard_map/pallas_call | solution.py:217
  59.2 3.9 %all-to-all-start.1 = ((bf16[8,80,768]{2,1,0:T(8,128)(2,1)}), bf16[8,80,768]{2,1,0:T(8,128)(2,1)S(1)}, u32[]{:S(2)}, u32[]{:S(2)}) async-start(bf16[8,80,768]{2,1,0:T(8,128)(2,1)} %shard_map.110), calls=%async_computation.1 | async-start | bytes 1966080 | tf_op jit(solution)/shard_map/all_to_all | solution.py:220
  63.1 0.6 shard_map.111
  63.8 9.4 %all-to-all-done.1.parts_ref = bf16[8,80,768]{2,1,0:T(8,128)(2,1)S(1)} async-done(((bf16[8,80,768]{2,1,0:T(8,128)(2,1)}), bf16[8,80,768]{2,1,0:T(8,128)(2,1)S(1)}, u32[]{:S(2)}, u32[]{:S(2)}) %all-to-all-start.1) | async-done | bytes 983072 | tf_op jit(solution)/shard_map/all_to_all | solution.py:220
  73.1 0.8 shard_map.112.own_ref
  74.0 3.3 %collective-permute-start.6 = (bf16[80,640]{1,0:T(8,128)(2,1)S(1)}, bf16[80,640]{1,0:T(8,128)(2,1)S(1)}, u32[]{:S(2)}, u32[]{:S(2)}) collective-permute-start(bf16[80,640]{1,0:T(8,128)(2,1)S(1)} %shard_map.112.own_ref), channel_id=1, source_target_pairs={{0,256},{256,0},{1,257},{257,1},{2,258},{258,2},{3,259},{259,3},{4... | collective-permute-start | bytes 307208 | tf_op jit(solution)/shard_map/ppermute | solution.py:25
  77.4 2.3 %collective-permute-done.6.other_ref = bf16[80,640]{1,0:T(8,128)(2,1)S(1)} collective-permute-done((bf16[80,640]{1,0:T(8,128)(2,1)S(1)}, bf16[80,640]{1,0:T(8,128)(2,1)S(1)}, u32[]{:S(2)}, u32[]{:S(2)}) %collective-permute-start.6) | collective-permute-done | bytes 102432 | tf_op jit(solution)/shard_map/ppermute | solution.py:25
  79.7 2.0 %shard_map.113 = bf16[4,80,640]{2,1,0:T(8,128)(2,1)} custom-call(f32[2]{0:T(128)S(1)} %broadcast_select_fusion.factor_ref, bf16[80,640]{1,0:T(8,128)(2,1)S(1)} %shard_map.112.own_ref, bf16[80,640]{1,0:T(8,128)(2,1)S(1)} %collective-permute-done.6.other_ref, bf16[640,2560]{1,0:T(8,128)(2,1)S(1)} %copy-done), custom_call_target="tpu_custom_call" | custom-call | bytes 1048576 | tf_op jit(solution)/shard_map/pallas_call | solution.py:235
  81.7 14.4 %all-to-all-start.2 = ((bf16[4,80,640]{2,1,0:T(8,128)(2,1)}), bf16[4,80,640]{2,1,0:T(8,128)(2,1)S(1)}, u32[]{:S(2)}, u32[]{:S(2)}) async-start(bf16[4,80,640]{2,1,0:T(8,128)(2,1)} %shard_map.113), calls=%async_computation.2 | async-start | bytes 819200 | tf_op jit(solution)/shard_map/all_to_all | solution.py:238
  96.7 0.1 select_reduce_fusion
  96.8 7.5 %all-to-all-done.2 = bf16[4,80,640]{2,1,0:T(8,128)(2,1)S(1)} async-done(((bf16[4,80,640]{2,1,0:T(8,128)(2,1)}), bf16[4,80,640]{2,1,0:T(8,128)(2,1)S(1)}, u32[]{:S(2)}, u32[]{:S(2)}) %all-to-all-start.2) | async-done | bytes 409632 | tf_op jit(solution)/shard_map/all_to_all | solution.py:238
  104.3 0.7 fusion.4
  (30 shorter events, 0.3 us)
Async XLA Ops:
  0.0 44.7 %copy-start.8 = (s32[8]{0:T(128)S(1)}, s32[8]{0:T(128)}, u32[]{:S(2)}) copy-start(s32[8]{0:T(128)} %constant.90.clone) | copy-start | bytes 100
  0.0 55.1 %copy-start.2 = (bf16[1,2,80,640]{3,2,1,0:T(8,128)(2,1)S(1)}, bf16[1,2,80,640]{3,2,1,0:T(8,128)(2,1)}, u32[]{:S(2)}) copy-start(bf16[1,2,80,640]{3,2,1,0:T(8,128)(2,1)} %param.13) | copy-start | bytes 614404
  0.0 17.7 %collective-permute-start.1 = (bf16[2,80,640]{2,1,0:T(8,128)(2,1)}, bf16[2,80,640]{2,1,0:T(8,128)(2,1)S(1)}, u32[]{:S(2)}, u32[]{:S(2)}) collective-permute-start(bf16[2,80,640]{2,1,0:T(8,128)(2,1)} %bitcast.34), channel_id=1, source_target_pairs={{0,8},{1,57},{2,10},{3,59},{8,0},{9,17},{10,2},{11,19},{16,24},{17... | collective-permute-start | bytes 614408 | tf_op jit(solution)/shard_map/ppermute | solution.py:37
  12.5 11.5 %collective-permute-start.2 = (bf16[2,80,640]{2,1,0:T(8,128)(2,1)}, bf16[2,80,640]{2,1,0:T(8,128)(2,1)S(1)}, u32[]{:S(2)}, u32[]{:S(2)}) collective-permute-start(bf16[2,80,640]{2,1,0:T(8,128)(2,1)} %bitcast.35), channel_id=1, source_target_pairs={{0,56},{1,9},{2,58},{3,11},{8,16},{9,1},{10,18},{11,3},{16,8},{17,... | collective-permute-start | bytes 614408 | tf_op jit(solution)/shard_map/ppermute | solution.py:37
  17.8 7.6 %collective-permute-start.3 = (bf16[2,80,640]{2,1,0:T(8,128)(2,1)S(1)}, bf16[2,80,640]{2,1,0:T(8,128)(2,1)S(1)}, u32[]{:S(2)}, u32[]{:S(2)}) collective-permute-start(bf16[2,80,640]{2,1,0:T(8,128)(2,1)S(1)} %collective-permute-done.1.refs_1_), channel_id=1, source_target_pairs={{0,56},{1,9},{2,58},{3,11},{8,16},{9,1},{10,18},{11,3},{16,8},{17,... | collective-permute-start | bytes 614408 | tf_op jit(solution)/shard_map/ppermute | solution.py:37
  20.7 10.5 %collective-permute-start = (bf16[80,768]{1,0:T(8,128)(2,1)S(1)}, bf16[80,768]{1,0:T(8,128)(2,1)S(1)}, u32[]{:S(2)}, u32[]{:S(2)}) collective-permute-start(bf16[80,768]{1,0:T(8,128)(2,1)S(1)} %maximum_maximum_fusion), channel_id=1, source_target_pairs={{0,4},{4,0},{1,5},{5,1},{2,6},{6,2},{3,7},{7,3},{8,12},{12,8},{9,1... | collective-permute-start | bytes 368648 | tf_op jit(solution)/shard_map/ppermute | solution.py:25
  25.4 14.1 %collective-permute-start.4 = (bf16[2,2,80,640]{3,2,1,0:T(8,128)(2,1)S(1)}, bf16[2,2,80,640]{3,2,1,0:T(8,128)(2,1)S(1)}, u32[]{:S(2)}, u32[]{:S(2)}) collective-permute-start(bf16[2,2,80,640]{3,2,1,0:T(8,128)(2,1)S(1)} %shard_map.109), channel_id=1, source_target_pairs={{0,8},{1,57},{2,10},{3,59},{8,0},{9,17},{10,2},{11,19},{16,24},{17... | collective-permute-start | bytes 1228808 | tf_op jit(solution)/shard_map/ppermute | solution.py:37
  33.2 15.2 %all-to-all-start = ((bf16[4,2,80,768]{3,2,1,0:T(8,128)(2,1)}), bf16[4,2,80,768]{3,2,1,0:T(8,128)(2,1)S(1)}, u32[]{:S(2)}, u32[]{:S(2)}) async-start(bf16[4,2,80,768]{3,2,1,0:T(8,128)(2,1)} %broadcast_in_dim.34), calls=%async_computation | async-start | bytes 1966080 | tf_op jit(solution)/shard_map/all_to_all | solution.py:206
  39.5 15.6 %collective-permute-start.5 = (bf16[2,2,80,640]{3,2,1,0:T(8,128)(2,1)S(1)}, bf16[2,2,80,640]{3,2,1,0:T(8,128)(2,1)S(1)}, u32[]{:S(2)}, u32[]{:S(2)}) collective-permute-start(bf16[2,2,80,640]{3,2,1,0:T(8,128)(2,1)S(1)} %collective-permute-done.4.refs_4_), channel_id=1, source_target_pairs={{0,56},{1,9},{2,58},{3,11},{8,16},{9,1},{10,18},{11,3},{16,8},{17,... | collective-permute-start | bytes 1228808 | tf_op jit(solution)/shard_map/ppermute | solution.py:37
  55.1 8.0 %copy-start.1 = (bf16[1,80,640]{2,1,0:T(8,128)(2,1)S(1)}, bf16[1,80,640]{2,1,0:T(8,128)(2,1)}, u32[]{:S(2)}) copy-start(bf16[1,80,640]{2,1,0:T(8,128)(2,1)} %param.11) | copy-start | bytes 307204
  55.1 8.0 %copy-start.3 = (bf16[1,2,80,640]{3,2,1,0:T(8,128)(2,1)S(1)}, bf16[1,2,80,640]{3,2,1,0:T(8,128)(2,1)}, u32[]{:S(2)}) copy-start(bf16[1,2,80,640]{3,2,1,0:T(8,128)(2,1)} %param.12) | copy-start | bytes 614404
  59.2 13.9 %all-to-all-start.1 = ((bf16[8,80,768]{2,1,0:T(8,128)(2,1)}), bf16[8,80,768]{2,1,0:T(8,128)(2,1)S(1)}, u32[]{:S(2)}, u32[]{:S(2)}) async-start(bf16[8,80,768]{2,1,0:T(8,128)(2,1)} %shard_map.110), calls=%async_computation.1 | async-start | bytes 1966080 | tf_op jit(solution)/shard_map/all_to_all | solution.py:220
  73.1 4.2 %copy-start.6 = (f32[2]{0:T(128)S(1)}, f32[2]{0:T(128)}, u32[]{:S(2)}) copy-start(f32[2]{0:T(128)} %constant.91.clone) | copy-start | bytes 28
  73.1 4.2 %copy-start.7 = (f32[2]{0:T(128)S(1)}, f32[2]{0:T(128)}, u32[]{:S(2)}) copy-start(f32[2]{0:T(128)} %constant.92.clone) | copy-start | bytes 28
  73.1 6.5 %copy-start = (bf16[640,2560]{1,0:T(8,128)(2,1)S(1)}, bf16[640,2560]{1,0:T(8,128)(2,1)}, u32[]{:S(2)}) copy-start(bf16[640,2560]{1,0:T(8,128)(2,1)} %weight_ref.1) | copy-start | bytes 9830404
  74.0 22.1 %copy-start.4 = (bf16[2,80,640]{2,1,0:T(8,128)(2,1)S(1)}, bf16[2,80,640]{2,1,0:T(8,128)(2,1)}, u32[]{:S(2)}) copy-start(bf16[2,80,640]{2,1,0:T(8,128)(2,1)} %param.17) | copy-start | bytes 614404
  74.0 22.7 %copy-start.5 = (f32[50,640]{1,0:T(8,128)S(1)}, f32[50,640]{1,0:T(8,128)}, u32[]{:S(2)}) copy-start(f32[50,640]{1,0:T(8,128)} %param.16) | copy-start | bytes 384004
  74.0 5.6 %collective-permute-start.6 = (bf16[80,640]{1,0:T(8,128)(2,1)S(1)}, bf16[80,640]{1,0:T(8,128)(2,1)S(1)}, u32[]{:S(2)}, u32[]{:S(2)}) collective-permute-start(bf16[80,640]{1,0:T(8,128)(2,1)S(1)} %shard_map.112.own_ref), channel_id=1, source_target_pairs={{0,256},{256,0},{1,257},{257,1},{2,258},{258,2},{3,259},{259,3},{4... | collective-permute-start | bytes 307208 | tf_op jit(solution)/shard_map/ppermute | solution.py:25
  81.7 22.6 %all-to-all-start.2 = ((bf16[4,80,640]{2,1,0:T(8,128)(2,1)}), bf16[4,80,640]{2,1,0:T(8,128)(2,1)S(1)}, u32[]{:S(2)}, u32[]{:S(2)}) async-start(bf16[4,80,640]{2,1,0:T(8,128)(2,1)} %shard_map.113), calls=%async_computation.2 | async-start | bytes 819200 | tf_op jit(solution)/shard_map/all_to_all | solution.py:238

commit v5 on v4

--- a/solution.py
+++ b/solution.py
@@ -41,12 +41,14 @@
     return slice(head * HD, (head + 1) * HD)
 
 
-def softmax_sums(queries, keys, values, bias):
-    total = keys.shape[0]
+def pieces_of(total):
     cut = total * 3 // 5 // LANES * LANES
-    pieces = [(0, cut), (cut, total)] if cut else [(0, total)]
+    return [(0, cut), (cut, total)] if cut else [(0, total)]
+
+
+def scores_of(queries, keys, bias):
     scores = []
-    for low, high in pieces:
+    for low, high in pieces_of(keys.shape[0]):
         score = lax.dot_general(
             queries, keys[low:high], (((1,), (1,)), ((), ())), preferred_element_type=jnp.float32
         )
@@ -55,13 +57,17 @@
             score = score.reshape(slabs, -1, high - low) + bias[:, :, low:high]
             score = score.reshape(-1, high - low)
         scores.append(score)
+    return scores
+
+
+def softmax_sums(scores, values):
     maxima = [jnp.max(score, axis=1, keepdims=True) for score in scores]
     maxima = functools.reduce(jnp.maximum, maxima)
+    weights = [jnp.exp2((score - maxima) * EXPONENT).astype(jnp.bfloat16) for score in scores]
     beside = jnp.concatenate([values, jnp.ones_like(values)], axis=1)
     sums = None
-    for (low, high), score in zip(pieces, scores, strict=True):
-        weights = jnp.exp2((score - maxima) * EXPONENT).astype(jnp.bfloat16)
-        part = jnp.dot(weights, beside[low:high], preferred_element_type=jnp.float32)
+    for (low, high), weight in zip(pieces_of(values.shape[0]), weights, strict=True):
+        part = jnp.dot(weight, beside[low:high], preferred_element_type=jnp.float32)
         sums = part if sums is None else sums + part
     return sums[:, :HD], sums[:, HD:], maxima
 
@@ -77,9 +83,8 @@
     stats = jnp.zeros((rows, LANES), jnp.float32)
     for head in range(width // HD):
         at = head_lanes(head)
-        update, totals, maxima = softmax_sums(
-            query_ref[:, at], fresh_ref[0, :, at], fresh_ref[1, :, at], None
-        )
+        scores = scores_of(query_ref[:, at], fresh_ref[0, :, at], None)
+        update, totals, maxima = softmax_sums(scores, fresh_ref[1, :, at])
         out_ref[:, at] = update / totals
         stats = place_stats(stats, lane, head, maxima, totals)
     stats_ref[...] = stats
@@ -109,20 +114,31 @@
     bias = own_bias(query_ref, keys_ref[0:1, :])
     lane = lax.broadcasted_iota(jnp.int32, (slabs * rows, LANES), 1)
     stats = jnp.zeros((slabs * rows, LANES), jnp.float32)
-    for head in range(wide // HD - 1):
+    heads = wide // HD - 1
+
+    def head_scores(head):
         at = head_lanes(head)
         keys = jnp.concatenate([b[0, :, at] for b in blocks], axis=0)
+        return scores_of(query_ref[:, :, at].reshape(slabs * rows, HD), keys, bias)
+
+    scores = head_scores(0)
+    for head in range(heads):
+        at = head_lanes(head)
+        later = head_scores(head + 1) if head + 1 < heads else None
         values = jnp.concatenate([b[1, :, at] for b in blocks], axis=0)
-        queries = query_ref[:, :, at].reshape(slabs * rows, HD)
-        update, totals, maxima = softmax_sums(queries, keys, values, bias)
-        part = (update / totals).astype(jnp.bfloat16)
-        out_ref[:, :, at] = part.reshape(slabs, rows, HD)
+        update, totals, maxima = softmax_sums(scores, values)
+        part = (update / totals).astype(jnp.bfloat16).reshape(slabs, rows, HD)
+        for slab in range(slabs):
+            out_ref[slab % 2 * (slabs // 2) + slab // 2, :, at] = part[slab]
         stats = place_stats(stats, lane, head, maxima, totals)
+        scores = later
     high = stats.astype(jnp.bfloat16).astype(jnp.float32)
     mid = (stats - high).astype(jnp.bfloat16).astype(jnp.float32)
     low = stats - high - mid
     sent = jnp.where(lane < SPAN, high, jnp.where(lane < 2 * SPAN, mid, low))
-    out_ref[:, :, wide - LANES :] = sent.astype(jnp.bfloat16).reshape(slabs, rows, LANES)
+    sent = sent.astype(jnp.bfloat16).reshape(slabs, rows, LANES)
+    for slab in range(slabs):
+        out_ref[slab % 2 * (slabs // 2) + slab // 2, :, wide - LANES :] = sent[slab]
 
 
 def combine_kernel(parts_ref, fresh_ref, fresh_stats_ref, out_ref):
@@ -217,7 +233,7 @@
     parts_out = local_call(stale_kernel, parts_out, specs, 14, 2**33, 2**22)(
         key_ids, queries, *singles, *pairs
     )
-    parts_out = lax.all_to_all(parts_out, ("x", "zl"), 0, 0)
+    parts_out = lax.all_to_all(parts_out, ("zl", "x"), 0, 0)
 
     attended = jax.ShapeDtypeStruct((rows, width), jnp.bfloat16)
     attended = local_call(combine_kernel, attended, [VMEM] * 3, 4, 2**33, 2**20)(

time: 106 us -> 105 us (level)
  no operation moved by 1% of the time
where the time goes in v5:
time: 105 us; the launch traced here: 104 us
  starting transfers between devices  56.1 us (53%)
  waiting for transfers between devices  34.4 us (33%)
  Pallas kernels  7.39 us (7%)
  other arithmetic  3.63 us (3%)
  local copies, waits for them, and re-layouts  1.46 us (1%)
    ppermute x5, starting transfers between devices, trade(): return lax.ppermute(value, ('zh', 't'), pairs)  27.4 us
    all_to_all x1, starting transfers between devices, shards(): projected = lax.all_to_all(projected, 't', 0, 0)  14.2 us
    ppermute x5, waiting for transfers between devices, trade(): return lax.ppermute(value, ('zh', 't'), pairs)  12.6 us
    all_to_all x1, waiting for transfers between devices, shards(): parts_out = lax.all_to_all(parts_out, ('zl', 'x'), 0, 0)  8.45 us
    all_to_all x1, waiting for transfers between devices, shards(): projected = lax.all_to_all(projected, 't', 0, 0)  7.45 us
    ppermute x2, starting transfers between devices, shift(): lax.ppermute(value, axis, [(i, (i + step) % size) for i in range(size)])  6.63 us
    all_to_all x1, starting transfers between devices, shards(): lax.all_to_all(jnp.broadcast_to(pair[None], (lax.axis_size('x'), *pair.sh...  4.01 us
    all_to_all x1, starting transfers between devices, shards(): parts_out = lax.all_to_all(parts_out, ('zl', 'x'), 0, 0)  3.9 us
  transfers between devices with their start and end apart: 10, of which 8 were waited for; matrix products, arithmetic and copies ran while one was open for 4% of the time, Pallas kernels for 1%

profile of v5, /device:TPU:1, one launch (start us, length us, event | category | flops | bytes accessed | tf_op | source)
XLA Modules:
  0.0 103.9 jit_solution(8099530533648308854)
XLA Ops:
  0.0 12.5 %collective-permute-start.1 = (bf16[2,80,640]{2,1,0:T(8,128)(2,1)}, bf16[2,80,640]{2,1,0:T(8,128)(2,1)S(1)}, u32[]{:S(2)}, u32[]{:S(2)}) collective-permute-start(bf16[2,80,640]{2,1,0:T(8,128)(2,1)} %bitcast.34), channel_id=1, source_target_pairs={{0,8},{1,57},{2,10},{3,59},{8,0},{9,17},{10,2},{11,19},{16,24},{17... | collective-permute-start | bytes 614408 | tf_op jit(solution)/shard_map/ppermute | solution.py:37
  12.5 1.9 %collective-permute-start.2 = (bf16[2,80,640]{2,1,0:T(8,128)(2,1)}, bf16[2,80,640]{2,1,0:T(8,128)(2,1)S(1)}, u32[]{:S(2)}, u32[]{:S(2)}) collective-permute-start(bf16[2,80,640]{2,1,0:T(8,128)(2,1)} %bitcast.35), channel_id=1, source_target_pairs={{0,56},{1,9},{2,58},{3,11},{8,16},{9,1},{10,18},{11,3},{16,8},{17,... | collective-permute-start | bytes 614408 | tf_op jit(solution)/shard_map/ppermute | solution.py:37
  14.5 0.7 convert_bitcast_fusion
  15.1 0.1 copy.12
  15.2 0.1 copy.13
  15.4 0.1 pad.5.clone
  15.4 2.3 %collective-permute-done.1.refs_1_ = bf16[2,80,640]{2,1,0:T(8,128)(2,1)S(1)} collective-permute-done((bf16[2,80,640]{2,1,0:T(8,128)(2,1)}, bf16[2,80,640]{2,1,0:T(8,128)(2,1)S(1)}, u32[]{:S(2)}, u32[]{:S(2)}) %collective-permute-start.1) | collective-permute-done | bytes 204832 | tf_op jit(solution)/shard_map/ppermute | solution.py:37
  17.8 1.9 %collective-permute-start.3 = (bf16[2,80,640]{2,1,0:T(8,128)(2,1)S(1)}, bf16[2,80,640]{2,1,0:T(8,128)(2,1)S(1)}, u32[]{:S(2)}, u32[]{:S(2)}) collective-permute-start(bf16[2,80,640]{2,1,0:T(8,128)(2,1)S(1)} %collective-permute-done.1.refs_1_), channel_id=1, source_target_pairs={{0,56},{1,9},{2,58},{3,11},{8,16},{9,1},{10,18},{11,3},{16,8},{17,... | collective-permute-start | bytes 614408 | tf_op jit(solution)/shard_map/ppermute | solution.py:37
  19.7 1.0 maximum_maximum_fusion
  20.7 3.3 %collective-permute-start = (bf16[80,768]{1,0:T(8,128)(2,1)S(1)}, bf16[80,768]{1,0:T(8,128)(2,1)S(1)}, u32[]{:S(2)}, u32[]{:S(2)}) collective-permute-start(bf16[80,768]{1,0:T(8,128)(2,1)S(1)} %maximum_maximum_fusion), channel_id=1, source_target_pairs={{0,4},{4,0},{1,5},{5,1},{2,6},{6,2},{3,7},{7,3},{8,12},{12,8},{9,1... | collective-permute-start | bytes 368648 | tf_op jit(solution)/shard_map/ppermute | solution.py:25
  24.0 1.3 %collective-permute-done.3.other_ref.refs_3_ = bf16[2,80,640]{2,1,0:T(8,128)(2,1)S(1)} collective-permute-done((bf16[2,80,640]{2,1,0:T(8,128)(2,1)S(1)}, bf16[2,80,640]{2,1,0:T(8,128)(2,1)S(1)}, u32[]{:S(2)}, u32[]{:S(2)}) %collective-permute-start.3) | collective-permute-done | bytes 204832 | tf_op jit(solution)/shard_map/ppermute | solution.py:37
  25.4 5.8 %collective-permute-start.4 = (bf16[2,2,80,640]{3,2,1,0:T(8,128)(2,1)S(1)}, bf16[2,2,80,640]{3,2,1,0:T(8,128)(2,1)S(1)}, u32[]{:S(2)}, u32[]{:S(2)}) collective-permute-start(bf16[2,2,80,640]{3,2,1,0:T(8,128)(2,1)S(1)} %shard_map.109), channel_id=1, source_target_pairs={{0,8},{1,57},{2,10},{3,59},{8,0},{9,17},{10,2},{11,19},{16,24},{17... | collective-permute-start | bytes 1228808 | tf_op jit(solution)/shard_map/ppermute | solution.py:37
  31.2 1.0 select_bitcast_fusion.1
  32.2 1.0 broadcast_in_dim.34
  33.2 4.0 %all-to-all-start = ((bf16[4,2,80,768]{3,2,1,0:T(8,128)(2,1)}), bf16[4,2,80,768]{3,2,1,0:T(8,128)(2,1)S(1)}, u32[]{:S(2)}, u32[]{:S(2)}) async-start(bf16[4,2,80,768]{3,2,1,0:T(8,128)(2,1)} %broadcast_in_dim.34), calls=%async_computation | async-start | bytes 1966080 | tf_op jit(solution)/shard_map/all_to_all | solution.py:222
  37.2 2.2 %collective-permute-done.4.refs_4_ = bf16[2,2,80,640]{3,2,1,0:T(8,128)(2,1)S(1)} collective-permute-done((bf16[2,2,80,640]{3,2,1,0:T(8,128)(2,1)S(1)}, bf16[2,2,80,640]{3,2,1,0:T(8,128)(2,1)S(1)}, u32[]{:S(2)}, u32[]{:S(2)}) %collective-permute-start.4) | collective-permute-done | bytes 409632 | tf_op jit(solution)/shard_map/ppermute | solution.py:37
  39.5 5.2 %collective-permute-start.5 = (bf16[2,2,80,640]{3,2,1,0:T(8,128)(2,1)S(1)}, bf16[2,2,80,640]{3,2,1,0:T(8,128)(2,1)S(1)}, u32[]{:S(2)}, u32[]{:S(2)}) collective-permute-start(bf16[2,2,80,640]{3,2,1,0:T(8,128)(2,1)S(1)} %collective-permute-done.4.refs_4_), channel_id=1, source_target_pairs={{0,56},{1,9},{2,58},{3,11},{8,16},{9,1},{10,18},{11,3},{16,8},{17,... | collective-permute-start | bytes 1228808 | tf_op jit(solution)/shard_map/ppermute | solution.py:37
  44.8 0.1 convert_element_type.22
  44.9 3.5 %all-to-all-done = bf16[4,2,80,768]{3,2,1,0:T(8,128)(2,1)S(1)} async-done(((bf16[4,2,80,768]{3,2,1,0:T(8,128)(2,1)}), bf16[4,2,80,768]{3,2,1,0:T(8,128)(2,1)S(1)}, u32[]{:S(2)}, u32[]{:S(2)}) %all-to-all-start) | async-done | bytes 983072 | tf_op jit(solution)/shard_map/all_to_all | solution.py:222
  48.4 6.7 %collective-permute-done.5.refs_5_ = bf16[2,2,80,640]{3,2,1,0:T(8,128)(2,1)S(1)} collective-permute-done((bf16[2,2,80,640]{3,2,1,0:T(8,128)(2,1)S(1)}, bf16[2,2,80,640]{3,2,1,0:T(8,128)(2,1)S(1)}, u32[]{:S(2)}, u32[]{:S(2)}) %collective-permute-start.5) | collective-permute-done | bytes 409632 | tf_op jit(solution)/shard_map/ppermute | solution.py:37
  55.1 3.9 %shard_map.110 = bf16[8,80,768]{2,1,0:T(8,128)(2,1)} custom-call(f32[8,640]{1,0:T(8,128)S(1)} %broadcast_in_dim.32.keys_ref, bf16[8,80,768]{2,1,0:T(8,128)(2,1)S(1)} %bitcast.30, bf16[2,80,640]{2,1,0:T(8,128)(2,1)S(1)} %bitcast.36, bf16[2,80,640]{2,1,0:T(8,128)(2,1)S(1)} %collective-permute-done.1.refs_1_, ...), custom_call_target="tpu_custom_call" | custom-call | flops 8589934592 | bytes 1048576 | tf_op jit(solution)/shard_map/pallas_call | solution.py:233
  59.0 3.9 %all-to-all-start.1 = ((bf16[8,80,768]{2,1,0:T(8,128)(2,1)}), bf16[8,80,768]{2,1,0:T(8,128)(2,1)S(1)}, u32[]{:S(2)}, u32[]{:S(2)}) async-start(bf16[8,80,768]{2,1,0:T(8,128)(2,1)} %shard_map.110), calls=%async_computation.1 | async-start | bytes 1966080 | tf_op jit(solution)/shard_map/all_to_all | solution.py:236
  62.9 0.6 shard_map.111
  63.6 8.5 %all-to-all-done.1.parts_ref = bf16[8,80,768]{2,1,0:T(8,128)(2,1)S(1)} async-done(((bf16[8,80,768]{2,1,0:T(8,128)(2,1)}), bf16[8,80,768]{2,1,0:T(8,128)(2,1)S(1)}, u32[]{:S(2)}, u32[]{:S(2)}) %all-to-all-start.1) | async-done | bytes 983072 | tf_op jit(solution)/shard_map/all_to_all | solution.py:236
  72.0 0.8 shard_map.112.own_ref
  72.9 3.3 %collective-permute-start.6 = (bf16[80,640]{1,0:T(8,128)(2,1)S(1)}, bf16[80,640]{1,0:T(8,128)(2,1)S(1)}, u32[]{:S(2)}, u32[]{:S(2)}) collective-permute-start(bf16[80,640]{1,0:T(8,128)(2,1)S(1)} %shard_map.112.own_ref), channel_id=1, source_target_pairs={{0,256},{256,0},{1,257},{257,1},{2,258},{258,2},{3,259},{259,3},{4... | collective-permute-start | bytes 307208 | tf_op jit(solution)/shard_map/ppermute | solution.py:25
  76.3 2.5 %collective-permute-done.6.other_ref = bf16[80,640]{1,0:T(8,128)(2,1)S(1)} collective-permute-done((bf16[80,640]{1,0:T(8,128)(2,1)S(1)}, bf16[80,640]{1,0:T(8,128)(2,1)S(1)}, u32[]{:S(2)}, u32[]{:S(2)}) %collective-permute-start.6) | collective-permute-done | bytes 102432 | tf_op jit(solution)/shard_map/ppermute | solution.py:25
  78.7 2.0 %shard_map.113 = bf16[4,80,640]{2,1,0:T(8,128)(2,1)} custom-call(f32[2]{0:T(128)S(1)} %broadcast_select_fusion.factor_ref, bf16[80,640]{1,0:T(8,128)(2,1)S(1)} %shard_map.112.own_ref, bf16[80,640]{1,0:T(8,128)(2,1)S(1)} %collective-permute-done.6.other_ref, bf16[640,2560]{1,0:T(8,128)(2,1)S(1)} %copy-done), custom_call_target="tpu_custom_call" | custom-call | bytes 1048576 | tf_op jit(solution)/shard_map/pallas_call | solution.py:251
  80.7 14.2 %all-to-all-start.2 = ((bf16[4,80,640]{2,1,0:T(8,128)(2,1)}), bf16[4,80,640]{2,1,0:T(8,128)(2,1)S(1)}, u32[]{:S(2)}, u32[]{:S(2)}) async-start(bf16[4,80,640]{2,1,0:T(8,128)(2,1)} %shard_map.113), calls=%async_computation.2 | async-start | bytes 819200 | tf_op jit(solution)/shard_map/all_to_all | solution.py:254
  95.6 0.1 select_reduce_fusion
  95.7 7.5 %all-to-all-done.2 = bf16[4,80,640]{2,1,0:T(8,128)(2,1)S(1)} async-done(((bf16[4,80,640]{2,1,0:T(8,128)(2,1)}), bf16[4,80,640]{2,1,0:T(8,128)(2,1)S(1)}, u32[]{:S(2)}, u32[]{:S(2)}) %all-to-all-start.2) | async-done | bytes 409632 | tf_op jit(solution)/shard_map/all_to_all | solution.py:254
  103.2 0.7 fusion.4
  (30 shorter events, 0.3 us)
Async XLA Ops:
  0.0 44.7 %copy-start.8 = (s32[8]{0:T(128)S(1)}, s32[8]{0:T(128)}, u32[]{:S(2)}) copy-start(s32[8]{0:T(128)} %constant.90.clone) | copy-start | bytes 100
  0.0 55.1 %copy-start.2 = (bf16[1,2,80,640]{3,2,1,0:T(8,128)(2,1)S(1)}, bf16[1,2,80,640]{3,2,1,0:T(8,128)(2,1)}, u32[]{:S(2)}) copy-start(bf16[1,2,80,640]{3,2,1,0:T(8,128)(2,1)} %param.13) | copy-start | bytes 614404
  0.0 17.7 %collective-permute-start.1 = (bf16[2,80,640]{2,1,0:T(8,128)(2,1)}, bf16[2,80,640]{2,1,0:T(8,128)(2,1)S(1)}, u32[]{:S(2)}, u32[]{:S(2)}) collective-permute-start(bf16[2,80,640]{2,1,0:T(8,128)(2,1)} %bitcast.34), channel_id=1, source_target_pairs={{0,8},{1,57},{2,10},{3,59},{8,0},{9,17},{10,2},{11,19},{16,24},{17... | collective-permute-start | bytes 614408 | tf_op jit(solution)/shard_map/ppermute | solution.py:37
  12.5 11.5 %collective-permute-start.2 = (bf16[2,80,640]{2,1,0:T(8,128)(2,1)}, bf16[2,80,640]{2,1,0:T(8,128)(2,1)S(1)}, u32[]{:S(2)}, u32[]{:S(2)}) collective-permute-start(bf16[2,80,640]{2,1,0:T(8,128)(2,1)} %bitcast.35), channel_id=1, source_target_pairs={{0,56},{1,9},{2,58},{3,11},{8,16},{9,1},{10,18},{11,3},{16,8},{17,... | collective-permute-start | bytes 614408 | tf_op jit(solution)/shard_map/ppermute | solution.py:37
  17.8 7.6 %collective-permute-start.3 = (bf16[2,80,640]{2,1,0:T(8,128)(2,1)S(1)}, bf16[2,80,640]{2,1,0:T(8,128)(2,1)S(1)}, u32[]{:S(2)}, u32[]{:S(2)}) collective-permute-start(bf16[2,80,640]{2,1,0:T(8,128)(2,1)S(1)} %collective-permute-done.1.refs_1_), channel_id=1, source_target_pairs={{0,56},{1,9},{2,58},{3,11},{8,16},{9,1},{10,18},{11,3},{16,8},{17,... | collective-permute-start | bytes 614408 | tf_op jit(solution)/shard_map/ppermute | solution.py:37
  20.7 10.5 %collective-permute-start = (bf16[80,768]{1,0:T(8,128)(2,1)S(1)}, bf16[80,768]{1,0:T(8,128)(2,1)S(1)}, u32[]{:S(2)}, u32[]{:S(2)}) collective-permute-start(bf16[80,768]{1,0:T(8,128)(2,1)S(1)} %maximum_maximum_fusion), channel_id=1, source_target_pairs={{0,4},{4,0},{1,5},{5,1},{2,6},{6,2},{3,7},{7,3},{8,12},{12,8},{9,1... | collective-permute-start | bytes 368648 | tf_op jit(solution)/shard_map/ppermute | solution.py:25
  25.4 14.1 %collective-permute-start.4 = (bf16[2,2,80,640]{3,2,1,0:T(8,128)(2,1)S(1)}, bf16[2,2,80,640]{3,2,1,0:T(8,128)(2,1)S(1)}, u32[]{:S(2)}, u32[]{:S(2)}) collective-permute-start(bf16[2,2,80,640]{3,2,1,0:T(8,128)(2,1)S(1)} %shard_map.109), channel_id=1, source_target_pairs={{0,8},{1,57},{2,10},{3,59},{8,0},{9,17},{10,2},{11,19},{16,24},{17... | collective-permute-start | bytes 1228808 | tf_op jit(solution)/shard_map/ppermute | solution.py:37
  33.2 15.2 %all-to-all-start = ((bf16[4,2,80,768]{3,2,1,0:T(8,128)(2,1)}), bf16[4,2,80,768]{3,2,1,0:T(8,128)(2,1)S(1)}, u32[]{:S(2)}, u32[]{:S(2)}) async-start(bf16[4,2,80,768]{3,2,1,0:T(8,128)(2,1)} %broadcast_in_dim.34), calls=%async_computation | async-start | bytes 1966080 | tf_op jit(solution)/shard_map/all_to_all | solution.py:222
  39.5 15.6 %collective-permute-start.5 = (bf16[2,2,80,640]{3,2,1,0:T(8,128)(2,1)S(1)}, bf16[2,2,80,640]{3,2,1,0:T(8,128)(2,1)S(1)}, u32[]{:S(2)}, u32[]{:S(2)}) collective-permute-start(bf16[2,2,80,640]{3,2,1,0:T(8,128)(2,1)S(1)} %collective-permute-done.4.refs_4_), channel_id=1, source_target_pairs={{0,56},{1,9},{2,58},{3,11},{8,16},{9,1},{10,18},{11,3},{16,8},{17,... | collective-permute-start | bytes 1228808 | tf_op jit(solution)/shard_map/ppermute | solution.py:37
  55.1 7.8 %copy-start.1 = (bf16[1,80,640]{2,1,0:T(8,128)(2,1)S(1)}, bf16[1,80,640]{2,1,0:T(8,128)(2,1)}, u32[]{:S(2)}) copy-start(bf16[1,80,640]{2,1,0:T(8,128)(2,1)} %param.11) | copy-start | bytes 307204
  55.1 7.8 %copy-start.3 = (bf16[1,2,80,640]{3,2,1,0:T(8,128)(2,1)S(1)}, bf16[1,2,80,640]{3,2,1,0:T(8,128)(2,1)}, u32[]{:S(2)}) copy-start(bf16[1,2,80,640]{3,2,1,0:T(8,128)(2,1)} %param.12) | copy-start | bytes 614404
  59.0 13.0 %all-to-all-start.1 = ((bf16[8,80,768]{2,1,0:T(8,128)(2,1)}), bf16[8,80,768]{2,1,0:T(8,128)(2,1)S(1)}, u32[]{:S(2)}, u32[]{:S(2)}) async-start(bf16[8,80,768]{2,1,0:T(8,128)(2,1)} %shard_map.110), calls=%async_computation.1 | async-start | bytes 1966080 | tf_op jit(solution)/shard_map/all_to_all | solution.py:236
  72.0 4.2 %copy-start.6 = (f32[2]{0:T(128)S(1)}, f32[2]{0:T(128)}, u32[]{:S(2)}) copy-start(f32[2]{0:T(128)} %constant.91.clone) | copy-start | bytes 28
  72.0 4.2 %copy-start.7 = (f32[2]{0:T(128)S(1)}, f32[2]{0:T(128)}, u32[]{:S(2)}) copy-start(f32[2]{0:T(128)} %constant.92.clone) | copy-start | bytes 28
  72.0 6.7 %copy-start = (bf16[640,2560]{1,0:T(8,128)(2,1)S(1)}, bf16[640,2560]{1,0:T(8,128)(2,1)}, u32[]{:S(2)}) copy-start(bf16[640,2560]{1,0:T(8,128)(2,1)} %weight_ref.1) | copy-start | bytes 9830404
  72.9 22.1 %copy-start.4 = (bf16[2,80,640]{2,1,0:T(8,128)(2,1)S(1)}, bf16[2,80,640]{2,1,0:T(8,128)(2,1)}, u32[]{:S(2)}) copy-start(bf16[2,80,640]{2,1,0:T(8,128)(2,1)} %param.17) | copy-start | bytes 614404
  72.9 22.7 %copy-start.5 = (f32[50,640]{1,0:T(8,128)S(1)}, f32[50,640]{1,0:T(8,128)}, u32[]{:S(2)}) copy-start(f32[50,640]{1,0:T(8,128)} %param.16) | copy-start | bytes 384004
  72.9 5.8 %collective-permute-start.6 = (bf16[80,640]{1,0:T(8,128)(2,1)S(1)}, bf16[80,640]{1,0:T(8,128)(2,1)S(1)}, u32[]{:S(2)}, u32[]{:S(2)}) collective-permute-start(bf16[80,640]{1,0:T(8,128)(2,1)S(1)} %shard_map.112.own_ref), channel_id=1, source_target_pairs={{0,256},{256,0},{1,257},{257,1},{2,258},{258,2},{3,259},{259,3},{4... | collective-permute-start | bytes 307208 | tf_op jit(solution)/shard_map/ppermute | solution.py:25
  80.7 22.5 %all-to-all-start.2 = ((bf16[4,80,640]{2,1,0:T(8,128)(2,1)}), bf16[4,80,640]{2,1,0:T(8,128)(2,1)S(1)}, u32[]{:S(2)}, u32[]{:S(2)}) async-start(bf16[4,80,640]{2,1,0:T(8,128)(2,1)} %shard_map.113), calls=%async_computation.2 | async-start | bytes 819200 | tf_op jit(solution)/shard_map/all_to_all | solution.py:254

commit v6 on v5

--- a/solution.py
+++ b/solution.py
@@ -191,11 +191,6 @@
     ring = lax.axis_size("zh")
     slabs = lax.axis_size("x") * lax.axis_size("zl")
     parts = lax.axis_size("t")
-
-    places = jnp.stack([assign // LANES, assign % LANES], axis=1).astype(jnp.bfloat16)
-    message = jnp.concatenate(
-        [query[0], places, jnp.zeros((rows, LANES - 2), jnp.bfloat16)], axis=1
-    )
 
     own = stale_kv[0]
     first, second = trade(own, 0), trade(own, 1)
@@ -214,6 +209,11 @@
     key_ids = (slab_ids[:, None] * rows + jnp.arange(rows, dtype=jnp.int32)).astype(jnp.float32)
     key_ids = jnp.broadcast_to(key_ids.reshape(1, -1), (8, ring * rows))
 
+    assign, _ = lax.optimization_barrier((assign, second))
+    places = jnp.stack([assign // LANES, assign % LANES], axis=1).astype(jnp.bfloat16)
+    message = jnp.concatenate(
+        [query[0], places, jnp.zeros((rows, LANES - 2), jnp.bfloat16)], axis=1
+    )
     swapped = shift(message, "zl", 1)
     is_low = lax.axis_index("zl") == 0
     pair = jnp.stack(

time: 105 us -> 109 us (1.038)
  waiting for transfers between devices: 34.4 us -> 42.1 us
  starting transfers between devices: 56.1 us -> 52.7 us
    ppermute x5, waiting for transfers between devices: 12.6 us -> 18.6 us  [trade(): return lax.ppermute(value, ('zh', 't'), pairs)]
    ppermute x5, starting transfers between devices: 27.4 us -> 25.1 us  [trade(): return lax.ppermute(value, ('zh', 't'), pairs)]
    all_to_all x1, waiting for transfers between devices: 3.5 us -> 5.12 us  [shards(): lax.all_to_all(jnp.broadcast_to(pair[None], (lax.axis_size('x'), *pair.sh...]
where the time goes in v6:
time: 109 us; the launch traced here: 108 us
  starting transfers between devices  52.7 us (48%)
  waiting for transfers between devices  42.1 us (39%)
  Pallas kernels  7.39 us (7%)
  other arithmetic  3.63 us (3%)
  local copies, waits for them, and re-layouts  1.46 us (1%)
    ppermute x5, starting transfers between devices, trade(): return lax.ppermute(value, ('zh', 't'), pairs)  25.1 us
    ppermute x5, waiting for transfers between devices, trade(): return lax.ppermute(value, ('zh', 't'), pairs)  18.6 us
    all_to_all x1, starting transfers between devices, shards(): projected = lax.all_to_all(projected, 't', 0, 0)  13.7 us
    all_to_all x1, waiting for transfers between devices, shards(): parts_out = lax.all_to_all(parts_out, ('zl', 'x'), 0, 0)  8.45 us
    all_to_all x1, waiting for transfers between devices, shards(): projected = lax.all_to_all(projected, 't', 0, 0)  7.45 us
    ppermute x2, starting transfers between devices, shift(): lax.ppermute(value, axis, [(i, (i + step) % size) for i in range(size)])  5.85 us
    all_to_all x1, waiting for transfers between devices, shards(): lax.all_to_all(jnp.broadcast_to(pair[None], (lax.axis_size('x'), *pair.sh...  5.12 us
    all_to_all x1, starting transfers between devices, shards(): parts_out = lax.all_to_all(parts_out, ('zl', 'x'), 0, 0)  4.02 us
  transfers between devices with their start and end apart: 10, of which 8 were waited for; matrix products, arithmetic and copies ran while one was open for 4% of the time, Pallas kernels for 1%

profile of v6, /device:TPU:1, one launch (start us, length us, event | category | flops | bytes accessed | tf_op | source)
XLA Modules:
  0.0 108.2 jit_solution(15795034498758098854)
XLA Ops:
  0.0 5.8 %collective-permute-start = (bf16[2,80,640]{2,1,0:T(8,128)(2,1)}, bf16[2,80,640]{2,1,0:T(8,128)(2,1)S(1)}, u32[]{:S(2)}, u32[]{:S(2)}) collective-permute-start(bf16[2,80,640]{2,1,0:T(8,128)(2,1)} %bitcast.34), channel_id=1, source_target_pairs={{0,56},{1,9},{2,58},{3,11},{8,16},{9,1},{10,18},{11,3},{16,8},{17,... | collective-permute-start | bytes 614408 | tf_op jit(solution)/shard_map/ppermute | solution.py:37
  5.9 9.7 %collective-permute-start.2 = (bf16[2,80,640]{2,1,0:T(8,128)(2,1)}, bf16[2,80,640]{2,1,0:T(8,128)(2,1)S(1)}, u32[]{:S(2)}, u32[]{:S(2)}) collective-permute-start(bf16[2,80,640]{2,1,0:T(8,128)(2,1)} %bitcast.35), channel_id=1, source_target_pairs={{0,8},{1,57},{2,10},{3,59},{8,0},{9,17},{10,2},{11,19},{16,24},{17... | collective-permute-start | bytes 614408 | tf_op jit(solution)/shard_map/ppermute | solution.py:37
  15.6 0.1 pad.5.clone
  15.7 0.7 convert_bitcast_fusion
  16.4 0.1 copy.12
  16.5 0.1 copy.13
  16.6 6.7 %collective-permute-done.2.refs_1_ = bf16[2,80,640]{2,1,0:T(8,128)(2,1)S(1)} collective-permute-done((bf16[2,80,640]{2,1,0:T(8,128)(2,1)}, bf16[2,80,640]{2,1,0:T(8,128)(2,1)S(1)}, u32[]{:S(2)}, u32[]{:S(2)}) %collective-permute-start.2) | collective-permute-done | bytes 204832 | tf_op jit(solution)/shard_map/ppermute | solution.py:37
  23.4 1.9 %collective-permute-start.3 = (bf16[2,80,640]{2,1,0:T(8,128)(2,1)S(1)}, bf16[2,80,640]{2,1,0:T(8,128)(2,1)S(1)}, u32[]{:S(2)}, u32[]{:S(2)}) collective-permute-start(bf16[2,80,640]{2,1,0:T(8,128)(2,1)S(1)} %collective-permute-done.2.refs_1_), channel_id=1, source_target_pairs={{0,56},{1,9},{2,58},{3,11},{8,16},{9,1},{10,18},{11,3},{16,8},{17,... | collective-permute-start | bytes 614408 | tf_op jit(solution)/shard_map/ppermute | solution.py:37
  25.3 1.0 maximum_maximum_fusion
  26.3 2.5 %collective-permute-start.1 = (bf16[80,768]{1,0:T(8,128)(2,1)S(1)}, bf16[80,768]{1,0:T(8,128)(2,1)S(1)}, u32[]{:S(2)}, u32[]{:S(2)}) collective-permute-start(bf16[80,768]{1,0:T(8,128)(2,1)S(1)} %maximum_maximum_fusion), channel_id=1, source_target_pairs={{0,4},{4,0},{1,5},{5,1},{2,6},{6,2},{3,7},{7,3},{8,12},{12,8},{9,1... | collective-permute-start | bytes 368648 | tf_op jit(solution)/shard_map/ppermute | solution.py:25
  28.8 4.4 %collective-permute-done.3.other_ref.refs_3_ = bf16[2,80,640]{2,1,0:T(8,128)(2,1)S(1)} collective-permute-done((bf16[2,80,640]{2,1,0:T(8,128)(2,1)S(1)}, bf16[2,80,640]{2,1,0:T(8,128)(2,1)S(1)}, u32[]{:S(2)}, u32[]{:S(2)}) %collective-permute-start.3) | collective-permute-done | bytes 204832 | tf_op jit(solution)/shard_map/ppermute | solution.py:37
  33.3 3.3 %collective-permute-start.4 = (bf16[2,2,80,640]{3,2,1,0:T(8,128)(2,1)S(1)}, bf16[2,2,80,640]{3,2,1,0:T(8,128)(2,1)S(1)}, u32[]{:S(2)}, u32[]{:S(2)}) collective-permute-start(bf16[2,2,80,640]{3,2,1,0:T(8,128)(2,1)S(1)} %shard_map.109), channel_id=1, source_target_pairs={{0,8},{1,57},{2,10},{3,59},{8,0},{9,17},{10,2},{11,19},{16,24},{17... | collective-permute-start | bytes 1228808 | tf_op jit(solution)/shard_map/ppermute | solution.py:37
  36.6 1.0 select_bitcast_fusion.1
  37.6 1.0 broadcast_in_dim.34
  38.7 4.0 %all-to-all-start = ((bf16[4,2,80,768]{3,2,1,0:T(8,128)(2,1)}), bf16[4,2,80,768]{3,2,1,0:T(8,128)(2,1)S(1)}, u32[]{:S(2)}, u32[]{:S(2)}) async-start(bf16[4,2,80,768]{3,2,1,0:T(8,128)(2,1)} %broadcast_in_dim.34), calls=%async_computation | async-start | bytes 1966080 | tf_op jit(solution)/shard_map/all_to_all | solution.py:222
  42.7 2.7 %collective-permute-done.4.refs_4_ = bf16[2,2,80,640]{3,2,1,0:T(8,128)(2,1)S(1)} collective-permute-done((bf16[2,2,80,640]{3,2,1,0:T(8,128)(2,1)S(1)}, bf16[2,2,80,640]{3,2,1,0:T(8,128)(2,1)S(1)}, u32[]{:S(2)}, u32[]{:S(2)}) %collective-permute-start.4) | collective-permute-done | bytes 409632 | tf_op jit(solution)/shard_map/ppermute | solution.py:37
  45.4 4.3 %collective-permute-start.5 = (bf16[2,2,80,640]{3,2,1,0:T(8,128)(2,1)S(1)}, bf16[2,2,80,640]{3,2,1,0:T(8,128)(2,1)S(1)}, u32[]{:S(2)}, u32[]{:S(2)}) collective-permute-start(bf16[2,2,80,640]{3,2,1,0:T(8,128)(2,1)S(1)} %collective-permute-done.4.refs_4_), channel_id=1, source_target_pairs={{0,56},{1,9},{2,58},{3,11},{8,16},{9,1},{10,18},{11,3},{16,8},{17,... | collective-permute-start | bytes 1228808 | tf_op jit(solution)/shard_map/ppermute | solution.py:37
  49.8 0.1 convert_element_type.22
  49.9 5.1 %all-to-all-done = bf16[4,2,80,768]{3,2,1,0:T(8,128)(2,1)S(1)} async-done(((bf16[4,2,80,768]{3,2,1,0:T(8,128)(2,1)}), bf16[4,2,80,768]{3,2,1,0:T(8,128)(2,1)S(1)}, u32[]{:S(2)}, u32[]{:S(2)}) %all-to-all-start) | async-done | bytes 983072 | tf_op jit(solution)/shard_map/all_to_all | solution.py:222
  55.0 4.7 %collective-permute-done.5.refs_5_ = bf16[2,2,80,640]{3,2,1,0:T(8,128)(2,1)S(1)} collective-permute-done((bf16[2,2,80,640]{3,2,1,0:T(8,128)(2,1)S(1)}, bf16[2,2,80,640]{3,2,1,0:T(8,128)(2,1)S(1)}, u32[]{:S(2)}, u32[]{:S(2)}) %collective-permute-start.5) | collective-permute-done | bytes 409632 | tf_op jit(solution)/shard_map/ppermute | solution.py:37
  59.8 3.9 %shard_map.110 = bf16[8,80,768]{2,1,0:T(8,128)(2,1)} custom-call(f32[8,640]{1,0:T(8,128)S(1)} %broadcast_in_dim.32.keys_ref, bf16[8,80,768]{2,1,0:T(8,128)(2,1)S(1)} %bitcast.30, bf16[2,80,640]{2,1,0:T(8,128)(2,1)S(1)} %bitcast.36, bf16[2,80,640]{2,1,0:T(8,128)(2,1)S(1)} %collective-permute-done.2.refs_1_, ...), custom_call_target="tpu_custom_call" | custom-call | flops 8589934592 | bytes 1048576 | tf_op jit(solution)/shard_map/pallas_call | solution.py:233
  63.6 4.0 %all-to-all-start.1 = ((bf16[8,80,768]{2,1,0:T(8,128)(2,1)}), bf16[8,80,768]{2,1,0:T(8,128)(2,1)S(1)}, u32[]{:S(2)}, u32[]{:S(2)}) async-start(bf16[8,80,768]{2,1,0:T(8,128)(2,1)} %shard_map.110), calls=%async_computation.1 | async-start | bytes 1966080 | tf_op jit(solution)/shard_map/all_to_all | solution.py:236
  67.7 0.6 shard_map.111
  68.3 8.5 %all-to-all-done.1.parts_ref = bf16[8,80,768]{2,1,0:T(8,128)(2,1)S(1)} async-done(((bf16[8,80,768]{2,1,0:T(8,128)(2,1)}), bf16[8,80,768]{2,1,0:T(8,128)(2,1)S(1)}, u32[]{:S(2)}, u32[]{:S(2)}) %all-to-all-start.1) | async-done | bytes 983072 | tf_op jit(solution)/shard_map/all_to_all | solution.py:236
  76.8 0.8 shard_map.112.own_ref
  77.7 3.3 %collective-permute-start.6 = (bf16[80,640]{1,0:T(8,128)(2,1)S(1)}, bf16[80,640]{1,0:T(8,128)(2,1)S(1)}, u32[]{:S(2)}, u32[]{:S(2)}) collective-permute-start(bf16[80,640]{1,0:T(8,128)(2,1)S(1)} %shard_map.112.own_ref), channel_id=1, source_target_pairs={{0,256},{256,0},{1,257},{257,1},{2,258},{258,2},{3,259},{259,3},{4... | collective-permute-start | bytes 307208 | tf_op jit(solution)/shard_map/ppermute | solution.py:25
  81.0 2.5 %collective-permute-done.6.other_ref = bf16[80,640]{1,0:T(8,128)(2,1)S(1)} collective-permute-done((bf16[80,640]{1,0:T(8,128)(2,1)S(1)}, bf16[80,640]{1,0:T(8,128)(2,1)S(1)}, u32[]{:S(2)}, u32[]{:S(2)}) %collective-permute-start.6) | collective-permute-done | bytes 102432 | tf_op jit(solution)/shard_map/ppermute | solution.py:25
  83.5 2.0 %shard_map.113 = bf16[4,80,640]{2,1,0:T(8,128)(2,1)} custom-call(f32[2]{0:T(128)S(1)} %broadcast_select_fusion.factor_ref, bf16[80,640]{1,0:T(8,128)(2,1)S(1)} %shard_map.112.own_ref, bf16[80,640]{1,0:T(8,128)(2,1)S(1)} %collective-permute-done.6.other_ref, bf16[640,2560]{1,0:T(8,128)(2,1)S(1)} %copy-done), custom_call_target="tpu_custom_call" | custom-call | bytes 1048576 | tf_op jit(solution)/shard_map/pallas_call | solution.py:251
  85.5 13.7 %all-to-all-start.2 = ((bf16[4,80,640]{2,1,0:T(8,128)(2,1)}), bf16[4,80,640]{2,1,0:T(8,128)(2,1)S(1)}, u32[]{:S(2)}, u32[]{:S(2)}) async-start(bf16[4,80,640]{2,1,0:T(8,128)(2,1)} %shard_map.113), calls=%async_computation.2 | async-start | bytes 819200 | tf_op jit(solution)/shard_map/all_to_all | solution.py:254
  99.9 0.1 select_reduce_fusion
  100.0 7.5 %all-to-all-done.2 = bf16[4,80,640]{2,1,0:T(8,128)(2,1)S(1)} async-done(((bf16[4,80,640]{2,1,0:T(8,128)(2,1)}), bf16[4,80,640]{2,1,0:T(8,128)(2,1)S(1)}, u32[]{:S(2)}, u32[]{:S(2)}) %all-to-all-start.2) | async-done | bytes 409632 | tf_op jit(solution)/shard_map/all_to_all | solution.py:254
  107.5 0.7 fusion.4
  (30 shorter events, 0.3 us)
Async XLA Ops:
  0.0 49.7 %copy-start.8 = (s32[8]{0:T(128)S(1)}, s32[8]{0:T(128)}, u32[]{:S(2)}) copy-start(s32[8]{0:T(128)} %constant.90.clone) | copy-start | bytes 100
  0.0 59.7 %copy-start.2 = (bf16[1,2,80,640]{3,2,1,0:T(8,128)(2,1)S(1)}, bf16[1,2,80,640]{3,2,1,0:T(8,128)(2,1)}, u32[]{:S(2)}) copy-start(bf16[1,2,80,640]{3,2,1,0:T(8,128)(2,1)} %param.13) | copy-start | bytes 614404
  0.0 15.7 %collective-permute-start = (bf16[2,80,640]{2,1,0:T(8,128)(2,1)}, bf16[2,80,640]{2,1,0:T(8,128)(2,1)S(1)}, u32[]{:S(2)}, u32[]{:S(2)}) collective-permute-start(bf16[2,80,640]{2,1,0:T(8,128)(2,1)} %bitcast.34), channel_id=1, source_target_pairs={{0,56},{1,9},{2,58},{3,11},{8,16},{9,1},{10,18},{11,3},{16,8},{17,... | collective-permute-start | bytes 614408 | tf_op jit(solution)/shard_map/ppermute | solution.py:37
  5.9 17.5 %collective-permute-start.2 = (bf16[2,80,640]{2,1,0:T(8,128)(2,1)}, bf16[2,80,640]{2,1,0:T(8,128)(2,1)S(1)}, u32[]{:S(2)}, u32[]{:S(2)}) collective-permute-start(bf16[2,80,640]{2,1,0:T(8,128)(2,1)} %bitcast.35), channel_id=1, source_target_pairs={{0,8},{1,57},{2,10},{3,59},{8,0},{9,17},{10,2},{11,19},{16,24},{17... | collective-permute-start | bytes 614408 | tf_op jit(solution)/shard_map/ppermute | solution.py:37
  23.4 9.9 %collective-permute-start.3 = (bf16[2,80,640]{2,1,0:T(8,128)(2,1)S(1)}, bf16[2,80,640]{2,1,0:T(8,128)(2,1)S(1)}, u32[]{:S(2)}, u32[]{:S(2)}) collective-permute-start(bf16[2,80,640]{2,1,0:T(8,128)(2,1)S(1)} %collective-permute-done.2.refs_1_), channel_id=1, source_target_pairs={{0,56},{1,9},{2,58},{3,11},{8,16},{9,1},{10,18},{11,3},{16,8},{17,... | collective-permute-start | bytes 614408 | tf_op jit(solution)/shard_map/ppermute | solution.py:37
  26.3 10.4 %collective-permute-start.1 = (bf16[80,768]{1,0:T(8,128)(2,1)S(1)}, bf16[80,768]{1,0:T(8,128)(2,1)S(1)}, u32[]{:S(2)}, u32[]{:S(2)}) collective-permute-start(bf16[80,768]{1,0:T(8,128)(2,1)S(1)} %maximum_maximum_fusion), channel_id=1, source_target_pairs={{0,4},{4,0},{1,5},{5,1},{2,6},{6,2},{3,7},{7,3},{8,12},{12,8},{9,1... | collective-permute-start | bytes 368648 | tf_op jit(solution)/shard_map/ppermute | solution.py:25
  33.3 12.1 %collective-permute-start.4 = (bf16[2,2,80,640]{3,2,1,0:T(8,128)(2,1)S(1)}, bf16[2,2,80,640]{3,2,1,0:T(8,128)(2,1)S(1)}, u32[]{:S(2)}, u32[]{:S(2)}) collective-permute-start(bf16[2,2,80,640]{3,2,1,0:T(8,128)(2,1)S(1)} %shard_map.109), channel_id=1, source_target_pairs={{0,8},{1,57},{2,10},{3,59},{8,0},{9,17},{10,2},{11,19},{16,24},{17... | collective-permute-start | bytes 1228808 | tf_op jit(solution)/shard_map/ppermute | solution.py:37
  38.7 16.4 %all-to-all-start = ((bf16[4,2,80,768]{3,2,1,0:T(8,128)(2,1)}), bf16[4,2,80,768]{3,2,1,0:T(8,128)(2,1)S(1)}, u32[]{:S(2)}, u32[]{:S(2)}) async-start(bf16[4,2,80,768]{3,2,1,0:T(8,128)(2,1)} %broadcast_in_dim.34), calls=%async_computation | async-start | bytes 1966080 | tf_op jit(solution)/shard_map/all_to_all | solution.py:222
  45.4 14.3 %collective-permute-start.5 = (bf16[2,2,80,640]{3,2,1,0:T(8,128)(2,1)S(1)}, bf16[2,2,80,640]{3,2,1,0:T(8,128)(2,1)S(1)}, u32[]{:S(2)}, u32[]{:S(2)}) collective-permute-start(bf16[2,2,80,640]{3,2,1,0:T(8,128)(2,1)S(1)} %collective-permute-done.4.refs_4_), channel_id=1, source_target_pairs={{0,56},{1,9},{2,58},{3,11},{8,16},{9,1},{10,18},{11,3},{16,8},{17,... | collective-permute-start | bytes 1228808 | tf_op jit(solution)/shard_map/ppermute | solution.py:37
  59.8 7.9 %copy-start.1 = (bf16[1,80,640]{2,1,0:T(8,128)(2,1)S(1)}, bf16[1,80,640]{2,1,0:T(8,128)(2,1)}, u32[]{:S(2)}) copy-start(bf16[1,80,640]{2,1,0:T(8,128)(2,1)} %param.11) | copy-start | bytes 307204
  59.8 7.9 %copy-start.3 = (bf16[1,2,80,640]{3,2,1,0:T(8,128)(2,1)S(1)}, bf16[1,2,80,640]{3,2,1,0:T(8,128)(2,1)}, u32[]{:S(2)}) copy-start(bf16[1,2,80,640]{3,2,1,0:T(8,128)(2,1)} %param.12) | copy-start | bytes 614404
  63.6 13.1 %all-to-all-start.1 = ((bf16[8,80,768]{2,1,0:T(8,128)(2,1)}), bf16[8,80,768]{2,1,0:T(8,128)(2,1)S(1)}, u32[]{:S(2)}, u32[]{:S(2)}) async-start(bf16[8,80,768]{2,1,0:T(8,128)(2,1)} %shard_map.110), calls=%async_computation.1 | async-start | bytes 1966080 | tf_op jit(solution)/shard_map/all_to_all | solution.py:236
  76.8 4.2 %copy-start.6 = (f32[2]{0:T(128)S(1)}, f32[2]{0:T(128)}, u32[]{:S(2)}) copy-start(f32[2]{0:T(128)} %constant.91.clone) | copy-start | bytes 28
  76.8 4.2 %copy-start.7 = (f32[2]{0:T(128)S(1)}, f32[2]{0:T(128)}, u32[]{:S(2)}) copy-start(f32[2]{0:T(128)} %constant.92.clone) | copy-start | bytes 28
  76.8 6.7 %copy-start = (bf16[640,2560]{1,0:T(8,128)(2,1)S(1)}, bf16[640,2560]{1,0:T(8,128)(2,1)}, u32[]{:S(2)}) copy-start(bf16[640,2560]{1,0:T(8,128)(2,1)} %weight_ref.1) | copy-start | bytes 9830404
  77.6 21.5 %copy-start.4 = (bf16[2,80,640]{2,1,0:T(8,128)(2,1)S(1)}, bf16[2,80,640]{2,1,0:T(8,128)(2,1)}, u32[]{:S(2)}) copy-start(bf16[2,80,640]{2,1,0:T(8,128)(2,1)} %param.17) | copy-start | bytes 614404
  77.7 22.2 %copy-start.5 = (f32[50,640]{1,0:T(8,128)S(1)}, f32[50,640]{1,0:T(8,128)}, u32[]{:S(2)}) copy-start(f32[50,640]{1,0:T(8,128)} %param.16) | copy-start | bytes 384004
  77.7 5.8 %collective-permute-start.6 = (bf16[80,640]{1,0:T(8,128)(2,1)S(1)}, bf16[80,640]{1,0:T(8,128)(2,1)S(1)}, u32[]{:S(2)}, u32[]{:S(2)}) collective-permute-start(bf16[80,640]{1,0:T(8,128)(2,1)S(1)} %shard_map.112.own_ref), channel_id=1, source_target_pairs={{0,256},{256,0},{1,257},{257,1},{2,258},{258,2},{3,259},{259,3},{4... | collective-permute-start | bytes 307208 | tf_op jit(solution)/shard_map/ppermute | solution.py:25
  85.5 21.9 %all-to-all-start.2 = ((bf16[4,80,640]{2,1,0:T(8,128)(2,1)}), bf16[4,80,640]{2,1,0:T(8,128)(2,1)S(1)}, u32[]{:S(2)}, u32[]{:S(2)}) async-start(bf16[4,80,640]{2,1,0:T(8,128)(2,1)} %shard_map.113), calls=%async_computation.2 | async-start | bytes 819200 | tf_op jit(solution)/shard_map/all_to_all | solution.py:254
